TPU v7x, 128 devices: a whole 4x4x4 slice. The times are simulated.
128 devices in a mesh: row: 32 (over z_hi, x, y), col: 4 (over z_lo, core).
Axes of the slice: x: 4, y: 4, z: 4 (z_hi: 2, z_lo: 2; z = z_hi * 2 + z_lo), core: 2. Of those that a mesh axis runs over, the one named last changes fastest.
Arguments:
- pair_left: bfloat16 [4096, 384, 128], P('row', 'col'), may hold values from -6 to 6
- pair_right: bfloat16 [1024, 384, 128], P('col', 'row'), may hold values from -6 to 6
- pair_gate: bfloat16 [4096, 1024, 128], P('row', 'col'), may hold values from -6 to 6
- left_proj: bfloat16 [128, 128], replicated, may hold values from -0.5 to 0.5
- left_gate: bfloat16 [128, 128], replicated, may hold values from -0.5 to 0.5
- right_proj: bfloat16 [128, 128], replicated, may hold values from -0.5 to 0.5
- right_gate: bfloat16 [128, 128], replicated, may hold values from -0.5 to 0.5
- out_gate: bfloat16 [128, 128], replicated, may hold values from -0.5 to 0.5
- out_proj: bfloat16 [128, 128], replicated, may hold values from -0.5 to 0.5
Outputs:
- update: bfloat16 [4096, 1024, 128], P('row', 'col')
All inputs are finite; a program needn't handle non-finite values.
Results may differ from a plain program's by a relative error of at most 0.0078.
Values may be sent and summed in bfloat16 or wider, within the bound.
No kernel may reach another device: no remote copies, remote signals or barrier semaphores. Data moves between devices by JAX's collectives and lax.ppermute only.
A program may use at most 256 MiB of HBM per device.

v0:
```python
import jax
import jax.numpy as jnp
from jax import lax
from jax.sharding import PartitionSpec as P

epsilon = 1e-05


def normalize(values, channel_axis):
    floats = values.astype(jnp.float32)
    average = jnp.mean(floats, axis=channel_axis, keepdims=True)
    variance = jnp.mean(jnp.square(floats - average), axis=channel_axis, keepdims=True)
    return ((floats - average) * lax.rsqrt(variance + epsilon)).astype(jnp.bfloat16)


def project(pair, proj_weight, gate_weight, form):
    normed = normalize(pair, 2)
    linear = jnp.einsum(form, normed, proj_weight, preferred_element_type=jnp.float32)
    logits = jnp.einsum(form, normed, gate_weight, preferred_element_type=jnp.float32)
    return (jax.nn.sigmoid(logits) * linear).astype(jnp.bfloat16)


def shards(
    pair_left,
    pair_right,
    pair_gate,
    left_proj,
    left_gate,
    right_proj,
    right_gate,
    out_gate,
    out_proj,
):
    left_local = project(pair_left, left_proj, left_gate, "ikc,cd->dik")
    right_local = project(pair_right, right_proj, right_gate, "jkc,cd->dkj")
    left_whole = lax.all_gather(left_local, "col", axis=2, tiled=True)
    right_whole = lax.all_gather(right_local, "row", axis=1, tiled=True)
    combined = jnp.einsum(
        "cik,ckj->cij", left_whole, right_whole, preferred_element_type=jnp.float32
    )
    combined_normed = normalize(combined, 0)
    mixed = jnp.einsum("cij,cd->ijd", combined_normed, out_proj, preferred_element_type=jnp.float32)
    gate_normed = normalize(pair_gate, 2)
    logits = jnp.einsum("ijc,cd->ijd", gate_normed, out_gate, preferred_element_type=jnp.float32)
    return (jax.nn.sigmoid(logits) * mixed).astype(jnp.bfloat16)


def solution(mesh):
    placed = (
        P("row", "col", None),
        P("col", "row", None),
        P("row", "col", None),
        P(),
        P(),
        P(),
        P(),
        P(),
        P(),
    )
    return jax.shard_map(
        shards, mesh=mesh, in_specs=placed, out_specs=P("row", "col", None), check_vma=False
    )
```

profile of v0, /device:TPU:0, one launch (start us, length us, event | category | flops | bytes accessed | tf_op | source)
XLA Modules:
  0.0 489.8 jit_solution(15139846752729737639)
XLA Ops:
  6.5 0.0 copy-start
  6.5 0.0 copy-start.2
  6.5 0.0 copy-start.4
  6.5 0.0 all-gather.3.cloned.1.call-start
  6.5 3.2 convert_reduce_fusion.1
  9.8 5.4 %fusion.13 = f32[128,96]{1,0:T(8,128)S(1)} fusion(bf16[128,96,128]{2,1,0:T(8,128)(2,1)} %param.9, f32[128,96]{1,0:T(8,128)S(1)} %broadcast_multiply_fusion.2), kind=kLoop, calls=%fused_computation.19 | loop fusion | flops 6279168 | bytes 3244032 | tf_op jit(solution)/shard_map/reduce_sum | solution.py:12
  15.3 0.0 copy-done.2
  15.3 0.0 copy-done.4
  15.3 6.6 %fusion.18 = f32[128,96,128]{2,1,0:T(8,128)} fusion(bf16[128,96,128]{2,1,0:T(8,128)(2,1)S(1)} %copy-done.2, f32[128,96]{1,0:T(8,128)S(1)} %add_rsqrt_fusion.2, f32[128,96]{1,0:T(8,128)S(1)} %broadcast_multiply_fusion.2, bf16[128,128]{1,0:T(8,128)(2,1)S(1)} %copy-done.4), kind=kOutput, calls=%fused_computation.24 | convolution fusion | flops 408944640 | bytes 9568256 | tf_op jit(solution)/shard_map/ikc,cd->dik/dot_general | solution.py:19
  21.9 0.0 copy-start.5
  21.9 6.7 %copy.13 = f32[128,96,128]{0,1,2:T(8,128)} copy(f32[128,96,128]{2,1,0:T(8,128)} %fusion.18) | data formatting | bytes 12582912 | tf_op jit(solution)/shard_map/ikc,cd->dik/dot_general | solution.py:19
  28.6 0.0 copy-done.5
  28.6 6.5 %fusion.16 = f32[128,96,128]{2,1,0:T(8,128)} fusion(bf16[128,96,128]{2,1,0:T(8,128)(2,1)S(1)} %copy-done.2, f32[128,96]{1,0:T(8,128)S(1)} %add_rsqrt_fusion.2, f32[128,96]{1,0:T(8,128)S(1)} %broadcast_multiply_fusion.2, bf16[128,128]{1,0:T(8,128)(2,1)S(1)} %copy-done.5), kind=kOutput, calls=%fused_computation.23 | convolution fusion | flops 408944640 | bytes 9568256 | tf_op jit(solution)/shard_map/ikc,cd->dik/dot_general | solution.py:18
  35.1 6.7 %copy.14 = f32[128,96,128]{0,1,2:T(8,128)} copy(f32[128,96,128]{2,1,0:T(8,128)} %fusion.16) | data formatting | bytes 12582912 | tf_op jit(solution)/shard_map/ikc,cd->dik/dot_general | solution.py:18
  41.8 0.0 copy-start.3
  41.8 0.0 copy-start.6
  41.8 8.0 %fusion.15 = bf16[128,128,96]{1,2,0:T(8,128)(2,1)} fusion(f32[128,96,128]{0,1,2:T(8,128)} %copy.14, f32[128,96,128]{0,1,2:T(8,128)} %copy.13), kind=kLoop, calls=%fused_computation.22 | loop fusion | flops 7864320 | bytes 15728640 | tf_op jit(solution)/shard_map/convert_element_type | solution.py:20
  49.8 0.0 copy-start.7
  49.8 0.0 all-gather.3.cloned.1.call-update
  49.8 0.2 all-gather.5.cloned.1.call-start
  50.0 0.0 copy-done.3
  50.0 0.3 convert_reduce_fusion.2
  50.3 0.9 fusion.22
  51.3 0.0 copy-done.6
  51.3 2.3 fusion.25
  53.6 0.0 copy-done.7
  53.6 2.3 fusion.24
  55.8 0.0 all-gather.5.cloned.1.call-update
  55.9 0.0 slice-start
  55.9 5.8 %convert_reduce_fusion = f32[128,256]{1,0:T(8,128)S(1)} fusion(bf16[128,256,128]{2,1,0:T(8,128)(2,1)} %param.11), kind=kLoop, calls=%fused_computation.3 | loop fusion | flops 8355840 | bytes 8519680 | tf_op jit(solution)/shard_map/reduce_sum | solution.py:11
  61.7 0.0 slice-start.1
  61.7 11.0 %fusion.4 = f32[128,256]{1,0:T(8,128)S(1)} fusion(bf16[128,256,128]{2,1,0:T(8,128)(2,1)} %param.11, f32[128,256]{1,0:T(8,128)S(1)} %broadcast_multiply_fusion.1), kind=kLoop, calls=%fused_computation.6 | loop fusion | flops 16744448 | bytes 8650752 | tf_op jit(solution)/shard_map/reduce_sum | solution.py:12
  72.8 0.0 copy-done
  72.8 0.0 slice-done
  72.8 0.0 slice-done.1
  72.8 12.9 %fusion.6 = f32[128,256,128]{2,1,0:T(8,128)} fusion(bf16[128,256,128]{2,1,0:T(8,128)(2,1)S(1)} %bitcast.24, f32[128,256]{1,0:T(8,128)S(1)} %add_rsqrt_fusion.1, f32[128,256]{1,0:T(8,128)S(1)} %broadcast_multiply_fusion.1, bf16[128,128]{1,0:T(8,128)(2,1)S(1)} %copy-done), kind=kOutput, calls=%fused_computation.11 | convolution fusion | flops 1090519040 | bytes 25460736 | tf_op jit(solution)/shard_map/ijc,cd->ijd/dot_general | solution.py:44
  85.7 81.1 %all-gather.3.cloned.1.call-done = bf16[128,128,384]{1,2,0:T(8,128)(2,1)} async-done(((bf16[128,128,96]{1,2,0:T(8,128)(2,1)}), bf16[128,128,384]{1,2,0:T(8,128)(2,1)}) %all-gather.3.cloned.1.call-update) | async-done | bytes 12582928 | tf_op jit(solution)/shard_map/all_gather | solution.py:36
  166.9 214.5 %all-gather.5.cloned.1.call-done = bf16[128,384,256]{2,0,1:T(8,128)(2,1)} async-done(((bf16[128,12,256]{2,0,1:T(8,128)(2,1)}), bf16[128,384,256]{2,0,1:T(8,128)(2,1)}) %all-gather.5.cloned.1.call-update) | async-done | bytes 25165840 | tf_op jit(solution)/shard_map/all_gather | solution.py:37
  381.4 62.2 %fusion.34 = (f32[128,256]{1,0:T(8,128)S(1)}, f32[128,128,256]{2,1,0:T(8,128)}) fusion(bf16[128,128,384]{1,2,0:T(8,128)(2,1)} %all-gather.3.cloned.1.call-done, bf16[128,384,256]{2,0,1:T(8,128)(2,1)} %all-gather.5.cloned.1.call-done), kind=kOutput, calls=%fused_computation.48 | convolution fusion | flops 3225387008 | bytes 54657024 | tf_op jit(solution)/shard_map/cik,ckj->cij/dot_general | solution.py:38
  443.7 7.5 %multiply_reduce_fusion = f32[128,256]{1,0:T(8,128)S(1)} fusion(f32[128,128,256]{2,1,0:T(8,128)} %get-tuple-element.6, f32[128,256]{1,0:T(8,128)S(1)} %broadcast_multiply_fusion), kind=kLoop, calls=%fused_computation.10 | loop fusion | flops 12550144 | bytes 17039360 | tf_op jit(solution)/shard_map/reduce_sum | solution.py:12
  451.2 0.0 copy-start.8
  451.2 7.3 %multiply_convert_fusion.1 = bf16[128,128,256]{2,1,0:T(8,128)(2,1)S(1)} fusion(f32[128,128,256]{2,1,0:T(8,128)} %get-tuple-element.6, f32[128,256]{1,0:T(8,128)S(1)} %add_rsqrt_fusion, f32[128,256]{1,0:T(8,128)S(1)} %broadcast_multiply_fusion), kind=kLoop, calls=%fused_computation.9 | loop fusion | flops 12582912 | bytes 25427968 | tf_op jit(solution)/shard_map/convert_element_type | solution.py:13
  458.6 0.0 copy-done.8
  458.6 0.0 copy-start.1
  458.6 24.0 %multiply_convert_fusion = bf16[128,256,128]{2,1,0:T(8,128)(2,1)} fusion(f32[128,256,128]{2,1,0:T(8,128)} %fusion.6, bf16[128,128,256]{2,1,0:T(8,128)(2,1)S(1)} %multiply_convert_fusion.1, bf16[128,128]{1,0:T(8,128)(2,1)S(1)} %copy-done.8), kind=kOutput, calls=%fused_computation.8 | convolution fusion | flops 1094713344 | bytes 33587200 | tf_op jit(solution)/shard_map/cij,cd->ijd/dot_general | solution.py:42
  482.6 0.0 copy-done.1
  (9 shorter events, 0.1 us)
Async XLA Ops:
  6.5 66.2 %copy-start = (bf16[128,128]{1,0:T(8,128)(2,1)S(1)}, bf16[128,128]{1,0:T(8,128)(2,1)}, u32[]{:S(2)}) copy-start(bf16[128,128]{1,0:T(8,128)(2,1)} %param.16) | copy-start | bytes 98308
  6.5 8.7 %copy-start.2 = (bf16[128,96,128]{2,1,0:T(8,128)(2,1)S(1)}, bf16[128,96,128]{2,1,0:T(8,128)(2,1)}, u32[]{:S(2)}) copy-start(bf16[128,96,128]{2,1,0:T(8,128)(2,1)} %param.9) | copy-start | bytes 9437188
  6.5 8.7 %copy-start.4 = (bf16[128,128]{1,0:T(8,128)(2,1)S(1)}, bf16[128,128]{1,0:T(8,128)(2,1)}, u32[]{:S(2)}) copy-start(bf16[128,128]{1,0:T(8,128)(2,1)} %param.13) | copy-start | bytes 98308
  6.5 160.4 %all-gather.3.cloned.1.call-start = ((), (), s32[]{:S(2)}) async-start(), calls=%async_computation | async-start | bytes 15728640 | tf_op jit(solution)/shard_map/all_gather | solution.py:36
  21.9 6.7 %copy-start.5 = (bf16[128,128]{1,0:T(8,128)(2,1)S(1)}, bf16[128,128]{1,0:T(8,128)(2,1)}, u32[]{:S(2)}) copy-start(bf16[128,128]{1,0:T(8,128)(2,1)} %param.12) | copy-start | bytes 98308
  41.8 8.2 %copy-start.3 = (bf16[256,12,128]{2,0,1:T(8,128)(2,1)S(1)}, bf16[256,12,128]{2,0,1:T(8,128)(2,1)}, u32[]{:S(2)}) copy-start(bf16[256,12,128]{2,0,1:T(8,128)(2,1)} %param.10) | copy-start | bytes 2359300
  41.8 9.5 %copy-start.6 = (bf16[128,128]{1,0:T(8,128)(2,1)S(1)}, bf16[128,128]{1,0:T(8,128)(2,1)}, u32[]{:S(2)}) copy-start(bf16[128,128]{1,0:T(8,128)(2,1)} %param.14) | copy-start | bytes 98308
  49.8 3.8 copy-start.7
  49.8 331.6 %all-gather.5.cloned.1.call-start = ((), (), s32[]{:S(2)}) async-start(), calls=%async_computation.1 | async-start | bytes 25952256 | tf_op jit(solution)/shard_map/all_gather | solution.py:37
  55.9 16.9 %slice-start = ((s8[8388608]{0:T(1024)(128)(4,1)}), s8[4194304]{0:T(1024)(128)(4,1)S(1)}, s32[]{:S(2)}) async-start(s8[8388608]{0:T(1024)(128)(4,1)} %bitcast.23), calls=%async_computation.2 | async-start | bytes 8388608
  61.7 11.1 %slice-start.1 = ((s8[8388608]{0:T(1024)(128)(4,1)}), s8[4194304]{0:T(1024)(128)(4,1)S(1)}, s32[]{:S(2)}) async-start(s8[8388608]{0:T(1024)(128)(4,1)} %bitcast.23), calls=%async_computation.3 | async-start | bytes 8388608
  451.2 7.4 %copy-start.8 = (bf16[128,128]{1,0:T(8,128)(2,1)S(1)}, bf16[128,128]{1,0:T(8,128)(2,1)}, u32[]{:S(2)}) copy-start(bf16[128,128]{1,0:T(8,128)(2,1)} %param.17) | copy-start | bytes 98308
  458.6 24.0 %copy-start.1 = (bf16[128,128]{1,0:T(8,128)(2,1)S(1)}, bf16[128,128]{1,0:T(8,128)(2,1)}, u32[]{:S(2)}) copy-start(bf16[128,128]{1,0:T(8,128)(2,1)} %param.16) | copy-start | bytes 98308
Sparse Core Ops, SparseCore 0:
  49.9 116.9 all-gather.2
  169.8 211.5 all-gather.4
where the time goes:
time: 495 us; the launch traced here: 490 us
  waiting for transfers between devices  296 us (60%)
  matrix products  117 us (24%)
  other arithmetic  49.6 us (10%)
  between operations  14.1 us (3%)
  local copies, waits for them, and re-layouts  13.5 us (3%)
    all_gather x1, waiting for transfers between devices, shards(): right_whole = lax.all_gather(right_local, 'row', axis=1, tiled=True)  215 us
    all_gather x1, waiting for transfers between devices, shards(): left_whole = lax.all_gather(left_local, 'col', axis=2, tiled=True)  81.1 us
    dot_general x1, matrix products, shards(): jnp.einsum('cik,ckj->cij', left_whole, right_whole, preferred_element_typ...  62.2 us
    reduce_sum x4, other arithmetic, normalize(): jnp.mean(jnp.square(floats - average), axis=channel_axis, keepdims=True)  24.8 us
    dot_general x1, matrix products, shards(): jnp.einsum('cij,cd->ijd', combined_normed, out_proj, preferred_element_ty...  24 us
    dot_general x1, matrix products, shards(): jnp.einsum('ijc,cd->ijd', gate_normed, out_gate, preferred_element_type=j...  12.9 us
  transfers between devices with their start and end apart: 2, of which 2 were waited for; matrix products, arithmetic and copies ran while one was open for 7% of the time, Pallas kernels for 0%

commit v1 on v0

v1 whole, which is shorter than its diff:
```python
import functools

import jax
import jax.numpy as jnp
from jax import lax
from jax.experimental import pallas as pl
from jax.experimental.pallas import tpu as pltpu
from jax.sharding import PartitionSpec as P

epsilon = 1e-05
AXES = ("row", "col")
NX, NY, NZ = 4, 4, 4
VMEM_LIMIT = 56 * 1024 * 1024
CHANNELS = 128
SHORT = pl.CostEstimate(flops=1000, bytes_accessed=1000, transcendentals=0)


def device_index(x, y, z, core):
    return (((z // 2) * NX + x) * NY + y) * 4 + (z % 2) * 2 + core


def permutation(move):
    pairs = []
    for x in range(NX):
        for y in range(NY):
            for z in range(NZ):
                for core in range(2):
                    tx, ty, tz, tc = move(x, y, z, core)
                    pairs.append(
                        (
                            device_index(x, y, z, core),
                            device_index(tx % NX, ty % NY, tz % NZ, tc % 2),
                        )
                    )
    return pairs


RING_X = permutation(lambda x, y, z, c: (x + 1 - 2 * c, y, z, c))
RING_Y = permutation(lambda x, y, z, c: (x, y + 1 - 2 * c, z, c))
SWAP_Z_HI = permutation(lambda x, y, z, c: (x, y, z + 2, c))
SWAP_Z_LO = permutation(lambda x, y, z, c: (x, y, z + 1 - 2 * (z % 2), c))
SWAP_CORE = permutation(lambda x, y, z, c: (x, y, z, c + 1))


def normed_rows(values):
    floats = values.astype(jnp.float32)
    average = jnp.mean(floats, axis=-1, keepdims=True)
    centred = floats - average
    variance = jnp.mean(centred * centred, axis=-1, keepdims=True)
    return centred * lax.rsqrt(variance + epsilon)


def gated(both):
    return jax.nn.sigmoid(both[CHANNELS:]) * both[:CHANNELS]


def contract_last(a, b):
    return lax.dot_general(
        a, b, (((1,), (1,)), ((), ())), preferred_element_type=jnp.float32
    )


def both_weights(proj_ref, gate_ref):
    return jnp.concatenate([proj_ref[...].T, gate_ref[...].T], axis=0)


def left_kernel(x_ref, proj_ref, gate_ref, o_ref, rows, turned):
    n_i, n_k, _ = x_ref.shape
    rows[...] = normed_rows(x_ref[...]).reshape(n_i * n_k, CHANNELS)
    w = both_weights(proj_ref, gate_ref)
    for k in range(n_k):
        normed = rows[pl.ds(k, n_i, stride=n_k), :].astype(jnp.bfloat16)
        turned[pl.ds(k, CHANNELS, stride=n_k), :] = gated(contract_last(w, normed))
    o_ref[...] = turned[...].reshape(CHANNELS, n_k, n_i).astype(jnp.bfloat16)


def project_left(pair, proj, gate):
    n_i, n_k, _ = pair.shape
    block = 16
    return pl.pallas_call(
        left_kernel,
        grid=(n_k // block,),
        in_specs=[
            pl.BlockSpec((n_i, block, CHANNELS), lambda s: (0, s, 0)),
            pl.BlockSpec((CHANNELS, CHANNELS), lambda s: (0, 0)),
            pl.BlockSpec((CHANNELS, CHANNELS), lambda s: (0, 0)),
        ],
        out_specs=pl.BlockSpec((CHANNELS, block, n_i), lambda s: (0, s, 0)),
        out_shape=jax.ShapeDtypeStruct((CHANNELS, n_k, n_i), jnp.bfloat16),
        scratch_shapes=[
            pltpu.VMEM((n_i * block, CHANNELS), jnp.float32),
            pltpu.VMEM((CHANNELS * block, n_i), jnp.float32),
        ],
        compiler_params=pltpu.CompilerParams(vmem_limit_bytes=VMEM_LIMIT),
        cost_estimate=SHORT,
        name="project_left",
    )(pair, proj, gate)


def right_kernel(own_ref, other_ref, proj_ref, gate_ref, x_out, y_out, turned):
    n_k, n_j, _ = own_ref.shape
    w = both_weights(proj_ref, gate_ref)
    for at, ref in ((0, own_ref), (n_k, other_ref)):
        normed = normed_rows(ref[...]).astype(jnp.bfloat16)
        for k in range(n_k):
            turned[pl.ds(at + k, CHANNELS, stride=2 * n_k), :] = gated(contract_last(w, normed[k]))
    half = CHANNELS // 2
    whole = turned[...].reshape(CHANNELS, 2 * n_k, n_j).astype(jnp.bfloat16)
    x_out[...] = whole[:half]
    y_out[...] = whole[half:]


def project_right(own, other, proj, gate):
    n_k, n_j, _ = own.shape
    half = jax.ShapeDtypeStruct((CHANNELS // 2, 2 * n_k, n_j), jnp.bfloat16)
    return pl.pallas_call(
        right_kernel,
        out_shape=(half, half),
        scratch_shapes=[pltpu.VMEM((CHANNELS * 2 * n_k, n_j), jnp.float32)],
        compiler_params=pltpu.CompilerParams(vmem_limit_bytes=VMEM_LIMIT),
        cost_estimate=SHORT,
        name="project_right",
    )(own, other, proj, gate)


def gate_kernel(x_ref, w_ref, o_ref):
    n_i, n_j, _ = x_ref.shape
    normed = normed_rows(x_ref[...]).reshape(n_i * n_j, CHANNELS).astype(jnp.bfloat16)
    logits = jnp.dot(normed, w_ref[...], preferred_element_type=jnp.float32)
    o_ref[...] = jax.nn.sigmoid(logits).reshape(n_i, n_j, CHANNELS).astype(jnp.bfloat16)


def gate_values(pair, weights, at, n_j):
    n_i = pair.shape[0]
    block = 16
    return pl.pallas_call(
        gate_kernel,
        grid=(n_i // block,),
        in_specs=[
            pl.BlockSpec((block, n_j, CHANNELS), lambda s: (s, at, 0)),
            pl.BlockSpec((CHANNELS, CHANNELS), lambda s: (0, 0)),
        ],
        out_specs=pl.BlockSpec((block, n_j, CHANNELS), lambda s: (s, 0, 0)),
        out_shape=jax.ShapeDtypeStruct((n_i, n_j, CHANNELS), jnp.bfloat16),
        compiler_params=pltpu.CompilerParams(vmem_limit_bytes=VMEM_LIMIT),
        cost_estimate=SHORT,
        name="gate_values",
    )(pair, weights)


def arrange_kernel(a_ref, b_ref, c_ref, d_ref, order_ref, *rest):
    o_ref = rest[-1]
    order = order_ref[0]
    for ch in range(o_ref.shape[0]):
        rows = jnp.concatenate([a_ref[ch], b_ref[ch], c_ref[ch], d_ref[ch]], axis=0)
        o_ref[ch] = lax.dot_general(
            rows, order, (((0,), (0,)), ((), ())), preferred_element_type=jnp.float32
        ).astype(jnp.bfloat16)


def arrange_left(parts, orders, first, whole=None):
    n_c, n_k, n_i = parts[0].shape
    block = 8
    depth = 4 * n_k
    steps = n_c // 2 // block
    in_specs = [pl.BlockSpec((block, n_k, n_i), lambda s: (s + first * steps, 0, 0))] * 4 + [
        pl.BlockSpec((1, depth, depth), lambda s: (first, 0, 0))
    ]
    operands = [*parts, orders]
    aliases = {}
    if whole is not None:
        in_specs.append(pl.BlockSpec(memory_space=pl.ANY))
        aliases = {len(operands): 0}
        operands.append(whole)
    return pl.pallas_call(
        arrange_kernel,
        grid=(steps,),
        in_specs=in_specs,
        out_specs=pl.BlockSpec((block, n_i, depth), lambda s: (s + first * steps, 0, 0)),
        out_shape=jax.ShapeDtypeStruct((n_c, n_i, depth), jnp.bfloat16),
        input_output_aliases=aliases,
        compiler_params=pltpu.CompilerParams(vmem_limit_bytes=VMEM_LIMIT),
        cost_estimate=SHORT,
        name="arrange_left",
    )(*operands)


def left_orders():
    row, col = lax.axis_index("row"), lax.axis_index("col")
    z_hi, x, y = row // 16, (row // 4) % 4, row % 4
    z_lo, core = col // 2, col % 2
    sign = 1 - 2 * core
    depth = 384
    k = lax.broadcasted_iota(jnp.int32, (depth, depth), 1)
    source = lax.broadcasted_iota(jnp.int32, (depth, depth), 0)
    second, first, z_rel, within = k // 96, (k // 24) % 4, (k // 12) % 2, k % 12
    z_abs = z_hi ^ z_rel

    def order(x_rel, y_rel):
        x_abs = (x - sign * x_rel) % 4
        y_abs = (y - sign * y_rel) % 4
        part = (z_abs ^ z_lo) * 2 + ((x_abs // 2) ^ core)
        return part * 96 + (x_abs % 2) * 48 + y_abs * 12 + within == source

    return jnp.stack([order(first, second), order(second, first)]).astype(jnp.bfloat16)


def update_kernel(n_sum, lx_ref, ly_ref, *refs):
    x_refs, y_refs, (s_ref, w_ref), (o_ref, combined) = refs[:4], refs[4:8], refs[8:10], refs[-2:]
    step = pl.program_id(0)

    @pl.when(step < n_sum)
    def _():
        n_c, n_i, _ = lx_ref.shape
        for at, l_ref, parts in ((0, lx_ref, x_refs), (CHANNELS // 2, ly_ref, y_refs)):
            for ch in range(n_c):
                right = jnp.concatenate([r[ch] for r in parts], axis=0)
                product = jnp.dot(l_ref[ch], right, preferred_element_type=jnp.float32)
                combined[pl.ds(at + step * n_c + ch, n_i, stride=CHANNELS), :] = product

    @pl.when(step >= n_sum)
    def _():
        block = o_ref.shape[0]
        w = w_ref[...]
        first = pl.multiple_of((step - n_sum) * block * CHANNELS, block * CHANNELS)
        for i in range(block):
            values = combined[pl.ds(first + i * CHANNELS, CHANNELS), :]
            average = jnp.mean(values, axis=0, keepdims=True)
            centred = values - average
            variance = jnp.mean(centred * centred, axis=0, keepdims=True)
            normed = (centred * lax.rsqrt(variance + epsilon)).astype(jnp.bfloat16)
            mixed = lax.dot_general(
                normed, w, (((0,), (0,)), ((), ())), preferred_element_type=jnp.float32
            )
            o_ref[i] = (mixed * s_ref[i].astype(jnp.float32)).astype(jnp.bfloat16)


def update_block(left, x_parts, y_parts, gate, weights, at, n_blocks, part, n_parts, whole=None):
    n_c, n_i, depth = left.shape
    half, n_k, n_j = x_parts[0].shape
    c_block, i_block = 16, 16
    rows = n_i // n_parts
    n_sum = half // c_block
    n_out = rows // i_block
    within = lambda s: jnp.minimum(s, n_sum - 1)
    out_at = lambda s: jnp.maximum(s - n_sum, 0) + part * n_out
    in_specs = (
        [
            pl.BlockSpec((c_block, rows, depth), lambda s: (within(s), part, 0)),
            pl.BlockSpec((c_block, rows, depth), lambda s: (within(s) + n_sum, part, 0)),
        ]
        + [pl.BlockSpec((c_block, n_k, n_j), lambda s: (within(s), 0, 0))] * 8
        + [
            pl.BlockSpec((i_block, n_j, CHANNELS), lambda s: (out_at(s), 0, 0)),
            pl.BlockSpec((CHANNELS, CHANNELS), lambda s: (0, 0)),
        ]
    )
    operands = [left, left, *x_parts, *y_parts, gate, weights]
    aliases = {}
    if whole is not None:
        in_specs.append(pl.BlockSpec(memory_space=pl.ANY))
        aliases = {len(operands): 0}
        operands.append(whole)
    return pl.pallas_call(
        functools.partial(update_kernel, n_sum),
        grid=(n_sum + n_out,),
        in_specs=in_specs,
        out_specs=pl.BlockSpec((i_block, n_j, CHANNELS), lambda s: (out_at(s), at, 0)),
        out_shape=jax.ShapeDtypeStruct((n_i, n_blocks * n_j, CHANNELS), jnp.bfloat16),
        scratch_shapes=[pltpu.VMEM((rows * CHANNELS, n_j), jnp.float32)],
        input_output_aliases=aliases,
        compiler_params=pltpu.CompilerParams(vmem_limit_bytes=VMEM_LIMIT),
        cost_estimate=SHORT,
        name="update_block",
    )(*operands)


def after(value, *others):
    return lax.optimization_barrier((value, *others))[0]


def step_on(pieces, rings, *others):
    ready = lax.optimization_barrier((*(held[-1] for held in pieces), *others))
    for held, ring, piece in zip(pieces, rings, ready):
        held.append(lax.ppermute(piece, AXES, ring))


def joined(pieces):
    return [[jnp.concatenate(held, axis=1)] for held in pieces]


def shards(
    pair_left,
    pair_right,
    pair_gate,
    left_proj,
    left_gate,
    right_proj,
    right_gate,
    out_gate,
    out_proj,
):
    right = jnp.transpose(pair_right, (1, 0, 2))
    n_j = 128
    n_blocks = right.shape[1] // n_j
    first_rings, second_rings = (RING_X, RING_Y), (RING_Y, RING_X)

    blocks = [right[:, b * n_j : (b + 1) * n_j] for b in range(n_blocks)]
    others = [lax.ppermute(block, AXES, SWAP_Z_HI) for block in blocks]
    left_local = project_left(pair_left, left_proj, left_gate)
    halves_0 = project_right(blocks[0], after(others[0], left_local), right_proj, right_gate)
    f0 = [[half] for half in halves_0]
    step_on(f0, first_rings)
    halves_1 = project_right(blocks[1], after(others[1], halves_0[0]), right_proj, right_gate)
    f1 = [[half] for half in halves_1]
    step_on(f1, first_rings)
    left_sent = after(left_local, others[1])
    left_far = lax.ppermute(left_sent, AXES, SWAP_Z_LO)
    step_on(f0, first_rings)
    step_on(f1, first_rings)
    step_on(f0, first_rings)
    step_on(f1, first_rings)
    c0 = joined(f0)
    step_on(c0, second_rings)
    c1 = joined(f1)
    step_on(c1, second_rings)
    gate_0 = gate_values(pair_gate, after(out_gate, c0[0][0], c0[1][0], c1[0][0], c1[1][0]), 0, n_j)
    left_core = lax.ppermute(after(left_local, f1[0][-1]), AXES, SWAP_CORE)
    step_on(c0, second_rings, gate_0)
    gate_1 = gate_values(pair_gate, after(out_gate, gate_0, c0[0][1], c0[1][1]), 1, n_j)
    left_far_core = lax.ppermute(after(left_far, gate_1), AXES, SWAP_CORE)
    parts = (left_local, left_core, left_far, left_far_core)
    orders = left_orders()
    left = arrange_left(parts, orders, 0)
    step_on(c0, second_rings, left)
    step_on(c1, second_rings, left, c0[0][2], c0[1][2])
    left = arrange_left(parts, after(orders, c0[0][2]), 1, left)
    whole = update_block(left, *c0, gate_0, out_proj, 0, n_blocks, 0, 2)
    step_on(c1, second_rings, whole)
    whole = update_block(
        left, *c0, gate_0, after(out_proj, c1[0][2], c1[1][2]), 0, n_blocks, 1, 2, whole
    )
    return update_block(left, *c1, gate_1, out_proj, 1, n_blocks, 0, 1, whole)


def solution(mesh):
    placed = (
        P("row", "col", None),
        P("col", "row", None),
        P("row", "col", None),
        P(),
        P(),
        P(),
        P(),
        P(),
        P(),
    )
    return jax.shard_map(
        shards, mesh=mesh, in_specs=placed, out_specs=P("row", "col", None), check_vma=False
    )
```

time: 495 us -> 233 us (0.47)
  waiting for transfers between devices: 296 us -> 81.4 us
  matrix products: 117 us -> 0 us
  Pallas kernels: 0 us -> 106 us
  other arithmetic: 49.6 us -> 1.24 us
  starting transfers between devices: 0.22 us -> 24 us
  between operations: 14.1 us -> 0.18 us
    all_gather x2 -> x0, waiting for transfers between devices: 296 us -> none  [the longest x1 215 us: shards(): right_whole = lax.all_gather(right_local, 'row', axis=1, tiled=True)]
    dot_general x7 -> x0, matrix products: 117 us -> none  [the longest x1 62.2 us: shards(): jnp.einsum('cik,ckj->cij', left_whole, right_whole, preferred_element_typ...]
    pallas_call x0 -> x10, Pallas kernels: none -> 106 us  [the longest x3 48.6 us: update_block(): pl.pallas_call(functools.partial(update_kernel, n_sum), grid=(n_sum + n_o...]
    ppermute x0 -> x29, waiting for transfers between devices: none -> 81.4 us  [the longest x24 74.3 us: step_on(): held.append(lax.ppermute(piece, AXES, ring))]
    reduce_sum x7 -> x0, other arithmetic: 34.1 us -> none  [the longest x4 24.8 us: normalize(): jnp.mean(jnp.square(floats - average), axis=channel_axis, keepdims=True)]
    ppermute x0 -> x29, starting transfers between devices: none -> 24 us  [the longest x24 18.3 us: step_on(): held.append(lax.ppermute(piece, AXES, ring))]
    convert_element_type x2 -> x1, other arithmetic: 15.3 us -> 0.94 us  [left_orders(): jnp.stack([order(first, second), order(second, first)]).astype(jnp.bfloat16)]
    unnamed x22 -> x46, local copies, waits for them, and re-layouts: 0.05 us -> 14.1 us
  transfers between devices with their start and end apart: 2 -> 29, of which waited for: 2 -> 20; matrix products, arithmetic and copies ran while one was open for 7% -> 6% of each run, Pallas kernels for 0% -> 36%
where the time goes in v1:
time: 233 us; the launch traced here: 231 us
  Pallas kernels  106 us (45%)
  waiting for transfers between devices  81.4 us (35%)
  starting transfers between devices  24 us (10%)
  local copies, waits for them, and re-layouts  17.9 us (8%)
    ppermute x24, waiting for transfers between devices, step_on(): held.append(lax.ppermute(piece, AXES, ring))  74.3 us
    pallas_call x3, Pallas kernels, update_block(): pl.pallas_call(functools.partial(update_kernel, n_sum), grid=(n_sum + n_o...  48.6 us
    pallas_call x2, Pallas kernels, arrange_left(): pl.pallas_call(arrange_kernel, grid=(steps,), in_specs=in_specs, out_spec...  21 us
    pallas_call x2, Pallas kernels, gate_values(): pl.pallas_call(gate_kernel, grid=(n_i // block,), in_specs=[pl.BlockSpec(...  19.2 us
    ppermute x24, starting transfers between devices, step_on(): held.append(lax.ppermute(piece, AXES, ring))  18.3 us
    unnamed x46, local copies, waits for them, and re-layouts  14.1 us
    pallas_call x1, Pallas kernels, project_left(): pl.pallas_call(left_kernel, grid=(n_k // block,), in_specs=[pl.BlockSpec(...  10.5 us
    pallas_call x2, Pallas kernels, project_right(): pl.pallas_call(right_kernel, out_shape=(half, half), scratch_shapes=[pltp...  6.8 us
  transfers between devices with their start and end apart: 29, of which 20 were waited for; matrix products, arithmetic and copies ran while one was open for 6% of the time, Pallas kernels for 36%

profile of v1, /device:TPU:0, one launch (start us, length us, event | category | flops | bytes accessed | tf_op | source)
XLA Modules:
  0.0 230.8 jit_solution(1094008632342676403)
XLA Ops:
  0.0 1.2 fusion.44
  1.2 4.0 %collective-permute-start = (bf16[12,128,128]{2,1,0:T(8,128)(2,1)S(1)}, bf16[12,128,128]{2,1,0:T(8,128)(2,1)S(1)}, u32[]{:S(2)}, u32[]{:S(2)}) collective-permute-start(bf16[12,128,128]{2,1,0:T(8,128)(2,1)S(1)} %get-tuple-element.80.own_ref), channel_id=1, source_target_pairs={{0,64},{1,65},{2,66},{3,67},{64,0},{65,1},{66,2},{67,3},{4,68},{5,... | collective-permute-start | bytes 1179656 | tf_op jit(solution)/shard_map/ppermute | solution.py:309
  5.3 10.5 %project_left.1.a_ref = bf16[128,96,128]{2,1,0:T(8,128)(2,1)} custom-call(bf16[128,96,128]{2,1,0:T(8,128)(2,1)} %x_ref.3, bf16[128,128]{1,0:T(8,128)(2,1)} %proj_ref.3, bf16[128,128]{1,0:T(8,128)(2,1)} %gate_ref.3), custom_call_target="tpu_custom_call" | custom-call | flops 1000 | bytes 1000 | tf_op jit(solution)/shard_map/project_left/pallas_call | solution.py:80
  15.8 1.6 collective-permute-start.8
  17.4 6.2 %collective-permute-done.1.other_ref = bf16[12,128,128]{2,1,0:T(8,128)(2,1)S(1)} collective-permute-done((bf16[12,128,128]{2,1,0:T(8,128)(2,1)S(1)}, bf16[12,128,128]{2,1,0:T(8,128)(2,1)S(1)}, u32[]{:S(2)}, u32[]{:S(2)}) %collective-permute-start.1) | collective-permute-done | bytes 393248 | tf_op jit(solution)/shard_map/ppermute | solution.py:309
  23.6 0.8 copy-done.16
  24.4 3.4 %project_right.2 = (bf16[64,24,128]{2,1,0:T(8,128)(2,1)}, bf16[64,24,128]{2,1,0:T(8,128)(2,1)}) custom-call(bf16[12,128,128]{2,1,0:T(8,128)(2,1)} %copy-done.6, bf16[12,128,128]{2,1,0:T(8,128)(2,1)} %copy-done.16, bf16[128,128]{1,0:T(8,128)(2,1)} %proj_ref.5, bf16[128,128]{1,0:T(8,128)(2,1)} %gate_ref.5), custom_call_target="tpu_custom_call" | custom-call | flops 1000 | bytes 1000 | tf_op jit(solution)/shard_map/project_right/pallas_call | solution.py:116
  27.8 1.5 collective-permute-start.9
  29.3 1.6 collective-permute-start.10
  30.9 3.4 %project_right.3 = (bf16[64,24,128]{2,1,0:T(8,128)(2,1)}, bf16[64,24,128]{2,1,0:T(8,128)(2,1)}) custom-call(bf16[12,128,128]{2,1,0:T(8,128)(2,1)} %copy-done.5, bf16[12,128,128]{2,1,0:T(8,128)(2,1)} %copy-done.15, bf16[128,128]{1,0:T(8,128)(2,1)} %proj_ref.5, bf16[128,128]{1,0:T(8,128)(2,1)} %gate_ref.5), custom_call_target="tpu_custom_call" | custom-call | flops 1000 | bytes 1000 | tf_op jit(solution)/shard_map/project_right/pallas_call | solution.py:116
  34.2 1.5 collective-permute-start.2
  35.7 1.6 collective-permute-start.3
  37.3 1.2 collective-permute-done.10
  38.5 1.5 collective-permute-start.11
  40.3 3.1 %collective-permute-done.2 = bf16[64,24,128]{2,1,0:T(8,128)(2,1)S(1)} collective-permute-done((bf16[64,24,128]{2,1,0:T(8,128)(2,1)}, bf16[64,24,128]{2,1,0:T(8,128)(2,1)S(1)}, u32[]{:S(2)}, u32[]{:S(2)}) %collective-permute-start.2) | collective-permute-done | bytes 393248 | tf_op jit(solution)/shard_map/ppermute | solution.py:285
  43.4 1.5 collective-permute-done.3
  44.9 1.2 collective-permute-start.4
  46.5 1.0 constant_dynamic-update-slice_fusion.3
  47.6 0.9 constant_dynamic-update-slice_fusion.7
  48.4 0.7 collective-permute-done.12
  49.1 0.6 collective-permute-start.14
  49.7 0.9 constant_dynamic-update-slice_fusion.6
  50.6 1.0 collective-permute-start.13
  51.7 2.3 collective-permute-done.4
  53.9 1.2 collective-permute-done.5
  55.6 0.9 constant_dynamic-update-slice_fusion.5
  56.6 2.8 %collective-permute-done.14 = bf16[64,24,128]{2,1,0:T(8,128)(2,1)S(1)} collective-permute-done((bf16[64,24,128]{2,1,0:T(8,128)(2,1)S(1)}, bf16[64,24,128]{2,1,0:T(8,128)(2,1)S(1)}, u32[]{:S(2)}, u32[]{:S(2)}) %collective-permute-start.14) | collective-permute-done | bytes 393248 | tf_op jit(solution)/shard_map/ppermute | solution.py:285
  59.3 0.9 constant_dynamic-update-slice_fusion.4.refs_4_
  60.9 3.2 %collective-permute-done.6 = bf16[64,24,128]{2,1,0:T(8,128)(2,1)S(1)} collective-permute-done((bf16[64,24,128]{2,1,0:T(8,128)(2,1)S(1)}, bf16[64,24,128]{2,1,0:T(8,128)(2,1)S(1)}, u32[]{:S(2)}, u32[]{:S(2)}) %collective-permute-start.6) | collective-permute-done | bytes 393248 | tf_op jit(solution)/shard_map/ppermute | solution.py:285
  64.1 0.8 constant_dynamic-update-slice_fusion.11
  65.0 0.9 constant_dynamic-update-slice_fusion.15
  65.8 0.9 constant_dynamic-update-slice_fusion.10
  66.7 0.7 collective-permute-start.15
  67.4 0.8 constant_dynamic-update-slice_fusion.14
  68.3 0.9 constant_dynamic-update-slice_fusion.9
  69.2 0.8 constant_dynamic-update-slice_fusion.13
  70.0 0.9 constant_dynamic-update-slice_fusion.8.refs_0_
  70.9 15.3 %collective-permute-done.15 = bf16[64,24,128]{2,1,0:T(8,128)(2,1)S(1)} collective-permute-done((bf16[64,24,128]{2,1,0:T(8,128)(2,1)S(1)}, bf16[64,24,128]{2,1,0:T(8,128)(2,1)S(1)}, u32[]{:S(2)}, u32[]{:S(2)}) %collective-permute-start.15) | collective-permute-done | bytes 393248 | tf_op jit(solution)/shard_map/ppermute | solution.py:285
  86.2 0.9 constant_dynamic-update-slice_fusion.12.refs_4_
  87.1 9.6 %gate_values.2.refs_8_ = bf16[128,128,128]{2,1,0:T(8,128)(2,1)} custom-call(bf16[128,256,128]{2,1,0:T(8,128)(2,1)} %x_ref.5, bf16[128,128]{1,0:T(8,128)(2,1)} %w_ref.1), custom_call_target="tpu_custom_call" | custom-call | flops 1000 | bytes 1000 | tf_op jit(solution)/shard_map/gate_values/pallas_call | solution.py:136
  96.7 9.6 %gate_values.3.refs_8_ = bf16[128,128,128]{2,1,0:T(8,128)(2,1)} custom-call(bf16[128,256,128]{2,1,0:T(8,128)(2,1)} %x_ref.5, bf16[128,128]{1,0:T(8,128)(2,1)} %w_ref.1), custom_call_target="tpu_custom_call" | custom-call | flops 1000 | bytes 1000 | tf_op jit(solution)/shard_map/gate_values/pallas_call | solution.py:136
  106.9 0.6 collective-permute-start.20
  107.5 1.7 copy-done.1
  109.2 0.9 collective-permute-start.21
  110.5 0.9 add_convert_fusion.order_ref
  111.4 0.9 collective-permute-done.18.d_ref
  112.3 10.5 %arrange_left.2.rest_0_ = bf16[128,128,384]{2,1,0:T(8,128)(2,1)} custom-call(bf16[128,96,128]{2,1,0:T(8,128)(2,1)} %project_left.1.a_ref, bf16[128,96,128]{2,1,0:T(8,128)(2,1)} %copy-done.1, bf16[128,96,128]{2,1,0:T(8,128)(2,1)} %collective-permute-done.8.c_ref, bf16[128,96,128]{2,1,0:T(8,128)(2,1)} %collective-permute-done.18.d_ref, ...), custom_call_target="tpu_custom_call" | custom-call | flops 1000 | bytes 1000 | tf_op jit(solution)/shard_map/arrange_left/pallas_call | solution.py:175
  122.8 5.5 %collective-permute-done.19.refs_2_ = bf16[64,96,128]{2,1,0:T(8,128)(2,1)} collective-permute-done((bf16[64,96,128]{2,1,0:T(8,128)(2,1)}, bf16[64,96,128]{2,1,0:T(8,128)(2,1)}, u32[]{:S(2)}, u32[]{:S(2)}) %collective-permute-start.19) | collective-permute-done | bytes 1572896 | tf_op jit(solution)/shard_map/ppermute | solution.py:285
  128.4 16.8 %collective-permute-done.20.refs_1_ = bf16[64,96,128]{2,1,0:T(8,128)(2,1)} collective-permute-done((bf16[64,96,128]{2,1,0:T(8,128)(2,1)}, bf16[64,96,128]{2,1,0:T(8,128)(2,1)}, u32[]{:S(2)}, u32[]{:S(2)}) %collective-permute-start.20) | collective-permute-done | bytes 1572896 | tf_op jit(solution)/shard_map/ppermute | solution.py:285
  145.2 1.0 collective-permute-start.25
  146.2 1.1 collective-permute-start.23
  147.3 10.5 %arrange_left.3.lx_ref.ly_ref = bf16[128,128,384]{2,1,0:T(8,128)(2,1)} custom-call(bf16[128,96,128]{2,1,0:T(8,128)(2,1)} %project_left.1.a_ref, bf16[128,96,128]{2,1,0:T(8,128)(2,1)} %copy-done.1, bf16[128,96,128]{2,1,0:T(8,128)(2,1)} %collective-permute-done.8.c_ref, ...), custom_call_target="tpu_custom_call", output_to_operand_aliasing={{}: (5, {})} | custom-call | flops 1000 | bytes 1000 | tf_op jit(solution)/shard_map/arrange_left/pallas_call | solution.py:175
  157.8 9.2 %collective-permute-done.25.refs_3_ = bf16[64,96,128]{2,1,0:T(8,128)(2,1)S(1)} collective-permute-done((bf16[64,96,128]{2,1,0:T(8,128)(2,1)}, bf16[64,96,128]{2,1,0:T(8,128)(2,1)S(1)}, u32[]{:S(2)}, u32[]{:S(2)}) %collective-permute-start.25) | collective-permute-done | bytes 1572896 | tf_op jit(solution)/shard_map/ppermute | solution.py:285
  167.0 1.0 collective-permute-done.26.refs_7_
  168.2 1.1 copy-done.4
  169.4 13.3 %update_block.3.refs_10_ = bf16[128,256,128]{2,1,0:T(8,128)(2,1)} custom-call(bf16[128,128,384]{2,1,0:T(8,128)(2,1)} %arrange_left.3.lx_ref.ly_ref, bf16[128,128,384]{2,1,0:T(8,128)(2,1)} %arrange_left.3.lx_ref.ly_ref, bf16[64,96,128]{2,1,0:T(8,128)(2,1)} %copy-done.2, bf16[64,96,128]{2,1,0:T(8,128)(2,1)} %collective-permute-done.16.refs_1_, ...), custom_call_target="tpu_custom_call" | custom-call | flops 1000 | bytes 1000 | tf_op jit(solution)/shard_map/update_block/pallas_call | solution.py:264
  182.7 1.2 collective-permute-done.23.refs_2_
  183.8 1.0 collective-permute-done.24.refs_6_
  184.9 1.1 collective-permute-start.27
  186.0 13.4 %update_block.4.refs_10_ = bf16[128,256,128]{2,1,0:T(8,128)(2,1)} custom-call(bf16[128,128,384]{2,1,0:T(8,128)(2,1)} %arrange_left.3.lx_ref.ly_ref, bf16[128,128,384]{2,1,0:T(8,128)(2,1)} %arrange_left.3.lx_ref.ly_ref, bf16[64,96,128]{2,1,0:T(8,128)(2,1)} %copy-done.2, ...), custom_call_target="tpu_custom_call", output_to_operand_aliasing={{}: (12, {})} | custom-call | flops 1000 | bytes 1000 | tf_op jit(solution)/shard_map/update_block/pallas_call | solution.py:264
  199.4 7.1 %collective-permute-done.27.refs_3_ = bf16[64,96,128]{2,1,0:T(8,128)(2,1)S(1)} collective-permute-done((bf16[64,96,128]{2,1,0:T(8,128)(2,1)S(1)}, bf16[64,96,128]{2,1,0:T(8,128)(2,1)S(1)}, u32[]{:S(2)}, u32[]{:S(2)}) %collective-permute-start.27) | collective-permute-done | bytes 1572896 | tf_op jit(solution)/shard_map/ppermute | solution.py:285
  206.5 1.1 collective-permute-done.28.refs_7_
  207.7 1.2 copy-done.11
  208.8 21.9 %update_block.5 = bf16[128,256,128]{2,1,0:T(8,128)(2,1)} custom-call(bf16[128,128,384]{2,1,0:T(8,128)(2,1)} %arrange_left.3.lx_ref.ly_ref, bf16[128,128,384]{2,1,0:T(8,128)(2,1)} %arrange_left.3.lx_ref.ly_ref, bf16[64,96,128]{2,1,0:T(8,128)(2,1)} %constant_dynamic-update-slice_fusion.8.refs_0_, ...), custom_call_target="tpu_custom_call", output_to_operand_aliasing={{}: (12, {})} | custom-call | flops 1000 | bytes 1000 | tf_op jit(solution)/shard_map/update_block/pallas_call | solution.py:264
  (63 shorter events, 3.5 us)
Async XLA Ops:
  1.2 14.6 %copy-start.5 = (bf16[12,128,128]{2,1,0:T(8,128)(2,1)}, bf16[12,128,128]{2,1,0:T(8,128)(2,1)S(1)}, u32[]{:S(2)}) copy-start(bf16[12,128,128]{2,1,0:T(8,128)(2,1)S(1)} %get-tuple-element.80.own_ref) | copy-start | bytes 1179652
  1.2 14.6 %copy-start.6 = (bf16[12,128,128]{2,1,0:T(8,128)(2,1)}, bf16[12,128,128]{2,1,0:T(8,128)(2,1)S(1)}, u32[]{:S(2)}) copy-start(bf16[12,128,128]{2,1,0:T(8,128)(2,1)S(1)} %get-tuple-element.79.own_ref) | copy-start | bytes 1179652
  1.2 14.6 %collective-permute-start = (bf16[12,128,128]{2,1,0:T(8,128)(2,1)S(1)}, bf16[12,128,128]{2,1,0:T(8,128)(2,1)S(1)}, u32[]{:S(2)}, u32[]{:S(2)}) collective-permute-start(bf16[12,128,128]{2,1,0:T(8,128)(2,1)S(1)} %get-tuple-element.80.own_ref), channel_id=1, source_target_pairs={{0,64},{1,65},{2,66},{3,67},{64,0},{65,1},{66,2},{67,3},{4,68},{5,... | collective-permute-start | bytes 1179656 | tf_op jit(solution)/shard_map/ppermute | solution.py:309
  5.2 18.4 %collective-permute-start.1 = (bf16[12,128,128]{2,1,0:T(8,128)(2,1)S(1)}, bf16[12,128,128]{2,1,0:T(8,128)(2,1)S(1)}, u32[]{:S(2)}, u32[]{:S(2)}) collective-permute-start(bf16[12,128,128]{2,1,0:T(8,128)(2,1)S(1)} %get-tuple-element.79.own_ref), channel_id=1, source_target_pairs={{0,64},{1,65},{2,66},{3,67},{64,0},{65,1},{66,2},{67,3},{4,68},{5,... | collective-permute-start | bytes 1179656 | tf_op jit(solution)/shard_map/ppermute | solution.py:309
  15.8 15.0 %copy-start.15 = (bf16[12,128,128]{2,1,0:T(8,128)(2,1)}, bf16[12,128,128]{2,1,0:T(8,128)(2,1)S(1)}, u32[]{:S(2)}) copy-start(bf16[12,128,128]{2,1,0:T(8,128)(2,1)S(1)} %collective-permute-done.other_ref) | copy-start | bytes 1179652
  15.8 90.4 %collective-permute-start.8 = (bf16[128,96,128]{2,1,0:T(8,128)(2,1)}, bf16[128,96,128]{2,1,0:T(8,128)(2,1)}, u32[]{:S(2)}, u32[]{:S(2)}) collective-permute-start(bf16[128,96,128]{2,1,0:T(8,128)(2,1)} %project_left.1.a_ref), channel_id=1, source_target_pairs={{0,2},{1,3},{2,0},{3,1},{64,66},{65,67},{66,64},{67,65},{4,6},{5,7... | collective-permute-start | bytes 9437192 | tf_op jit(solution)/shard_map/ppermute | solution.py:318
  23.6 0.8 copy-start.16
  27.8 19.8 %copy-start.14 = (bf16[64,24,128]{2,1,0:T(8,128)(2,1)S(1)}, bf16[64,24,128]{2,1,0:T(8,128)(2,1)}, u32[]{:S(2)}) copy-start(bf16[64,24,128]{2,1,0:T(8,128)(2,1)} %get-tuple-element.53) | copy-start | bytes 1179652
  27.8 9.5 %collective-permute-start.9 = (bf16[64,24,128]{2,1,0:T(8,128)(2,1)}, bf16[64,24,128]{2,1,0:T(8,128)(2,1)S(1)}, u32[]{:S(2)}, u32[]{:S(2)}) collective-permute-start(bf16[64,24,128]{2,1,0:T(8,128)(2,1)} %get-tuple-element.43), channel_id=1, source_target_pairs={{0,16},{1,49},{2,18},{3,51},{64,80},{65,113},{66,82},{67,115},{4,2... | collective-permute-start | bytes 1179656 | tf_op jit(solution)/shard_map/ppermute | solution.py:285
  29.3 9.2 %collective-permute-start.10 = (bf16[64,24,128]{2,1,0:T(8,128)(2,1)}, bf16[64,24,128]{2,1,0:T(8,128)(2,1)S(1)}, u32[]{:S(2)}, u32[]{:S(2)}) collective-permute-start(bf16[64,24,128]{2,1,0:T(8,128)(2,1)} %get-tuple-element.53), channel_id=1, source_target_pairs={{0,4},{1,13},{2,6},{3,15},{64,68},{65,77},{66,70},{67,79},{4,8},{5... | collective-permute-start | bytes 1179656 | tf_op jit(solution)/shard_map/ppermute | solution.py:285
  34.2 9.2 %collective-permute-start.2 = (bf16[64,24,128]{2,1,0:T(8,128)(2,1)}, bf16[64,24,128]{2,1,0:T(8,128)(2,1)S(1)}, u32[]{:S(2)}, u32[]{:S(2)}) collective-permute-start(bf16[64,24,128]{2,1,0:T(8,128)(2,1)} %get-tuple-element.59), channel_id=1, source_target_pairs={{0,16},{1,49},{2,18},{3,51},{64,80},{65,113},{66,82},{67,115},{4,2... | collective-permute-start | bytes 1179656 | tf_op jit(solution)/shard_map/ppermute | solution.py:285
  35.7 9.2 %collective-permute-start.3 = (bf16[64,24,128]{2,1,0:T(8,128)(2,1)}, bf16[64,24,128]{2,1,0:T(8,128)(2,1)S(1)}, u32[]{:S(2)}, u32[]{:S(2)}) collective-permute-start(bf16[64,24,128]{2,1,0:T(8,128)(2,1)} %get-tuple-element.46), channel_id=1, source_target_pairs={{0,4},{1,13},{2,6},{3,15},{64,68},{65,77},{66,70},{67,79},{4,8},{5... | collective-permute-start | bytes 1179656 | tf_op jit(solution)/shard_map/ppermute | solution.py:285
  38.5 10.0 %collective-permute-start.11 = (bf16[64,24,128]{2,1,0:T(8,128)(2,1)S(1)}, bf16[64,24,128]{2,1,0:T(8,128)(2,1)S(1)}, u32[]{:S(2)}, u32[]{:S(2)}) collective-permute-start(bf16[64,24,128]{2,1,0:T(8,128)(2,1)S(1)} %collective-permute-done.9), channel_id=1, source_target_pairs={{0,16},{1,49},{2,18},{3,51},{64,80},{65,113},{66,82},{67,115},{4,2... | collective-permute-start | bytes 1179656 | tf_op jit(solution)/shard_map/ppermute | solution.py:285
  40.0 9.2 %collective-permute-start.12 = (bf16[64,24,128]{2,1,0:T(8,128)(2,1)S(1)}, bf16[64,24,128]{2,1,0:T(8,128)(2,1)S(1)}, u32[]{:S(2)}, u32[]{:S(2)}) collective-permute-start(bf16[64,24,128]{2,1,0:T(8,128)(2,1)S(1)} %collective-permute-done.10), channel_id=1, source_target_pairs={{0,4},{1,13},{2,6},{3,15},{64,68},{65,77},{66,70},{67,79},{4,8},{5... | collective-permute-start | bytes 1179656 | tf_op jit(solution)/shard_map/ppermute | solution.py:285
  44.9 9.0 %collective-permute-start.4 = (bf16[64,24,128]{2,1,0:T(8,128)(2,1)S(1)}, bf16[64,24,128]{2,1,0:T(8,128)(2,1)S(1)}, u32[]{:S(2)}, u32[]{:S(2)}) collective-permute-start(bf16[64,24,128]{2,1,0:T(8,128)(2,1)S(1)} %collective-permute-done.2), channel_id=1, source_target_pairs={{0,16},{1,49},{2,18},{3,51},{64,80},{65,113},{66,82},{67,115},{4,2... | collective-permute-start | bytes 1179656 | tf_op jit(solution)/shard_map/ppermute | solution.py:285
  46.1 9.0 %collective-permute-start.5 = (bf16[64,24,128]{2,1,0:T(8,128)(2,1)S(1)}, bf16[64,24,128]{2,1,0:T(8,128)(2,1)S(1)}, u32[]{:S(2)}, u32[]{:S(2)}) collective-permute-start(bf16[64,24,128]{2,1,0:T(8,128)(2,1)S(1)} %collective-permute-done.3), channel_id=1, source_target_pairs={{0,4},{1,13},{2,6},{3,15},{64,68},{65,77},{66,70},{67,79},{4,8},{5... | collective-permute-start | bytes 1179656 | tf_op jit(solution)/shard_map/ppermute | solution.py:285
  49.1 10.2 %collective-permute-start.14 = (bf16[64,24,128]{2,1,0:T(8,128)(2,1)S(1)}, bf16[64,24,128]{2,1,0:T(8,128)(2,1)S(1)}, u32[]{:S(2)}, u32[]{:S(2)}) collective-permute-start(bf16[64,24,128]{2,1,0:T(8,128)(2,1)S(1)} %collective-permute-done.12), channel_id=1, source_target_pairs={{0,4},{1,13},{2,6},{3,15},{64,68},{65,77},{66,70},{67,79},{4,8},{5... | collective-permute-start | bytes 1179656 | tf_op jit(solution)/shard_map/ppermute | solution.py:285
  50.6 9.6 %collective-permute-start.13 = (bf16[64,24,128]{2,1,0:T(8,128)(2,1)S(1)}, bf16[64,24,128]{2,1,0:T(8,128)(2,1)S(1)}, u32[]{:S(2)}, u32[]{:S(2)}) collective-permute-start(bf16[64,24,128]{2,1,0:T(8,128)(2,1)S(1)} %collective-permute-done.11), channel_id=1, source_target_pairs={{0,16},{1,49},{2,18},{3,51},{64,80},{65,113},{66,82},{67,115},{4,2... | collective-permute-start | bytes 1179656 | tf_op jit(solution)/shard_map/ppermute | solution.py:285
  51.6 12.5 %copy-start = (bf16[128,96,128]{2,1,0:T(8,128)(2,1)S(1)}, bf16[128,96,128]{2,1,0:T(8,128)(2,1)}, u32[]{:S(2)}) copy-start(bf16[128,96,128]{2,1,0:T(8,128)(2,1)} %project_left.1.a_ref) | copy-start | bytes 9437188
  51.7 12.5 %copy-start.13 = (bf16[64,24,128]{2,1,0:T(8,128)(2,1)S(1)}, bf16[64,24,128]{2,1,0:T(8,128)(2,1)}, u32[]{:S(2)}) copy-start(bf16[64,24,128]{2,1,0:T(8,128)(2,1)} %get-tuple-element.59) | copy-start | bytes 1179652
  55.1 9.0 %collective-permute-start.6 = (bf16[64,24,128]{2,1,0:T(8,128)(2,1)S(1)}, bf16[64,24,128]{2,1,0:T(8,128)(2,1)S(1)}, u32[]{:S(2)}, u32[]{:S(2)}) collective-permute-start(bf16[64,24,128]{2,1,0:T(8,128)(2,1)S(1)} %collective-permute-done.4), channel_id=1, source_target_pairs={{0,16},{1,49},{2,18},{3,51},{64,80},{65,113},{66,82},{67,115},{4,2... | collective-permute-start | bytes 1179656 | tf_op jit(solution)/shard_map/ppermute | solution.py:285
  56.5 8.5 %copy-start.12 = (bf16[64,24,128]{2,1,0:T(8,128)(2,1)S(1)}, bf16[64,24,128]{2,1,0:T(8,128)(2,1)}, u32[]{:S(2)}) copy-start(bf16[64,24,128]{2,1,0:T(8,128)(2,1)} %get-tuple-element.46) | copy-start | bytes 1179652
  60.3 8.0 %copy-start.2 = (bf16[64,96,128]{2,1,0:T(8,128)(2,1)}, bf16[64,96,128]{2,1,0:T(8,128)(2,1)S(1)}, u32[]{:S(2)}) copy-start(bf16[64,96,128]{2,1,0:T(8,128)(2,1)S(1)} %constant_dynamic-update-slice_fusion.refs_0_) | copy-start | bytes 4718596
  60.3 36.4 %collective-permute-start.16 = (bf16[64,96,128]{2,1,0:T(8,128)(2,1)S(1)}, bf16[64,96,128]{2,1,0:T(8,128)(2,1)}, u32[]{:S(2)}, u32[]{:S(2)}) collective-permute-start(bf16[64,96,128]{2,1,0:T(8,128)(2,1)S(1)} %constant_dynamic-update-slice_fusion.refs_0_), channel_id=1, source_target_pairs={{0,4},{1,13},{2,6},{3,15},{64,68},{65,77},{66,70},{67,79},{4,8},{5... | collective-permute-start | bytes 4718600 | tf_op jit(solution)/shard_map/ppermute | solution.py:285
  60.8 35.9 %collective-permute-start.17 = (bf16[64,96,128]{2,1,0:T(8,128)(2,1)}, bf16[64,96,128]{2,1,0:T(8,128)(2,1)}, u32[]{:S(2)}, u32[]{:S(2)}) collective-permute-start(bf16[64,96,128]{2,1,0:T(8,128)(2,1)} %constant_dynamic-update-slice_fusion.4.refs_4_), channel_id=1, source_target_pairs={{0,16},{1,49},{2,18},{3,51},{64,80},{65,113},{66,82},{67,115},{4,2... | collective-permute-start | bytes 4718600 | tf_op jit(solution)/shard_map/ppermute | solution.py:285
  64.1 43.4 %collective-permute-start.7 = (bf16[128,96,128]{2,1,0:T(8,128)(2,1)S(1)}, bf16[128,96,128]{2,1,0:T(8,128)(2,1)S(1)}, u32[]{:S(2)}, u32[]{:S(2)}) collective-permute-start(bf16[128,96,128]{2,1,0:T(8,128)(2,1)S(1)} %copy-done), channel_id=1, source_target_pairs={{0,1},{1,0},{2,3},{3,2},{64,65},{65,64},{66,67},{67,66},{4,5},{5,4... | collective-permute-start | bytes 9437192 | tf_op jit(solution)/shard_map/ppermute | solution.py:328
  66.7 19.5 %collective-permute-start.15 = (bf16[64,24,128]{2,1,0:T(8,128)(2,1)S(1)}, bf16[64,24,128]{2,1,0:T(8,128)(2,1)S(1)}, u32[]{:S(2)}, u32[]{:S(2)}) collective-permute-start(bf16[64,24,128]{2,1,0:T(8,128)(2,1)S(1)} %collective-permute-done.5), channel_id=1, source_target_pairs={{0,4},{1,13},{2,6},{3,15},{64,68},{65,77},{66,70},{67,79},{4,8},{5... | collective-permute-start | bytes 1179656 | tf_op jit(solution)/shard_map/ppermute | solution.py:285
  106.3 6.0 %collective-permute-start.18 = (bf16[128,96,128]{2,1,0:T(8,128)(2,1)}, bf16[128,96,128]{2,1,0:T(8,128)(2,1)}, u32[]{:S(2)}, u32[]{:S(2)}) collective-permute-start(bf16[128,96,128]{2,1,0:T(8,128)(2,1)} %collective-permute-done.8.c_ref), channel_id=1, source_target_pairs={{0,1},{1,0},{2,3},{3,2},{64,65},{65,64},{66,67},{67,66},{4,5},{5,4... | collective-permute-start | bytes 9437192 | tf_op jit(solution)/shard_map/ppermute | solution.py:331
  106.3 22.0 %collective-permute-start.19 = (bf16[64,96,128]{2,1,0:T(8,128)(2,1)}, bf16[64,96,128]{2,1,0:T(8,128)(2,1)}, u32[]{:S(2)}, u32[]{:S(2)}) collective-permute-start(bf16[64,96,128]{2,1,0:T(8,128)(2,1)} %collective-permute-done.16.refs_1_), channel_id=1, source_target_pairs={{0,4},{1,13},{2,6},{3,15},{64,68},{65,77},{66,70},{67,79},{4,8},{5... | collective-permute-start | bytes 4718600 | tf_op jit(solution)/shard_map/ppermute | solution.py:285
  106.4 22.0 %collective-permute-start.22 = (bf16[64,96,128]{2,1,0:T(8,128)(2,1)}, bf16[64,96,128]{2,1,0:T(8,128)(2,1)}, u32[]{:S(2)}, u32[]{:S(2)}) collective-permute-start(bf16[64,96,128]{2,1,0:T(8,128)(2,1)} %collective-permute-done.17.refs_5_), channel_id=1, source_target_pairs={{0,16},{1,49},{2,18},{3,51},{64,80},{65,113},{66,82},{67,115},{4,2... | collective-permute-start | bytes 4718600 | tf_op jit(solution)/shard_map/ppermute | solution.py:285
  106.9 38.2 %collective-permute-start.20 = (bf16[64,96,128]{2,1,0:T(8,128)(2,1)}, bf16[64,96,128]{2,1,0:T(8,128)(2,1)}, u32[]{:S(2)}, u32[]{:S(2)}) collective-permute-start(bf16[64,96,128]{2,1,0:T(8,128)(2,1)} %constant_dynamic-update-slice_fusion.8.refs_0_), channel_id=1, source_target_pairs={{0,4},{1,13},{2,6},{3,15},{64,68},{65,77},{66,70},{67,79},{4,8},{5... | collective-permute-start | bytes 4718600 | tf_op jit(solution)/shard_map/ppermute | solution.py:285
  107.5 1.7 copy-start.1
  109.2 35.9 %collective-permute-start.21 = (bf16[64,96,128]{2,1,0:T(8,128)(2,1)}, bf16[64,96,128]{2,1,0:T(8,128)(2,1)S(1)}, u32[]{:S(2)}, u32[]{:S(2)}) collective-permute-start(bf16[64,96,128]{2,1,0:T(8,128)(2,1)} %constant_dynamic-update-slice_fusion.12.refs_4_), channel_id=1, source_target_pairs={{0,16},{1,49},{2,18},{3,51},{64,80},{65,113},{66,82},{67,115},{4,2... | collective-permute-start | bytes 4718600 | tf_op jit(solution)/shard_map/ppermute | solution.py:285
  145.2 12.6 %copy-start.7 = (bf16[64,96,128]{2,1,0:T(8,128)(2,1)}, bf16[64,96,128]{2,1,0:T(8,128)(2,1)S(1)}, u32[]{:S(2)}) copy-start(bf16[64,96,128]{2,1,0:T(8,128)(2,1)S(1)} %collective-permute-done.21.refs_5_) | copy-start | bytes 4718596
  145.2 21.8 %collective-permute-start.25 = (bf16[64,96,128]{2,1,0:T(8,128)(2,1)}, bf16[64,96,128]{2,1,0:T(8,128)(2,1)S(1)}, u32[]{:S(2)}, u32[]{:S(2)}) collective-permute-start(bf16[64,96,128]{2,1,0:T(8,128)(2,1)} %collective-permute-done.19.refs_2_), channel_id=1, source_target_pairs={{0,4},{1,13},{2,6},{3,15},{64,68},{65,77},{66,70},{67,79},{4,8},{5... | collective-permute-start | bytes 4718600 | tf_op jit(solution)/shard_map/ppermute | solution.py:285
  146.2 21.8 %collective-permute-start.26 = (bf16[64,96,128]{2,1,0:T(8,128)(2,1)}, bf16[64,96,128]{2,1,0:T(8,128)(2,1)S(1)}, u32[]{:S(2)}, u32[]{:S(2)}) collective-permute-start(bf16[64,96,128]{2,1,0:T(8,128)(2,1)} %collective-permute-done.22.refs_6_), channel_id=1, source_target_pairs={{0,16},{1,49},{2,18},{3,51},{64,80},{65,113},{66,82},{67,115},{4,2... | collective-permute-start | bytes 4718600 | tf_op jit(solution)/shard_map/ppermute | solution.py:285
  146.2 37.7 %collective-permute-start.23 = (bf16[64,96,128]{2,1,0:T(8,128)(2,1)}, bf16[64,96,128]{2,1,0:T(8,128)(2,1)S(1)}, u32[]{:S(2)}, u32[]{:S(2)}) collective-permute-start(bf16[64,96,128]{2,1,0:T(8,128)(2,1)} %collective-permute-done.20.refs_1_), channel_id=1, source_target_pairs={{0,4},{1,13},{2,6},{3,15},{64,68},{65,77},{66,70},{67,79},{4,8},{5... | collective-permute-start | bytes 4718600 | tf_op jit(solution)/shard_map/ppermute | solution.py:285
  147.3 37.6 %collective-permute-start.24 = (bf16[64,96,128]{2,1,0:T(8,128)(2,1)S(1)}, bf16[64,96,128]{2,1,0:T(8,128)(2,1)S(1)}, u32[]{:S(2)}, u32[]{:S(2)}) collective-permute-start(bf16[64,96,128]{2,1,0:T(8,128)(2,1)S(1)} %collective-permute-done.21.refs_5_), channel_id=1, source_target_pairs={{0,16},{1,49},{2,18},{3,51},{64,80},{65,113},{66,82},{67,115},{4,2... | collective-permute-start | bytes 4718600 | tf_op jit(solution)/shard_map/ppermute | solution.py:285
  167.0 1.2 copy-start.3
  168.2 1.1 copy-start.4
  183.8 15.5 %copy-start.8 = (bf16[64,96,128]{2,1,0:T(8,128)(2,1)}, bf16[64,96,128]{2,1,0:T(8,128)(2,1)S(1)}, u32[]{:S(2)}) copy-start(bf16[64,96,128]{2,1,0:T(8,128)(2,1)S(1)} %collective-permute-done.23.refs_2_) | copy-start | bytes 4718596
  184.9 14.5 %copy-start.9 = (bf16[64,96,128]{2,1,0:T(8,128)(2,1)}, bf16[64,96,128]{2,1,0:T(8,128)(2,1)S(1)}, u32[]{:S(2)}) copy-start(bf16[64,96,128]{2,1,0:T(8,128)(2,1)S(1)} %collective-permute-done.24.refs_6_) | copy-start | bytes 4718596
  184.9 21.6 %collective-permute-start.27 = (bf16[64,96,128]{2,1,0:T(8,128)(2,1)S(1)}, bf16[64,96,128]{2,1,0:T(8,128)(2,1)S(1)}, u32[]{:S(2)}, u32[]{:S(2)}) collective-permute-start(bf16[64,96,128]{2,1,0:T(8,128)(2,1)S(1)} %collective-permute-done.23.refs_2_), channel_id=1, source_target_pairs={{0,4},{1,13},{2,6},{3,15},{64,68},{65,77},{66,70},{67,79},{4,8},{5... | collective-permute-start | bytes 4718600 | tf_op jit(solution)/shard_map/ppermute | solution.py:285
  186.0 21.6 %collective-permute-start.28 = (bf16[64,96,128]{2,1,0:T(8,128)(2,1)S(1)}, bf16[64,96,128]{2,1,0:T(8,128)(2,1)S(1)}, u32[]{:S(2)}, u32[]{:S(2)}) collective-permute-start(bf16[64,96,128]{2,1,0:T(8,128)(2,1)S(1)} %collective-permute-done.24.refs_6_), channel_id=1, source_target_pairs={{0,16},{1,49},{2,18},{3,51},{64,80},{65,113},{66,82},{67,115},{4,2... | collective-permute-start | bytes 4718600 | tf_op jit(solution)/shard_map/ppermute | solution.py:285
  206.5 1.2 copy-start.10
  207.7 1.2 copy-start.11

commit v2 on v1

--- a/solution.py
+++ b/solution.py
@@ -10,7 +10,7 @@
 epsilon = 1e-05
 AXES = ("row", "col")
 NX, NY, NZ = 4, 4, 4
-VMEM_LIMIT = 56 * 1024 * 1024
+MIB = 1024 * 1024
 CHANNELS = 128
 SHORT = pl.CostEstimate(flops=1000, bytes_accessed=1000, transcendentals=0)
 
@@ -91,8 +91,12 @@
             pltpu.VMEM((n_i * block, CHANNELS), jnp.float32),
             pltpu.VMEM((CHANNELS * block, n_i), jnp.float32),
         ],
-        compiler_params=pltpu.CompilerParams(vmem_limit_bytes=VMEM_LIMIT),
-        cost_estimate=SHORT,
+        compiler_params=pltpu.CompilerParams(vmem_limit_bytes=16 * MIB),
+        cost_estimate=pl.CostEstimate(
+            flops=2 * n_i * n_k * CHANNELS * 256,
+            bytes_accessed=8 * n_i * n_k * CHANNELS,
+            transcendentals=2 * n_i * n_k * CHANNELS,
+        ),
         name="project_left",
     )(pair, proj, gate)
 
@@ -117,7 +121,7 @@
         right_kernel,
         out_shape=(half, half),
         scratch_shapes=[pltpu.VMEM((CHANNELS * 2 * n_k, n_j), jnp.float32)],
-        compiler_params=pltpu.CompilerParams(vmem_limit_bytes=VMEM_LIMIT),
+        compiler_params=pltpu.CompilerParams(vmem_limit_bytes=16 * MIB),
         cost_estimate=SHORT,
         name="project_right",
     )(own, other, proj, gate)
@@ -142,7 +146,7 @@
         ],
         out_specs=pl.BlockSpec((block, n_j, CHANNELS), lambda s: (s, 0, 0)),
         out_shape=jax.ShapeDtypeStruct((n_i, n_j, CHANNELS), jnp.bfloat16),
-        compiler_params=pltpu.CompilerParams(vmem_limit_bytes=VMEM_LIMIT),
+        compiler_params=pltpu.CompilerParams(vmem_limit_bytes=16 * MIB),
         cost_estimate=SHORT,
         name="gate_values",
     )(pair, weights)
@@ -158,15 +162,17 @@
         ).astype(jnp.bfloat16)
 
 
-def arrange_left(parts, orders, first, whole=None):
-    n_c, n_k, n_i = parts[0].shape
+def arrange_left(near, near_core, far, far_core, orders, first, whole=None):
+    n_c, n_k, n_i = near.shape
     block = 8
     depth = 4 * n_k
     steps = n_c // 2 // block
-    in_specs = [pl.BlockSpec((block, n_k, n_i), lambda s: (s + first * steps, 0, 0))] * 4 + [
-        pl.BlockSpec((1, depth, depth), lambda s: (first, 0, 0))
-    ]
-    operands = [*parts, orders]
+    in_specs = (
+        [pl.BlockSpec((block, n_k, n_i), lambda s: (s + first * steps, 0, 0))] * 2
+        + [pl.BlockSpec((block, n_k, n_i), lambda s: (s, 0, 0))] * 2
+        + [pl.BlockSpec((1, depth, depth), lambda s: (first, 0, 0))]
+    )
+    operands = [near, near_core, far, far_core, orders]
     aliases = {}
     if whole is not None:
         in_specs.append(pl.BlockSpec(memory_space=pl.ANY))
@@ -179,7 +185,7 @@
         out_specs=pl.BlockSpec((block, n_i, depth), lambda s: (s + first * steps, 0, 0)),
         out_shape=jax.ShapeDtypeStruct((n_c, n_i, depth), jnp.bfloat16),
         input_output_aliases=aliases,
-        compiler_params=pltpu.CompilerParams(vmem_limit_bytes=VMEM_LIMIT),
+        compiler_params=pltpu.CompilerParams(vmem_limit_bytes=12 * MIB),
         cost_estimate=SHORT,
         name="arrange_left",
     )(*operands)
@@ -269,7 +275,7 @@
         out_shape=jax.ShapeDtypeStruct((n_i, n_blocks * n_j, CHANNELS), jnp.bfloat16),
         scratch_shapes=[pltpu.VMEM((rows * CHANNELS, n_j), jnp.float32)],
         input_output_aliases=aliases,
-        compiler_params=pltpu.CompilerParams(vmem_limit_bytes=VMEM_LIMIT),
+        compiler_params=pltpu.CompilerParams(vmem_limit_bytes=30 * MIB),
         cost_estimate=SHORT,
         name="update_block",
     )(*operands)
@@ -308,33 +314,37 @@
     blocks = [right[:, b * n_j : (b + 1) * n_j] for b in range(n_blocks)]
     others = [lax.ppermute(block, AXES, SWAP_Z_HI) for block in blocks]
     left_local = project_left(pair_left, left_proj, left_gate)
+    near = [left_local[: CHANNELS // 2], left_local[CHANNELS // 2 :]]
     halves_0 = project_right(blocks[0], after(others[0], left_local), right_proj, right_gate)
     f0 = [[half] for half in halves_0]
     step_on(f0, first_rings)
-    halves_1 = project_right(blocks[1], after(others[1], halves_0[0]), right_proj, right_gate)
+    near_core = lax.ppermute(after(left_local, *others), AXES, SWAP_CORE)
+    far_0 = lax.ppermute(after(near[0], *others, *halves_0), AXES, SWAP_Z_LO)
+    halves_1 = project_right(blocks[1], after(others[1], *halves_0), right_proj, right_gate)
     f1 = [[half] for half in halves_1]
     step_on(f1, first_rings)
-    left_sent = after(left_local, others[1])
-    left_far = lax.ppermute(left_sent, AXES, SWAP_Z_LO)
-    step_on(f0, first_rings)
-    step_on(f1, first_rings)
-    step_on(f0, first_rings)
-    step_on(f1, first_rings)
+    step_on(f0, first_rings, near_core, *halves_1)
+    step_on(f1, first_rings, f0[0][1])
+    step_on(f0, first_rings, f1[0][1], f1[1][1])
+    step_on(f1, first_rings, f0[0][2], f0[1][2])
+
     c0 = joined(f0)
-    step_on(c0, second_rings)
+    step_on(c0, second_rings, f1[0][2], f1[1][2])
     c1 = joined(f1)
     step_on(c1, second_rings)
-    gate_0 = gate_values(pair_gate, after(out_gate, c0[0][0], c0[1][0], c1[0][0], c1[1][0]), 0, n_j)
-    left_core = lax.ppermute(after(left_local, f1[0][-1]), AXES, SWAP_CORE)
-    step_on(c0, second_rings, gate_0)
-    gate_1 = gate_values(pair_gate, after(out_gate, gate_0, c0[0][1], c0[1][1]), 1, n_j)
-    left_far_core = lax.ppermute(after(left_far, gate_1), AXES, SWAP_CORE)
-    parts = (left_local, left_core, left_far, left_far_core)
+    step_on(c0, second_rings, far_0)
+    far_1 = lax.ppermute(after(near[1], far_0), AXES, SWAP_Z_LO)
+    gate_0 = gate_values(pair_gate, after(out_gate, c1[0][1], c1[1][1]), 0, n_j)
+    far_core_0 = lax.ppermute(after(far_0, c1[0][1], c1[1][1]), AXES, SWAP_CORE)
+    gate_1 = gate_values(pair_gate, after(out_gate, gate_0), 1, n_j)
+    step_on(c0, second_rings, gate_1)
+    step_on(c1, second_rings, c0[0][2], c0[1][2], gate_1)
+    far_core_1 = lax.ppermute(after(far_1, c0[0][2], c0[1][2]), AXES, SWAP_CORE)
     orders = left_orders()
-    left = arrange_left(parts, orders, 0)
-    step_on(c0, second_rings, left)
-    step_on(c1, second_rings, left, c0[0][2], c0[1][2])
-    left = arrange_left(parts, after(orders, c0[0][2]), 1, left)
+    left = arrange_left(
+        left_local, near_core, far_0, far_core_0, after(orders, c0[0][2], c0[1][2]), 0
+    )
+    left = arrange_left(left_local, near_core, far_1, far_core_1, orders, 1, left)
     whole = update_block(left, *c0, gate_0, out_proj, 0, n_blocks, 0, 2)
     step_on(c1, second_rings, whole)
     whole = update_block(

time: 233 us -> 207 us (0.89)
  Pallas kernels: 106 us -> 79.6 us
  waiting for transfers between devices: 81.4 us -> 72.3 us
  local copies, waits for them, and re-layouts: 17.9 us -> 23.9 us
  starting transfers between devices: 24 us -> 29.5 us
    ppermute x24, waiting for transfers between devices: 74.3 us -> 65.7 us  [step_on(): held.append(lax.ppermute(piece, AXES, ring))]
    unnamed x46 -> x76, local copies, waits for them, and re-layouts: 14.1 us -> 22.3 us
    pallas_call x3, Pallas kernels: 48.6 us -> 40.6 us  [update_block(): pl.pallas_call(functools.partial(update_kernel, n_sum), grid=(n_sum + n_o...]
    pallas_call x2, Pallas kernels: 21 us -> 14.1 us  [arrange_left(): pl.pallas_call(arrange_kernel, grid=(steps,), in_specs=in_specs, out_spec...]
    pallas_call x2, Pallas kernels: 19.2 us -> 13.1 us  [gate_values(): pl.pallas_call(gate_kernel, grid=(n_i // block,), in_specs=[pl.BlockSpec(...]
    ppermute x24, starting transfers between devices: 18.3 us -> 22.3 us  [step_on(): held.append(lax.ppermute(piece, AXES, ring))]
    pallas_call x2, Pallas kernels: 6.8 us -> 2.83 us  [project_right(): pl.pallas_call(right_kernel, out_shape=(half, half), scratch_shapes=[pltp...]
    concatenate x4, local copies, waits for them, and re-layouts: 2.68 us -> 0.3 us  [joined(): return [[jnp.concatenate(held, axis=1)] for held in pieces]]
  transfers between devices with their start and end apart: 29 -> 31, of which waited for: 20 -> 16; matrix products, arithmetic and copies ran while one was open for 6% -> 1% of each run, Pallas kernels for 36% -> 30%
where the time goes in v2:
time: 207 us; the launch traced here: 206 us
  Pallas kernels  79.6 us (38%)
  waiting for transfers between devices  72.3 us (35%)
  starting transfers between devices  29.5 us (14%)
  local copies, waits for them, and re-layouts  23.9 us (12%)
    ppermute x24, waiting for transfers between devices, step_on(): held.append(lax.ppermute(piece, AXES, ring))  65.7 us
    pallas_call x3, Pallas kernels, update_block(): pl.pallas_call(functools.partial(update_kernel, n_sum), grid=(n_sum + n_o...  40.6 us
    ppermute x24, starting transfers between devices, step_on(): held.append(lax.ppermute(piece, AXES, ring))  22.3 us
    unnamed x76, local copies, waits for them, and re-layouts  22.3 us
    pallas_call x2, Pallas kernels, arrange_left(): pl.pallas_call(arrange_kernel, grid=(steps,), in_specs=in_specs, out_spec...  14.1 us
    pallas_call x2, Pallas kernels, gate_values(): pl.pallas_call(gate_kernel, grid=(n_i // block,), in_specs=[pl.BlockSpec(...  13.1 us
    pallas_call x1, Pallas kernels, project_left(): pl.pallas_call(left_kernel, grid=(n_k // block,), in_specs=[pl.BlockSpec(...  8.93 us
    ppermute x2, waiting for transfers between devices, shards(): others = [lax.ppermute(block, AXES, SWAP_Z_HI) for block in blocks]  6.58 us
  transfers between devices with their start and end apart: 31, of which 16 were waited for; matrix products, arithmetic and copies ran while one was open for 1% of the time, Pallas kernels for 30%

profile of v2, /device:TPU:0, one launch (start us, length us, event | category | flops | bytes accessed | tf_op | source)
XLA Modules:
  0.0 206.4 jit_solution(16898921950138058395)
XLA Ops:
  0.0 1.2 fusion.45
  1.2 4.0 %collective-permute-start = (bf16[12,128,128]{2,1,0:T(8,128)(2,1)S(1)}, bf16[12,128,128]{2,1,0:T(8,128)(2,1)S(1)}, u32[]{:S(2)}, u32[]{:S(2)}) collective-permute-start(bf16[12,128,128]{2,1,0:T(8,128)(2,1)S(1)} %get-tuple-element.86.own_ref), channel_id=1, source_target_pairs={{0,64},{1,65},{2,66},{3,67},{64,0},{65,1},{66,2},{67,3},{4,68},{5,... | collective-permute-start | bytes 1179656 | tf_op jit(solution)/shard_map/ppermute | solution.py:315
  5.2 0.1 collective-permute-start.1
  5.3 1.9 copy-done.15
  7.2 8.9 %project_left.1.a_ref = bf16[128,96,128]{2,1,0:T(8,128)(2,1)S(1)} custom-call(bf16[128,96,128]{2,1,0:T(8,128)(2,1)S(1)} %copy-done.15, bf16[128,128]{1,0:T(8,128)(2,1)S(1)} %copy-done.28, bf16[128,128]{1,0:T(8,128)(2,1)S(1)} %copy-done.29), custom_call_target="tpu_custom_call" | custom-call | flops 805306368 | bytes 12582912 | tf_op jit(solution)/shard_map/project_left/pallas_call | solution.py:80
  16.2 6.6 %collective-permute-done.1.other_ref = bf16[12,128,128]{2,1,0:T(8,128)(2,1)S(1)} collective-permute-done((bf16[12,128,128]{2,1,0:T(8,128)(2,1)S(1)}, bf16[12,128,128]{2,1,0:T(8,128)(2,1)S(1)}, u32[]{:S(2)}, u32[]{:S(2)}) %collective-permute-start.1) | collective-permute-done | bytes 393248 | tf_op jit(solution)/shard_map/ppermute | solution.py:315
  22.8 0.2 fusion.44
  23.0 1.4 project_right.2
  24.4 1.6 collective-permute-start.5
  26.0 1.6 collective-permute-start.6
  27.6 1.4 project_right.3
  29.0 1.6 collective-permute-start.9
  30.6 1.6 collective-permute-start.10
  32.3 1.2 collective-permute-done.5
  33.5 1.3 collective-permute-start.3
  34.8 3.3 %collective-permute-done.9 = bf16[64,24,128]{2,1,0:T(8,128)(2,1)S(1)} collective-permute-done((bf16[64,24,128]{2,1,0:T(8,128)(2,1)S(1)}, bf16[64,24,128]{2,1,0:T(8,128)(2,1)S(1)}, u32[]{:S(2)}, u32[]{:S(2)}) %collective-permute-start.9) | collective-permute-done | bytes 393248 | tf_op jit(solution)/shard_map/ppermute | solution.py:291
  38.0 1.5 collective-permute-done.10
  39.5 1.2 collective-permute-start.13
  40.7 0.4 collective-permute-start.14
  41.1 1.6 copy-done.5
  42.8 1.1 collective-permute-start.7
  43.9 1.6 collective-permute-start.8
  45.8 6.9 %collective-permute-done.7 = bf16[64,24,128]{2,1,0:T(8,128)(2,1)S(1)} collective-permute-done((bf16[64,24,128]{2,1,0:T(8,128)(2,1)S(1)}, bf16[64,24,128]{2,1,0:T(8,128)(2,1)S(1)}, u32[]{:S(2)}, u32[]{:S(2)}) %collective-permute-start.7) | collective-permute-done | bytes 393248 | tf_op jit(solution)/shard_map/ppermute | solution.py:291
  52.7 1.2 collective-permute-done.8
  53.9 1.1 collective-permute-start.11
  55.3 0.9 collective-permute-start.20
  56.2 0.6 collective-permute-start.21
  57.0 5.9 %collective-permute-done.11 = bf16[64,24,128]{2,1,0:T(8,128)(2,1)S(1)} collective-permute-done((bf16[64,24,128]{2,1,0:T(8,128)(2,1)S(1)}, bf16[64,24,128]{2,1,0:T(8,128)(2,1)S(1)}, u32[]{:S(2)}, u32[]{:S(2)}) %collective-permute-start.11) | collective-permute-done | bytes 393248 | tf_op jit(solution)/shard_map/ppermute | solution.py:291
  63.0 1.2 collective-permute-done.12
  64.4 1.3 copy-done.9
  65.7 0.8 collective-permute-start.16
  66.5 0.6 collective-permute-done.20
  67.2 1.2 collective-permute-done.21
  68.5 0.3 collective-permute-start.22
  68.8 0.9 collective-permute-start.23
  69.7 1.3 collective-permute-start.4
  71.0 15.0 %collective-permute-done.15.refs_1_ = bf16[64,96,128]{2,1,0:T(8,128)(2,1)S(1)} collective-permute-done((bf16[64,96,128]{2,1,0:T(8,128)(2,1)S(1)}, bf16[64,96,128]{2,1,0:T(8,128)(2,1)S(1)}, u32[]{:S(2)}, u32[]{:S(2)}) %collective-permute-start.15) | collective-permute-done | bytes 1572896 | tf_op jit(solution)/shard_map/ppermute | solution.py:291
  86.0 1.3 collective-permute-done.16.refs_5_
  87.4 15.6 %collective-permute-done.22.refs_1_ = bf16[64,96,128]{2,1,0:T(8,128)(2,1)} collective-permute-done((bf16[64,96,128]{2,1,0:T(8,128)(2,1)S(1)}, bf16[64,96,128]{2,1,0:T(8,128)(2,1)}, u32[]{:S(2)}, u32[]{:S(2)}) %collective-permute-start.22) | collective-permute-done | bytes 1572896 | tf_op jit(solution)/shard_map/ppermute | solution.py:291
  103.0 1.3 collective-permute-done.23.refs_5_
  104.3 6.5 %gate_values.2.refs_8_ = bf16[128,128,128]{2,1,0:T(8,128)(2,1)S(1)} custom-call(bf16[128,256,128]{2,1,0:T(8,128)(2,1)S(1)} %bitcast.2, bf16[128,128]{1,0:T(8,128)(2,1)S(1)} %copy-done.25), custom_call_target="tpu_custom_call" | custom-call | flops 1000 | bytes 1000 | tf_op jit(solution)/shard_map/gate_values/pallas_call | solution.py:140
  111.0 2.0 copy-done.1
  113.0 6.5 %gate_values.3.refs_8_ = bf16[128,128,128]{2,1,0:T(8,128)(2,1)S(1)} custom-call(bf16[128,256,128]{2,1,0:T(8,128)(2,1)S(1)} %bitcast.2, bf16[128,128]{1,0:T(8,128)(2,1)S(1)} %copy-done.25), custom_call_target="tpu_custom_call" | custom-call | flops 1000 | bytes 1000 | tf_op jit(solution)/shard_map/gate_values/pallas_call | solution.py:140
  119.5 1.9 copy-done.3
  121.4 0.6 collective-permute-start.19
  122.0 0.9 collective-permute-start.25
  122.9 1.2 copy-done.22
  124.0 1.1 collective-permute-start.26
  125.2 0.3 fusion
  125.5 0.1 add_convert_fusion.order_ref
  125.6 1.9 copy-done.6
  127.5 1.4 copy-done.21
  128.9 1.4 copy-done.23
  130.3 5.8 %arrange_left.2.rest_0_ = bf16[128,128,384]{2,1,0:T(8,128)(2,1)S(1)} custom-call(bf16[128,96,128]{2,1,0:T(8,128)(2,1)S(1)} %project_left.1.a_ref, bf16[128,96,128]{2,1,0:T(8,128)(2,1)S(1)} %copy-done.6, bf16[64,96,128]{2,1,0:T(8,128)(2,1)S(1)} %copy-done.21, bf16[64,96,128]{2,1,0:T(8,128)(2,1)S(1)} %copy-done.23, ...), custom_call_target="tpu_custom_call" | custom-call | flops 1000 | bytes 1000 | tf_op jit(solution)/shard_map/arrange_left/pallas_call | solution.py:181
  136.2 8.3 %arrange_left.3.lx_ref.ly_ref = bf16[128,128,384]{2,1,0:T(8,128)(2,1)S(1)} custom-call(bf16[128,96,128]{2,1,0:T(8,128)(2,1)S(1)} %project_left.1.a_ref, bf16[128,96,128]{2,1,0:T(8,128)(2,1)S(1)} %copy-done.6, bf16[64,96,128]{2,1,0:T(8,128)(2,1)} %collective-permute-done.4.c_ref, ...), custom_call_target="tpu_custom_call", output_to_operand_aliasing={{}: (5, {})} | custom-call | flops 1000 | bytes 1000 | tf_op jit(solution)/shard_map/arrange_left/pallas_call | solution.py:181
  144.5 4.6 %copy-done = bf16[128,128,384]{2,1,0:T(8,128)(2,1)} copy-done((bf16[128,128,384]{2,1,0:T(8,128)(2,1)}, bf16[128,128,384]{2,1,0:T(8,128)(2,1)S(1)}, u32[]{:S(2)}) %copy-start) | copy-done | bytes 12582936
  149.1 2.2 %copy-done.2 = bf16[128,128,128]{2,1,0:T(8,128)(2,1)S(1)} copy-done((bf16[128,128,128]{2,1,0:T(8,128)(2,1)S(1)}, bf16[128,128,128]{2,1,0:T(8,128)(2,1)}, u32[]{:S(2)}) %copy-start.2) | copy-done | bytes 4194328
  151.3 11.1 %update_block.3.refs_10_ = bf16[128,256,128]{2,1,0:T(8,128)(2,1)} custom-call(bf16[128,128,384]{2,1,0:T(8,128)(2,1)} %copy-done, bf16[128,128,384]{2,1,0:T(8,128)(2,1)} %copy-done, bf16[64,96,128]{2,1,0:T(8,128)(2,1)S(1)} %copy-done.10, bf16[64,96,128]{2,1,0:T(8,128)(2,1)S(1)} %copy-done.12, bf16[64,96,128]{2,1,0:T(8,128)(2,1)} %collective-permute-done.17.refs_2_, ...), custom_call_target="tpu_custom_call" | custom-call | flops 1000 | bytes 1000 | tf_op jit(solution)/shard_map/update_block/pallas_call | solution.py:270
  162.4 3.8 %collective-permute-start.29 = (bf16[64,96,128]{2,1,0:T(8,128)(2,1)}, bf16[64,96,128]{2,1,0:T(8,128)(2,1)S(1)}, u32[]{:S(2)}, u32[]{:S(2)}) collective-permute-start(bf16[64,96,128]{2,1,0:T(8,128)(2,1)} %collective-permute-done.25.refs_2_), channel_id=1, source_target_pairs={{0,4},{1,13},{2,6},{3,15},{64,68},{65,77},{66,70},{67,79},{4,8},{5... | collective-permute-start | bytes 4718600 | tf_op jit(solution)/shard_map/ppermute | solution.py:291
  166.2 1.2 collective-permute-start.30
  167.4 11.2 %update_block.4.refs_10_ = bf16[128,256,128]{2,1,0:T(8,128)(2,1)} custom-call(bf16[128,128,384]{2,1,0:T(8,128)(2,1)} %copy-done, bf16[128,128,384]{2,1,0:T(8,128)(2,1)} %copy-done, bf16[64,96,128]{2,1,0:T(8,128)(2,1)S(1)} %copy-done.10, bf16[64,96,128]{2,1,0:T(8,128)(2,1)S(1)} %copy-done.12, ...), custom_call_target="tpu_custom_call", output_to_operand_aliasing={{}: (12, {})} | custom-call | flops 1000 | bytes 1000 | tf_op jit(solution)/shard_map/update_block/pallas_call | solution.py:270
  178.7 5.8 %collective-permute-done.29.refs_3_ = bf16[64,96,128]{2,1,0:T(8,128)(2,1)S(1)} collective-permute-done((bf16[64,96,128]{2,1,0:T(8,128)(2,1)}, bf16[64,96,128]{2,1,0:T(8,128)(2,1)S(1)}, u32[]{:S(2)}, u32[]{:S(2)}) %collective-permute-start.29) | collective-permute-done | bytes 1572896 | tf_op jit(solution)/shard_map/ppermute | solution.py:291
  184.4 3.6 %collective-permute-done.30.refs_7_ = bf16[64,96,128]{2,1,0:T(8,128)(2,1)S(1)} collective-permute-done((bf16[64,96,128]{2,1,0:T(8,128)(2,1)}, bf16[64,96,128]{2,1,0:T(8,128)(2,1)S(1)}, u32[]{:S(2)}, u32[]{:S(2)}) %collective-permute-start.30) | collective-permute-done | bytes 1572896 | tf_op jit(solution)/shard_map/ppermute | solution.py:291
  188.0 18.3 %update_block.5 = bf16[128,256,128]{2,1,0:T(8,128)(2,1)} custom-call(bf16[128,128,384]{2,1,0:T(8,128)(2,1)} %copy-done, bf16[128,128,384]{2,1,0:T(8,128)(2,1)} %copy-done, bf16[64,96,128]{2,1,0:T(8,128)(2,1)S(1)} %copy-done.17, bf16[64,96,128]{2,1,0:T(8,128)(2,1)} %collective-permute-done.22.refs_1_, ...), custom_call_target="tpu_custom_call", output_to_operand_aliasing={{}: (12, {})} | custom-call | flops 1000 | bytes 1000 | tf_op jit(solution)/shard_map/update_block/pallas_call | solution.py:270
  (99 shorter events, 1.4 us)
Async XLA Ops:
  0.0 5.3 %copy-start.28 = (bf16[128,128]{1,0:T(8,128)(2,1)S(1)}, bf16[128,128]{1,0:T(8,128)(2,1)}, u32[]{:S(2)}) copy-start(bf16[128,128]{1,0:T(8,128)(2,1)} %proj_ref.3) | copy-start | bytes 98308
  0.0 5.3 %copy-start.29 = (bf16[128,128]{1,0:T(8,128)(2,1)S(1)}, bf16[128,128]{1,0:T(8,128)(2,1)}, u32[]{:S(2)}) copy-start(bf16[128,128]{1,0:T(8,128)(2,1)} %gate_ref.3) | copy-start | bytes 98308
  1.2 15.0 %collective-permute-start = (bf16[12,128,128]{2,1,0:T(8,128)(2,1)S(1)}, bf16[12,128,128]{2,1,0:T(8,128)(2,1)S(1)}, u32[]{:S(2)}, u32[]{:S(2)}) collective-permute-start(bf16[12,128,128]{2,1,0:T(8,128)(2,1)S(1)} %get-tuple-element.86.own_ref), channel_id=1, source_target_pairs={{0,64},{1,65},{2,66},{3,67},{64,0},{65,1},{66,2},{67,3},{4,68},{5,... | collective-permute-start | bytes 1179656 | tf_op jit(solution)/shard_map/ppermute | solution.py:315
  5.2 17.5 %collective-permute-start.1 = (bf16[12,128,128]{2,1,0:T(8,128)(2,1)S(1)}, bf16[12,128,128]{2,1,0:T(8,128)(2,1)S(1)}, u32[]{:S(2)}, u32[]{:S(2)}) collective-permute-start(bf16[12,128,128]{2,1,0:T(8,128)(2,1)S(1)} %get-tuple-element.85.own_ref), channel_id=1, source_target_pairs={{0,64},{1,65},{2,66},{3,67},{64,0},{65,1},{66,2},{67,3},{4,68},{5,... | collective-permute-start | bytes 1179656 | tf_op jit(solution)/shard_map/ppermute | solution.py:315
  5.3 1.9 copy-start.15
  16.2 6.8 %copy-start.26 = (bf16[128,128]{1,0:T(8,128)(2,1)S(1)}, bf16[128,128]{1,0:T(8,128)(2,1)}, u32[]{:S(2)}) copy-start(bf16[128,128]{1,0:T(8,128)(2,1)} %proj_ref.5) | copy-start | bytes 98308
  16.2 6.8 %copy-start.27 = (bf16[128,128]{1,0:T(8,128)(2,1)S(1)}, bf16[128,128]{1,0:T(8,128)(2,1)}, u32[]{:S(2)}) copy-start(bf16[128,128]{1,0:T(8,128)(2,1)} %gate_ref.5) | copy-start | bytes 98308
  22.8 18.3 %collective-permute-start.2 = (bf16[128,96,128]{2,1,0:T(8,128)(2,1)S(1)}, bf16[128,96,128]{2,1,0:T(8,128)(2,1)S(1)}, u32[]{:S(2)}, u32[]{:S(2)}) collective-permute-start(bf16[128,96,128]{2,1,0:T(8,128)(2,1)S(1)} %project_left.1.a_ref), channel_id=1, source_target_pairs={{0,1},{1,0},{2,3},{3,2},{64,65},{65,64},{66,67},{67,66},{4,5},{5,4... | collective-permute-start | bytes 9437192 | tf_op jit(solution)/shard_map/ppermute | solution.py:321
  22.8 81.5 %slice-start = ((s8[8388608]{0:T(1024)(128)(4,1)}), s8[4194304]{0:T(1024)(128)(4,1)S(1)}, s32[]{:S(2)}) async-start(s8[8388608]{0:T(1024)(128)(4,1)} %bitcast.1), calls=%async_computation | async-start | bytes 8388608
  24.4 9.1 %collective-permute-start.5 = (bf16[64,24,128]{2,1,0:T(8,128)(2,1)S(1)}, bf16[64,24,128]{2,1,0:T(8,128)(2,1)S(1)}, u32[]{:S(2)}, u32[]{:S(2)}) collective-permute-start(bf16[64,24,128]{2,1,0:T(8,128)(2,1)S(1)} %get-tuple-element.46), channel_id=1, source_target_pairs={{0,16},{1,49},{2,18},{3,51},{64,80},{65,113},{66,82},{67,115},{4,2... | collective-permute-start | bytes 1179656 | tf_op jit(solution)/shard_map/ppermute | solution.py:291
  26.0 15.1 %collective-permute-start.6 = (bf16[64,24,128]{2,1,0:T(8,128)(2,1)S(1)}, bf16[64,24,128]{2,1,0:T(8,128)(2,1)S(1)}, u32[]{:S(2)}, u32[]{:S(2)}) collective-permute-start(bf16[64,24,128]{2,1,0:T(8,128)(2,1)S(1)} %get-tuple-element.47), channel_id=1, source_target_pairs={{0,4},{1,13},{2,6},{3,15},{64,68},{65,77},{66,70},{67,79},{4,8},{5... | collective-permute-start | bytes 1179656 | tf_op jit(solution)/shard_map/ppermute | solution.py:291
  29.0 9.1 %collective-permute-start.9 = (bf16[64,24,128]{2,1,0:T(8,128)(2,1)S(1)}, bf16[64,24,128]{2,1,0:T(8,128)(2,1)S(1)}, u32[]{:S(2)}, u32[]{:S(2)}) collective-permute-start(bf16[64,24,128]{2,1,0:T(8,128)(2,1)S(1)} %get-tuple-element.53), channel_id=1, source_target_pairs={{0,16},{1,49},{2,18},{3,51},{64,80},{65,113},{66,82},{67,115},{4,2... | collective-permute-start | bytes 1179656 | tf_op jit(solution)/shard_map/ppermute | solution.py:291
  30.6 9.0 %collective-permute-start.10 = (bf16[64,24,128]{2,1,0:T(8,128)(2,1)S(1)}, bf16[64,24,128]{2,1,0:T(8,128)(2,1)S(1)}, u32[]{:S(2)}, u32[]{:S(2)}) collective-permute-start(bf16[64,24,128]{2,1,0:T(8,128)(2,1)S(1)} %get-tuple-element.54), channel_id=1, source_target_pairs={{0,4},{1,13},{2,6},{3,15},{64,68},{65,77},{66,70},{67,79},{4,8},{5... | collective-permute-start | bytes 1179656 | tf_op jit(solution)/shard_map/ppermute | solution.py:291
  32.2 72.1 %slice-start.1 = ((s8[8388608]{0:T(1024)(128)(4,1)}), s8[4194304]{0:T(1024)(128)(4,1)S(1)}, s32[]{:S(2)}) async-start(s8[8388608]{0:T(1024)(128)(4,1)} %bitcast.1), calls=%async_computation.1 | async-start | bytes 8388608
  33.5 36.2 %collective-permute-start.3 = (bf16[64,96,128]{2,1,0:T(8,128)(2,1)S(1)}, bf16[64,96,128]{2,1,0:T(8,128)(2,1)S(1)}, u32[]{:S(2)}, u32[]{:S(2)}) collective-permute-start(bf16[64,96,128]{2,1,0:T(8,128)(2,1)S(1)} %get-tuple-element.48), channel_id=1, source_target_pairs={{0,2},{1,3},{2,0},{3,1},{64,66},{65,67},{66,64},{67,65},{4,6},{5,7... | collective-permute-start | bytes 4718600 | tf_op jit(solution)/shard_map/ppermute | solution.py:322
  39.5 15.5 %collective-permute-start.13 = (bf16[64,24,128]{2,1,0:T(8,128)(2,1)S(1)}, bf16[64,24,128]{2,1,0:T(8,128)(2,1)S(1)}, u32[]{:S(2)}, u32[]{:S(2)}) collective-permute-start(bf16[64,24,128]{2,1,0:T(8,128)(2,1)S(1)} %collective-permute-done.9), channel_id=1, source_target_pairs={{0,16},{1,49},{2,18},{3,51},{64,80},{65,113},{66,82},{67,115},{4,2... | collective-permute-start | bytes 1179656 | tf_op jit(solution)/shard_map/ppermute | solution.py:291
  40.7 14.5 %collective-permute-start.14 = (bf16[64,24,128]{2,1,0:T(8,128)(2,1)S(1)}, bf16[64,24,128]{2,1,0:T(8,128)(2,1)S(1)}, u32[]{:S(2)}, u32[]{:S(2)}) collective-permute-start(bf16[64,24,128]{2,1,0:T(8,128)(2,1)S(1)} %collective-permute-done.10), channel_id=1, source_target_pairs={{0,4},{1,13},{2,6},{3,15},{64,68},{65,77},{66,70},{67,79},{4,8},{5... | collective-permute-start | bytes 1179656 | tf_op jit(solution)/shard_map/ppermute | solution.py:291
  41.1 1.6 copy-start.5
  42.8 10.0 %collective-permute-start.7 = (bf16[64,24,128]{2,1,0:T(8,128)(2,1)S(1)}, bf16[64,24,128]{2,1,0:T(8,128)(2,1)S(1)}, u32[]{:S(2)}, u32[]{:S(2)}) collective-permute-start(bf16[64,24,128]{2,1,0:T(8,128)(2,1)S(1)} %collective-permute-done.5), channel_id=1, source_target_pairs={{0,16},{1,49},{2,18},{3,51},{64,80},{65,113},{66,82},{67,115},{4,2... | collective-permute-start | bytes 1179656 | tf_op jit(solution)/shard_map/ppermute | solution.py:291
  43.9 10.0 %collective-permute-start.8 = (bf16[64,24,128]{2,1,0:T(8,128)(2,1)S(1)}, bf16[64,24,128]{2,1,0:T(8,128)(2,1)S(1)}, u32[]{:S(2)}, u32[]{:S(2)}) collective-permute-start(bf16[64,24,128]{2,1,0:T(8,128)(2,1)S(1)} %collective-permute-done.6), channel_id=1, source_target_pairs={{0,4},{1,13},{2,6},{3,15},{64,68},{65,77},{66,70},{67,79},{4,8},{5... | collective-permute-start | bytes 1179656 | tf_op jit(solution)/shard_map/ppermute | solution.py:291
  53.9 9.0 %collective-permute-start.11 = (bf16[64,24,128]{2,1,0:T(8,128)(2,1)S(1)}, bf16[64,24,128]{2,1,0:T(8,128)(2,1)S(1)}, u32[]{:S(2)}, u32[]{:S(2)}) collective-permute-start(bf16[64,24,128]{2,1,0:T(8,128)(2,1)S(1)} %collective-permute-done.7), channel_id=1, source_target_pairs={{0,16},{1,49},{2,18},{3,51},{64,80},{65,113},{66,82},{67,115},{4,2... | collective-permute-start | bytes 1179656 | tf_op jit(solution)/shard_map/ppermute | solution.py:291
  55.2 9.1 %collective-permute-start.12 = (bf16[64,24,128]{2,1,0:T(8,128)(2,1)S(1)}, bf16[64,24,128]{2,1,0:T(8,128)(2,1)S(1)}, u32[]{:S(2)}, u32[]{:S(2)}) collective-permute-start(bf16[64,24,128]{2,1,0:T(8,128)(2,1)S(1)} %collective-permute-done.8), channel_id=1, source_target_pairs={{0,4},{1,13},{2,6},{3,15},{64,68},{65,77},{66,70},{67,79},{4,8},{5... | collective-permute-start | bytes 1179656 | tf_op jit(solution)/shard_map/ppermute | solution.py:291
  55.3 11.8 %collective-permute-start.20 = (bf16[64,24,128]{2,1,0:T(8,128)(2,1)S(1)}, bf16[64,24,128]{2,1,0:T(8,128)(2,1)S(1)}, u32[]{:S(2)}, u32[]{:S(2)}) collective-permute-start(bf16[64,24,128]{2,1,0:T(8,128)(2,1)S(1)} %collective-permute-done.13), channel_id=1, source_target_pairs={{0,16},{1,49},{2,18},{3,51},{64,80},{65,113},{66,82},{67,115},{4,2... | collective-permute-start | bytes 1179656 | tf_op jit(solution)/shard_map/ppermute | solution.py:291
  56.2 12.2 %collective-permute-start.21 = (bf16[64,24,128]{2,1,0:T(8,128)(2,1)S(1)}, bf16[64,24,128]{2,1,0:T(8,128)(2,1)S(1)}, u32[]{:S(2)}, u32[]{:S(2)}) collective-permute-start(bf16[64,24,128]{2,1,0:T(8,128)(2,1)S(1)} %collective-permute-done.14), channel_id=1, source_target_pairs={{0,4},{1,13},{2,6},{3,15},{64,68},{65,77},{66,70},{67,79},{4,8},{5... | collective-permute-start | bytes 1179656 | tf_op jit(solution)/shard_map/ppermute | solution.py:291
  57.0 47.3 %copy-start.25 = (bf16[128,128]{1,0:T(8,128)(2,1)S(1)}, bf16[128,128]{1,0:T(8,128)(2,1)}, u32[]{:S(2)}) copy-start(bf16[128,128]{1,0:T(8,128)(2,1)} %w_ref.1) | copy-start | bytes 98308
  64.3 40.0 %copy-start.7 = (bf16[64,96,128]{2,1,0:T(8,128)(2,1)}, bf16[64,96,128]{2,1,0:T(8,128)(2,1)S(1)}, u32[]{:S(2)}) copy-start(bf16[64,96,128]{2,1,0:T(8,128)(2,1)S(1)} %constant_dynamic-update-slice_fusion.4.refs_4_) | copy-start | bytes 4718596
  64.3 21.7 %collective-permute-start.15 = (bf16[64,96,128]{2,1,0:T(8,128)(2,1)S(1)}, bf16[64,96,128]{2,1,0:T(8,128)(2,1)S(1)}, u32[]{:S(2)}, u32[]{:S(2)}) collective-permute-start(bf16[64,96,128]{2,1,0:T(8,128)(2,1)S(1)} %constant_dynamic-update-slice_fusion.refs_0_), channel_id=1, source_target_pairs={{0,4},{1,13},{2,6},{3,15},{64,68},{65,77},{66,70},{67,79},{4,8},{5... | collective-permute-start | bytes 4718600 | tf_op jit(solution)/shard_map/ppermute | solution.py:291
  64.4 1.3 copy-start.9
  65.7 21.6 %collective-permute-start.16 = (bf16[64,96,128]{2,1,0:T(8,128)(2,1)S(1)}, bf16[64,96,128]{2,1,0:T(8,128)(2,1)S(1)}, u32[]{:S(2)}, u32[]{:S(2)}) collective-permute-start(bf16[64,96,128]{2,1,0:T(8,128)(2,1)S(1)} %constant_dynamic-update-slice_fusion.4.refs_4_), channel_id=1, source_target_pairs={{0,16},{1,49},{2,18},{3,51},{64,80},{65,113},{66,82},{67,115},{4,2... | collective-permute-start | bytes 4718600 | tf_op jit(solution)/shard_map/ppermute | solution.py:291
  67.2 43.7 %copy-start.16 = (bf16[64,96,128]{2,1,0:T(8,128)(2,1)}, bf16[64,96,128]{2,1,0:T(8,128)(2,1)S(1)}, u32[]{:S(2)}) copy-start(bf16[64,96,128]{2,1,0:T(8,128)(2,1)S(1)} %constant_dynamic-update-slice_fusion.8.refs_0_) | copy-start | bytes 4718596
  68.5 42.4 %copy-start.18 = (bf16[64,96,128]{2,1,0:T(8,128)(2,1)}, bf16[64,96,128]{2,1,0:T(8,128)(2,1)S(1)}, u32[]{:S(2)}) copy-start(bf16[64,96,128]{2,1,0:T(8,128)(2,1)S(1)} %constant_dynamic-update-slice_fusion.12.refs_4_) | copy-start | bytes 4718596
  68.5 34.4 %collective-permute-start.22 = (bf16[64,96,128]{2,1,0:T(8,128)(2,1)S(1)}, bf16[64,96,128]{2,1,0:T(8,128)(2,1)}, u32[]{:S(2)}, u32[]{:S(2)}) collective-permute-start(bf16[64,96,128]{2,1,0:T(8,128)(2,1)S(1)} %constant_dynamic-update-slice_fusion.8.refs_0_), channel_id=1, source_target_pairs={{0,4},{1,13},{2,6},{3,15},{64,68},{65,77},{66,70},{67,79},{4,8},{5... | collective-permute-start | bytes 4718600 | tf_op jit(solution)/shard_map/ppermute | solution.py:291
  68.8 35.5 %collective-permute-start.23 = (bf16[64,96,128]{2,1,0:T(8,128)(2,1)S(1)}, bf16[64,96,128]{2,1,0:T(8,128)(2,1)}, u32[]{:S(2)}, u32[]{:S(2)}) collective-permute-start(bf16[64,96,128]{2,1,0:T(8,128)(2,1)S(1)} %constant_dynamic-update-slice_fusion.12.refs_4_), channel_id=1, source_target_pairs={{0,16},{1,49},{2,18},{3,51},{64,80},{65,113},{66,82},{67,115},{4,2... | collective-permute-start | bytes 4718600 | tf_op jit(solution)/shard_map/ppermute | solution.py:291
  69.7 41.2 %copy-start.20 = (bf16[64,96,128]{2,1,0:T(8,128)(2,1)}, bf16[64,96,128]{2,1,0:T(8,128)(2,1)S(1)}, u32[]{:S(2)}) copy-start(bf16[64,96,128]{2,1,0:T(8,128)(2,1)S(1)} %collective-permute-done.3.c_ref) | copy-start | bytes 4718596
  69.7 51.7 %collective-permute-start.4 = (bf16[64,96,128]{2,1,0:T(8,128)(2,1)S(1)}, bf16[64,96,128]{2,1,0:T(8,128)(2,1)}, u32[]{:S(2)}, u32[]{:S(2)}) collective-permute-start(bf16[64,96,128]{2,1,0:T(8,128)(2,1)S(1)} %get-tuple-element.49), channel_id=1, source_target_pairs={{0,2},{1,3},{2,0},{3,1},{64,66},{65,67},{66,64},{67,65},{4,6},{5,7... | collective-permute-start | bytes 4718600 | tf_op jit(solution)/shard_map/ppermute | solution.py:336
  86.0 24.9 %copy-start.11 = (bf16[64,96,128]{2,1,0:T(8,128)(2,1)}, bf16[64,96,128]{2,1,0:T(8,128)(2,1)S(1)}, u32[]{:S(2)}) copy-start(bf16[64,96,128]{2,1,0:T(8,128)(2,1)S(1)} %collective-permute-done.15.refs_1_) | copy-start | bytes 4718596
  87.3 23.6 %copy-start.13 = (bf16[64,96,128]{2,1,0:T(8,128)(2,1)}, bf16[64,96,128]{2,1,0:T(8,128)(2,1)S(1)}, u32[]{:S(2)}) copy-start(bf16[64,96,128]{2,1,0:T(8,128)(2,1)S(1)} %collective-permute-done.16.refs_5_) | copy-start | bytes 4718596
  87.3 34.1 %collective-permute-start.17 = (bf16[64,96,128]{2,1,0:T(8,128)(2,1)S(1)}, bf16[64,96,128]{2,1,0:T(8,128)(2,1)}, u32[]{:S(2)}, u32[]{:S(2)}) collective-permute-start(bf16[64,96,128]{2,1,0:T(8,128)(2,1)S(1)} %collective-permute-done.15.refs_1_), channel_id=1, source_target_pairs={{0,4},{1,13},{2,6},{3,15},{64,68},{65,77},{66,70},{67,79},{4,8},{5... | collective-permute-start | bytes 4718600 | tf_op jit(solution)/shard_map/ppermute | solution.py:291
  87.4 34.1 %collective-permute-start.18 = (bf16[64,96,128]{2,1,0:T(8,128)(2,1)S(1)}, bf16[64,96,128]{2,1,0:T(8,128)(2,1)}, u32[]{:S(2)}, u32[]{:S(2)}) collective-permute-start(bf16[64,96,128]{2,1,0:T(8,128)(2,1)S(1)} %collective-permute-done.16.refs_5_), channel_id=1, source_target_pairs={{0,16},{1,49},{2,18},{3,51},{64,80},{65,113},{66,82},{67,115},{4,2... | collective-permute-start | bytes 4718600 | tf_op jit(solution)/shard_map/ppermute | solution.py:291
  104.3 18.6 %collective-permute-start.24 = (bf16[64,96,128]{2,1,0:T(8,128)(2,1)S(1)}, bf16[64,96,128]{2,1,0:T(8,128)(2,1)S(1)}, u32[]{:S(2)}, u32[]{:S(2)}) collective-permute-start(bf16[64,96,128]{2,1,0:T(8,128)(2,1)S(1)} %collective-permute-done.3.c_ref), channel_id=1, source_target_pairs={{0,1},{1,0},{2,3},{3,2},{64,65},{65,64},{66,67},{67,66},{4,5},{5,4... | collective-permute-start | bytes 4718600 | tf_op jit(solution)/shard_map/ppermute | solution.py:338
  110.9 2.0 copy-start.1
  119.5 1.9 copy-start.3
  121.4 14.8 %collective-permute-start.19 = (bf16[64,96,128]{2,1,0:T(8,128)(2,1)}, bf16[64,96,128]{2,1,0:T(8,128)(2,1)}, u32[]{:S(2)}, u32[]{:S(2)}) collective-permute-start(bf16[64,96,128]{2,1,0:T(8,128)(2,1)} %collective-permute-done.4.c_ref), channel_id=1, source_target_pairs={{0,1},{1,0},{2,3},{3,2},{64,65},{65,64},{66,67},{67,66},{4,5},{5,4... | collective-permute-start | bytes 4718600 | tf_op jit(solution)/shard_map/ppermute | solution.py:342
  122.0 27.1 %collective-permute-start.27 = (bf16[64,96,128]{2,1,0:T(8,128)(2,1)}, bf16[64,96,128]{2,1,0:T(8,128)(2,1)}, u32[]{:S(2)}, u32[]{:S(2)}) collective-permute-start(bf16[64,96,128]{2,1,0:T(8,128)(2,1)} %collective-permute-done.17.refs_2_), channel_id=1, source_target_pairs={{0,4},{1,13},{2,6},{3,15},{64,68},{65,77},{66,70},{67,79},{4,8},{5... | collective-permute-start | bytes 4718600 | tf_op jit(solution)/shard_map/ppermute | solution.py:291
  122.0 27.1 %collective-permute-start.28 = (bf16[64,96,128]{2,1,0:T(8,128)(2,1)}, bf16[64,96,128]{2,1,0:T(8,128)(2,1)}, u32[]{:S(2)}, u32[]{:S(2)}) collective-permute-start(bf16[64,96,128]{2,1,0:T(8,128)(2,1)} %collective-permute-done.18.refs_6_), channel_id=1, source_target_pairs={{0,16},{1,49},{2,18},{3,51},{64,80},{65,113},{66,82},{67,115},{4,2... | collective-permute-start | bytes 4718600 | tf_op jit(solution)/shard_map/ppermute | solution.py:291
  122.0 40.4 %collective-permute-start.25 = (bf16[64,96,128]{2,1,0:T(8,128)(2,1)}, bf16[64,96,128]{2,1,0:T(8,128)(2,1)}, u32[]{:S(2)}, u32[]{:S(2)}) collective-permute-start(bf16[64,96,128]{2,1,0:T(8,128)(2,1)} %collective-permute-done.22.refs_1_), channel_id=1, source_target_pairs={{0,4},{1,13},{2,6},{3,15},{64,68},{65,77},{66,70},{67,79},{4,8},{5... | collective-permute-start | bytes 4718600 | tf_op jit(solution)/shard_map/ppermute | solution.py:291
  122.9 1.2 copy-start.22
  124.0 38.4 %collective-permute-start.26 = (bf16[64,96,128]{2,1,0:T(8,128)(2,1)}, bf16[64,96,128]{2,1,0:T(8,128)(2,1)}, u32[]{:S(2)}, u32[]{:S(2)}) collective-permute-start(bf16[64,96,128]{2,1,0:T(8,128)(2,1)} %collective-permute-done.23.refs_5_), channel_id=1, source_target_pairs={{0,16},{1,49},{2,18},{3,51},{64,80},{65,113},{66,82},{67,115},{4,2... | collective-permute-start | bytes 4718600 | tf_op jit(solution)/shard_map/ppermute | solution.py:291
  125.6 1.9 copy-start.6
  127.5 1.4 copy-start.21
  128.9 1.4 copy-start.23
  136.2 12.9 %copy-start.8 = (bf16[64,96,128]{2,1,0:T(8,128)(2,1)S(1)}, bf16[64,96,128]{2,1,0:T(8,128)(2,1)}, u32[]{:S(2)}) copy-start(bf16[64,96,128]{2,1,0:T(8,128)(2,1)} %copy-done.7) | copy-start | bytes 4718596
  136.2 12.9 %copy-start.10 = (bf16[64,96,128]{2,1,0:T(8,128)(2,1)S(1)}, bf16[64,96,128]{2,1,0:T(8,128)(2,1)}, u32[]{:S(2)}) copy-start(bf16[64,96,128]{2,1,0:T(8,128)(2,1)} %copy-done.9) | copy-start | bytes 4718596
  136.2 12.9 %copy-start.12 = (bf16[64,96,128]{2,1,0:T(8,128)(2,1)S(1)}, bf16[64,96,128]{2,1,0:T(8,128)(2,1)}, u32[]{:S(2)}) copy-start(bf16[64,96,128]{2,1,0:T(8,128)(2,1)} %copy-done.11) | copy-start | bytes 4718596
  136.2 12.9 %copy-start.14 = (bf16[64,96,128]{2,1,0:T(8,128)(2,1)S(1)}, bf16[64,96,128]{2,1,0:T(8,128)(2,1)}, u32[]{:S(2)}) copy-start(bf16[64,96,128]{2,1,0:T(8,128)(2,1)} %copy-done.13) | copy-start | bytes 4718596
  136.2 12.9 %copy-start.24 = (bf16[128,128]{1,0:T(8,128)(2,1)S(1)}, bf16[128,128]{1,0:T(8,128)(2,1)}, u32[]{:S(2)}) copy-start(bf16[128,128]{1,0:T(8,128)(2,1)} %refs_9_.4) | copy-start | bytes 98308
  144.5 4.6 %copy-start = (bf16[128,128,384]{2,1,0:T(8,128)(2,1)}, bf16[128,128,384]{2,1,0:T(8,128)(2,1)S(1)}, u32[]{:S(2)}) copy-start(bf16[128,128,384]{2,1,0:T(8,128)(2,1)S(1)} %arrange_left.3.lx_ref.ly_ref) | copy-start | bytes 37748740
  149.1 2.2 %copy-start.2 = (bf16[128,128,128]{2,1,0:T(8,128)(2,1)S(1)}, bf16[128,128,128]{2,1,0:T(8,128)(2,1)}, u32[]{:S(2)}) copy-start(bf16[128,128,128]{2,1,0:T(8,128)(2,1)} %copy-done.1) | copy-start | bytes 12582916
  162.4 25.6 %copy-start.17 = (bf16[64,96,128]{2,1,0:T(8,128)(2,1)S(1)}, bf16[64,96,128]{2,1,0:T(8,128)(2,1)}, u32[]{:S(2)}) copy-start(bf16[64,96,128]{2,1,0:T(8,128)(2,1)} %copy-done.16) | copy-start | bytes 4718596
  162.4 25.6 %copy-start.19 = (bf16[64,96,128]{2,1,0:T(8,128)(2,1)S(1)}, bf16[64,96,128]{2,1,0:T(8,128)(2,1)}, u32[]{:S(2)}) copy-start(bf16[64,96,128]{2,1,0:T(8,128)(2,1)} %copy-done.18) | copy-start | bytes 4718596
  162.4 22.0 %collective-permute-start.29 = (bf16[64,96,128]{2,1,0:T(8,128)(2,1)}, bf16[64,96,128]{2,1,0:T(8,128)(2,1)S(1)}, u32[]{:S(2)}, u32[]{:S(2)}) collective-permute-start(bf16[64,96,128]{2,1,0:T(8,128)(2,1)} %collective-permute-done.25.refs_2_), channel_id=1, source_target_pairs={{0,4},{1,13},{2,6},{3,15},{64,68},{65,77},{66,70},{67,79},{4,8},{5... | collective-permute-start | bytes 4718600 | tf_op jit(solution)/shard_map/ppermute | solution.py:291
  166.2 21.8 %collective-permute-start.30 = (bf16[64,96,128]{2,1,0:T(8,128)(2,1)}, bf16[64,96,128]{2,1,0:T(8,128)(2,1)S(1)}, u32[]{:S(2)}, u32[]{:S(2)}) collective-permute-start(bf16[64,96,128]{2,1,0:T(8,128)(2,1)} %collective-permute-done.26.refs_6_), channel_id=1, source_target_pairs={{0,16},{1,49},{2,18},{3,51},{64,80},{65,113},{66,82},{67,115},{4,2... | collective-permute-start | bytes 4718600 | tf_op jit(solution)/shard_map/ppermute | solution.py:291
  167.4 20.6 %copy-start.4 = (bf16[128,128,128]{2,1,0:T(8,128)(2,1)S(1)}, bf16[128,128,128]{2,1,0:T(8,128)(2,1)}, u32[]{:S(2)}) copy-start(bf16[128,128,128]{2,1,0:T(8,128)(2,1)} %copy-done.3) | copy-start | bytes 12582916

commit v3 on v2

--- a/solution.py
+++ b/solution.py
@@ -333,23 +333,20 @@
     c1 = joined(f1)
     step_on(c1, second_rings)
     step_on(c0, second_rings, far_0)
-    far_1 = lax.ppermute(after(near[1], far_0), AXES, SWAP_Z_LO)
-    gate_0 = gate_values(pair_gate, after(out_gate, c1[0][1], c1[1][1]), 0, n_j)
-    far_core_0 = lax.ppermute(after(far_0, c1[0][1], c1[1][1]), AXES, SWAP_CORE)
-    gate_1 = gate_values(pair_gate, after(out_gate, gate_0), 1, n_j)
+    far_core_0 = lax.ppermute(after(far_0, f1[0][3], f1[1][3]), AXES, SWAP_CORE)
+    far_1 = lax.ppermute(after(near[1], far_core_0), AXES, SWAP_Z_LO)
+    gate_0 = gate_values(pair_gate, after(out_gate, c0[0][1], c0[1][1], far_core_0), 0, n_j)
+    orders = left_orders()
+    left = arrange_left(left_local, near_core, far_0, far_core_0, after(orders, gate_0), 0)
+    gate_1 = gate_values(pair_gate, after(out_gate, left, c1[0][1], c1[1][1]), 1, n_j)
+    step_on(c1, second_rings, gate_1)
     step_on(c0, second_rings, gate_1)
-    step_on(c1, second_rings, c0[0][2], c0[1][2], gate_1)
     far_core_1 = lax.ppermute(after(far_1, c0[0][2], c0[1][2]), AXES, SWAP_CORE)
-    orders = left_orders()
     left = arrange_left(
-        left_local, near_core, far_0, far_core_0, after(orders, c0[0][2], c0[1][2]), 0
-    )
-    left = arrange_left(left_local, near_core, far_1, far_core_1, orders, 1, left)
-    whole = update_block(left, *c0, gate_0, out_proj, 0, n_blocks, 0, 2)
-    step_on(c1, second_rings, whole)
-    whole = update_block(
-        left, *c0, gate_0, after(out_proj, c1[0][2], c1[1][2]), 0, n_blocks, 1, 2, whole
-    )
+        left_local, near_core, far_1, far_core_1, after(orders, c0[0][2], c0[1][2]), 1, left
+    )
+    step_on(c1, second_rings, left)
+    whole = update_block(left, *c0, gate_0, out_proj, 0, n_blocks, 0, 1)
     return update_block(left, *c1, gate_1, out_proj, 1, n_blocks, 0, 1, whole)
 
 

time: 207 us -> 199 us (0.961)
  starting transfers between devices: 29.5 us -> 24 us
  Pallas kernels: 79.6 us -> 74.9 us
  local copies, waits for them, and re-layouts: 23.9 us -> 28.1 us
    ppermute x24, waiting for transfers between devices: 65.7 us -> 55.3 us  [step_on(): held.append(lax.ppermute(piece, AXES, ring))]
    ppermute x24, starting transfers between devices: 22.3 us -> 17.1 us  [step_on(): held.append(lax.ppermute(piece, AXES, ring))]
    ppermute x1, waiting for transfers between devices: 0.01 us -> 5.01 us  [shards(): far_0 = lax.ppermute(after(near[0], *others, *halves_0), AXES, SWAP_Z_LO)]
    pallas_call x3 -> x2, Pallas kernels: 40.6 us -> 36.7 us  [update_block(): pl.pallas_call(functools.partial(update_kernel, n_sum), grid=(n_sum + n_o...]
    ppermute x2, waiting for transfers between devices: 0.01 us -> 3.33 us  [the longest x1 3.32 us: shards(): far_1 = lax.ppermute(after(near[1], far_core_0), AXES, SWAP_Z_LO)]
    unnamed x76 -> x70, local copies, waits for them, and re-layouts: 22.3 us -> 23.7 us
  transfers between devices with their start and end apart: 31 -> 31, of which waited for: 16 -> 22; matrix products, arithmetic and copies ran while one was open for 1% -> 5% of each run, Pallas kernels for 30% -> 28%
where the time goes in v3:
time: 199 us
  Pallas kernels  74.9 us (38%)
  waiting for transfers between devices  71.2 us (36%)
  local copies, waits for them, and re-layouts  28.1 us (14%)
  starting transfers between devices  24 us (12%)
    ppermute x24, waiting for transfers between devices, step_on(): held.append(lax.ppermute(piece, AXES, ring))  55.3 us
    pallas_call x2, Pallas kernels, update_block(): pl.pallas_call(functools.partial(update_kernel, n_sum), grid=(n_sum + n_o...  36.7 us
    unnamed x70, local copies, waits for them, and re-layouts  23.7 us
    ppermute x24, starting transfers between devices, step_on(): held.append(lax.ppermute(piece, AXES, ring))  17.1 us
    pallas_call x2, Pallas kernels, arrange_left(): pl.pallas_call(arrange_kernel, grid=(steps,), in_specs=in_specs, out_spec...  13.3 us
    pallas_call x2, Pallas kernels, gate_values(): pl.pallas_call(gate_kernel, grid=(n_i // block,), in_specs=[pl.BlockSpec(...  13.1 us
    pallas_call x1, Pallas kernels, project_left(): pl.pallas_call(left_kernel, grid=(n_k // block,), in_specs=[pl.BlockSpec(...  8.93 us
    ppermute x2, waiting for transfers between devices, shards(): others = [lax.ppermute(block, AXES, SWAP_Z_HI) for block in blocks]  6.6 us
  transfers between devices with their start and end apart: 31, of which 22 were waited for; matrix products, arithmetic and copies ran while one was open for 5% of the time, Pallas kernels for 28%

profile of v3, /device:TPU:0, one launch (start us, length us, event | category | flops | bytes accessed | tf_op | source)
XLA Modules:
  0.0 199.1 jit_solution(16229963597927849364)
XLA Ops:
  0.0 1.2 fusion.45
  1.2 4.0 %collective-permute-start.1 = (bf16[12,128,128]{2,1,0:T(8,128)(2,1)S(1)}, bf16[12,128,128]{2,1,0:T(8,128)(2,1)S(1)}, u32[]{:S(2)}, u32[]{:S(2)}) collective-permute-start(bf16[12,128,128]{2,1,0:T(8,128)(2,1)S(1)} %get-tuple-element.85.own_ref), channel_id=1, source_target_pairs={{0,64},{1,65},{2,66},{3,67},{64,0},{65,1},{66,2},{67,3},{4,68},{5,... | collective-permute-start | bytes 1179656 | tf_op jit(solution)/shard_map/ppermute | solution.py:315
  5.3 1.9 copy-done.8
  7.2 8.9 %project_left.1.a_ref = bf16[128,96,128]{2,1,0:T(8,128)(2,1)S(1)} custom-call(bf16[128,96,128]{2,1,0:T(8,128)(2,1)S(1)} %copy-done.8, bf16[128,128]{1,0:T(8,128)(2,1)S(1)} %copy-done.25, bf16[128,128]{1,0:T(8,128)(2,1)S(1)} %copy-done.26), custom_call_target="tpu_custom_call" | custom-call | flops 805306368 | bytes 12582912 | tf_op jit(solution)/shard_map/project_left/pallas_call | solution.py:80
  16.2 6.6 %collective-permute-done.other_ref = bf16[12,128,128]{2,1,0:T(8,128)(2,1)S(1)} collective-permute-done((bf16[12,128,128]{2,1,0:T(8,128)(2,1)S(1)}, bf16[12,128,128]{2,1,0:T(8,128)(2,1)S(1)}, u32[]{:S(2)}, u32[]{:S(2)}) %collective-permute-start) | collective-permute-done | bytes 393248 | tf_op jit(solution)/shard_map/ppermute | solution.py:315
  22.8 1.4 project_right.2
  24.2 1.6 collective-permute-start.6
  25.8 1.4 fusion.44
  27.2 1.3 collective-permute-start.3
  28.5 1.6 collective-permute-start.9
  30.0 1.4 project_right.3
  31.5 1.6 collective-permute-start.4
  33.3 1.6 collective-permute-start.5
  34.9 2.6 %collective-permute-done.9 = bf16[64,24,128]{2,1,0:T(8,128)(2,1)S(1)} collective-permute-done((bf16[64,24,128]{2,1,0:T(8,128)(2,1)S(1)}, bf16[64,24,128]{2,1,0:T(8,128)(2,1)S(1)}, u32[]{:S(2)}, u32[]{:S(2)}) %collective-permute-start.9) | collective-permute-done | bytes 393248 | tf_op jit(solution)/shard_map/ppermute | solution.py:291
  37.4 1.5 collective-permute-start.10
  39.3 1.2 collective-permute-done.4
  40.5 1.7 collective-permute-done.5
  42.3 0.9 collective-permute-start.7
  43.7 2.8 %collective-permute-done.10 = bf16[64,24,128]{2,1,0:T(8,128)(2,1)S(1)} collective-permute-done((bf16[64,24,128]{2,1,0:T(8,128)(2,1)S(1)}, bf16[64,24,128]{2,1,0:T(8,128)(2,1)S(1)}, u32[]{:S(2)}, u32[]{:S(2)}) %collective-permute-start.10) | collective-permute-done | bytes 393248 | tf_op jit(solution)/shard_map/ppermute | solution.py:291
  46.4 1.5 collective-permute-done.11
  47.9 1.2 collective-permute-start.16
  49.4 1.9 collective-permute-done.7
  51.2 0.9 collective-permute-done.8
  52.2 1.1 collective-permute-start.12
  53.5 3.4 %collective-permute-done.16 = bf16[64,24,128]{2,1,0:T(8,128)(2,1)S(1)} collective-permute-done((bf16[64,24,128]{2,1,0:T(8,128)(2,1)S(1)}, bf16[64,24,128]{2,1,0:T(8,128)(2,1)S(1)}, u32[]{:S(2)}, u32[]{:S(2)}) %collective-permute-start.16) | collective-permute-done | bytes 393248 | tf_op jit(solution)/shard_map/ppermute | solution.py:291
  57.0 1.3 collective-permute-done.17
  58.4 0.5 collective-permute-start.19
  59.0 5.0 %collective-permute-done.3.c_ref = bf16[64,96,128]{2,1,0:T(8,128)(2,1)S(1)} collective-permute-done((bf16[64,96,128]{2,1,0:T(8,128)(2,1)S(1)}, bf16[64,96,128]{2,1,0:T(8,128)(2,1)S(1)}, u32[]{:S(2)}, u32[]{:S(2)}) %collective-permute-start.3) | collective-permute-done | bytes 1572896 | tf_op jit(solution)/shard_map/ppermute | solution.py:322
  64.0 0.7 collective-permute-start.14
  64.7 1.1 copy-done.15
  65.8 0.8 constant_dynamic-update-slice_fusion.11
  66.6 0.8 constant_dynamic-update-slice_fusion.15
  67.5 0.9 constant_dynamic-update-slice_fusion.10
  68.3 0.9 constant_dynamic-update-slice_fusion.14
  69.2 0.9 constant_dynamic-update-slice_fusion.9
  70.1 0.9 constant_dynamic-update-slice_fusion.13
  71.0 0.8 constant_dynamic-update-slice_fusion.8.refs_0_
  71.9 0.8 constant_dynamic-update-slice_fusion.12.refs_4_
  72.7 1.6 collective-permute-start.23
  74.3 5.8 %collective-permute-done.18.refs_1_ = bf16[64,96,128]{2,1,0:T(8,128)(2,1)} collective-permute-done((bf16[64,96,128]{2,1,0:T(8,128)(2,1)S(1)}, bf16[64,96,128]{2,1,0:T(8,128)(2,1)}, u32[]{:S(2)}, u32[]{:S(2)}) %collective-permute-start.18) | collective-permute-done | bytes 1572896 | tf_op jit(solution)/shard_map/ppermute | solution.py:291
  80.2 0.4 collective-permute-start.21
  80.6 1.1 copy-done.17
  81.8 0.8 collective-permute-start.15
  83.1 3.4 %copy-done.1 = bf16[128,256,128]{2,1,0:T(8,128)(2,1)S(1)} copy-done((bf16[128,256,128]{2,1,0:T(8,128)(2,1)S(1)}, bf16[128,256,128]{2,1,0:T(8,128)(2,1)}, u32[]{:S(2)}) %copy-start.1) | copy-done | bytes 8388632
  86.5 6.5 %gate_values.2.refs_8_ = bf16[128,128,128]{2,1,0:T(8,128)(2,1)S(1)} custom-call(bf16[128,256,128]{2,1,0:T(8,128)(2,1)S(1)} %copy-done.1, bf16[128,128]{1,0:T(8,128)(2,1)S(1)} %copy-done.21), custom_call_target="tpu_custom_call" | custom-call | flops 1000 | bytes 1000 | tf_op jit(solution)/shard_map/gate_values/pallas_call | solution.py:140
  93.1 5.9 %arrange_left.2.rest_0_ = bf16[128,128,384]{2,1,0:T(8,128)(2,1)S(1)} custom-call(bf16[128,96,128]{2,1,0:T(8,128)(2,1)S(1)} %project_left.1.a_ref, bf16[128,96,128]{2,1,0:T(8,128)(2,1)S(1)} %copy-done.7, bf16[64,96,128]{2,1,0:T(8,128)(2,1)S(1)} %copy-done.16, bf16[64,96,128]{2,1,0:T(8,128)(2,1)S(1)} %copy-done.18, ...), custom_call_target="tpu_custom_call" | custom-call | flops 1000 | bytes 1000 | tf_op jit(solution)/shard_map/arrange_left/pallas_call | solution.py:181
  99.0 6.5 %gate_values.3.refs_8_ = bf16[128,128,128]{2,1,0:T(8,128)(2,1)S(1)} custom-call(bf16[128,256,128]{2,1,0:T(8,128)(2,1)S(1)} %bitcast.2, bf16[128,128]{1,0:T(8,128)(2,1)S(1)} %copy-done.21), custom_call_target="tpu_custom_call" | custom-call | flops 1000 | bytes 1000 | tf_op jit(solution)/shard_map/gate_values/pallas_call | solution.py:140
  105.6 8.3 %collective-permute-done.20.refs_2_ = bf16[64,96,128]{2,1,0:T(8,128)(2,1)} collective-permute-done((bf16[64,96,128]{2,1,0:T(8,128)(2,1)}, bf16[64,96,128]{2,1,0:T(8,128)(2,1)}, u32[]{:S(2)}, u32[]{:S(2)}) %collective-permute-start.20) | collective-permute-done | bytes 1572896 | tf_op jit(solution)/shard_map/ppermute | solution.py:291
  113.9 3.3 %collective-permute-done.15.c_ref = bf16[64,96,128]{2,1,0:T(8,128)(2,1)} collective-permute-done((bf16[64,96,128]{2,1,0:T(8,128)(2,1)}, bf16[64,96,128]{2,1,0:T(8,128)(2,1)}, u32[]{:S(2)}, u32[]{:S(2)}) %collective-permute-start.15) | collective-permute-done | bytes 1572896 | tf_op jit(solution)/shard_map/ppermute | solution.py:337
  117.3 1.6 collective-permute-start.25
  119.3 0.6 collective-permute-start.30
  119.9 1.0 collective-permute-done.22.d_ref
  120.9 7.5 %arrange_left.3.lx_ref.ly_ref = bf16[128,128,384]{2,1,0:T(8,128)(2,1)S(1)} custom-call(bf16[128,96,128]{2,1,0:T(8,128)(2,1)S(1)} %project_left.1.a_ref, bf16[128,96,128]{2,1,0:T(8,128)(2,1)S(1)} %copy-done.7, bf16[64,96,128]{2,1,0:T(8,128)(2,1)} %collective-permute-done.15.c_ref, ...), custom_call_target="tpu_custom_call", output_to_operand_aliasing={{}: (5, {})} | custom-call | flops 1000 | bytes 1000 | tf_op jit(solution)/shard_map/arrange_left/pallas_call | solution.py:181
  128.4 4.6 %copy-done = bf16[128,128,384]{2,1,0:T(8,128)(2,1)} copy-done((bf16[128,128,384]{2,1,0:T(8,128)(2,1)}, bf16[128,128,384]{2,1,0:T(8,128)(2,1)S(1)}, u32[]{:S(2)}) %copy-start) | copy-done | bytes 12582936
  132.9 6.2 %collective-permute-done.25.refs_2_ = bf16[64,96,128]{2,1,0:T(8,128)(2,1)S(1)} collective-permute-done((bf16[64,96,128]{2,1,0:T(8,128)(2,1)}, bf16[64,96,128]{2,1,0:T(8,128)(2,1)S(1)}, u32[]{:S(2)}, u32[]{:S(2)}) %collective-permute-start.25) | collective-permute-done | bytes 1572896 | tf_op jit(solution)/shard_map/ppermute | solution.py:291
  139.1 1.7 collective-permute-done.26.refs_6_
  140.8 1.1 copy-done.19
  142.0 14.0 %collective-permute-done.29.refs_3_ = bf16[64,96,128]{2,1,0:T(8,128)(2,1)S(1)} collective-permute-done((bf16[64,96,128]{2,1,0:T(8,128)(2,1)}, bf16[64,96,128]{2,1,0:T(8,128)(2,1)S(1)}, u32[]{:S(2)}, u32[]{:S(2)}) %collective-permute-start.29) | collective-permute-done | bytes 1572896 | tf_op jit(solution)/shard_map/ppermute | solution.py:291
  156.0 1.6 collective-permute-done.30.refs_7_
  157.6 1.2 copy-done.13
  158.8 2.2 %copy-done.5 = bf16[128,128,128]{2,1,0:T(8,128)(2,1)S(1)} copy-done((bf16[128,128,128]{2,1,0:T(8,128)(2,1)S(1)}, bf16[128,128,128]{2,1,0:T(8,128)(2,1)}, u32[]{:S(2)}) %copy-start.5) | copy-done | bytes 4194328
  160.9 1.4 copy-done.14
  162.4 18.4 %update_block.2.refs_10_ = bf16[128,256,128]{2,1,0:T(8,128)(2,1)} custom-call(bf16[128,128,384]{2,1,0:T(8,128)(2,1)} %copy-done, bf16[128,128,384]{2,1,0:T(8,128)(2,1)} %copy-done, bf16[64,96,128]{2,1,0:T(8,128)(2,1)S(1)} %copy-done.12, bf16[64,96,128]{2,1,0:T(8,128)(2,1)} %collective-permute-done.18.refs_1_, ...), custom_call_target="tpu_custom_call" | custom-call | flops 1000 | bytes 1000 | tf_op jit(solution)/shard_map/update_block/pallas_call | solution.py:270
  180.8 18.3 %update_block.3 = bf16[128,256,128]{2,1,0:T(8,128)(2,1)} custom-call(bf16[128,128,384]{2,1,0:T(8,128)(2,1)} %copy-done, bf16[128,128,384]{2,1,0:T(8,128)(2,1)} %copy-done, bf16[64,96,128]{2,1,0:T(8,128)(2,1)} %constant_dynamic-update-slice_fusion.8.refs_0_, bf16[64,96,128]{2,1,0:T(8,128)(2,1)} %collective-permute-done.23.refs_1_, ...), custom_call_target="tpu_custom_call", output_to_operand_aliasing={{}: (12, {})} | custom-call | flops 1000 | bytes 1000 | tf_op jit(solution)/shard_map/update_block/pallas_call | solution.py:270
  (92 shorter events, 2.9 us)
Async XLA Ops:
  0.0 5.3 %copy-start.26 = (bf16[128,128]{1,0:T(8,128)(2,1)S(1)}, bf16[128,128]{1,0:T(8,128)(2,1)}, u32[]{:S(2)}) copy-start(bf16[128,128]{1,0:T(8,128)(2,1)} %gate_ref.3) | copy-start | bytes 98308
  0.0 5.3 %copy-start.25 = (bf16[128,128]{1,0:T(8,128)(2,1)S(1)}, bf16[128,128]{1,0:T(8,128)(2,1)}, u32[]{:S(2)}) copy-start(bf16[128,128]{1,0:T(8,128)(2,1)} %proj_ref.3) | copy-start | bytes 98308
  1.2 15.0 %collective-permute-start.1 = (bf16[12,128,128]{2,1,0:T(8,128)(2,1)S(1)}, bf16[12,128,128]{2,1,0:T(8,128)(2,1)S(1)}, u32[]{:S(2)}, u32[]{:S(2)}) collective-permute-start(bf16[12,128,128]{2,1,0:T(8,128)(2,1)S(1)} %get-tuple-element.85.own_ref), channel_id=1, source_target_pairs={{0,64},{1,65},{2,66},{3,67},{64,0},{65,1},{66,2},{67,3},{4,68},{5,... | collective-permute-start | bytes 1179656 | tf_op jit(solution)/shard_map/ppermute | solution.py:315
  5.2 17.5 %collective-permute-start = (bf16[12,128,128]{2,1,0:T(8,128)(2,1)S(1)}, bf16[12,128,128]{2,1,0:T(8,128)(2,1)S(1)}, u32[]{:S(2)}, u32[]{:S(2)}) collective-permute-start(bf16[12,128,128]{2,1,0:T(8,128)(2,1)S(1)} %get-tuple-element.86.own_ref), channel_id=1, source_target_pairs={{0,64},{1,65},{2,66},{3,67},{64,0},{65,1},{66,2},{67,3},{4,68},{5,... | collective-permute-start | bytes 1179656 | tf_op jit(solution)/shard_map/ppermute | solution.py:315
  5.3 1.9 copy-start.8
  7.2 15.6 %copy-start.22 = (bf16[128,128]{1,0:T(8,128)(2,1)S(1)}, bf16[128,128]{1,0:T(8,128)(2,1)}, u32[]{:S(2)}) copy-start(bf16[128,128]{1,0:T(8,128)(2,1)} %proj_ref.5) | copy-start | bytes 98308
  7.2 15.6 %copy-start.23 = (bf16[128,128]{1,0:T(8,128)(2,1)S(1)}, bf16[128,128]{1,0:T(8,128)(2,1)}, u32[]{:S(2)}) copy-start(bf16[128,128]{1,0:T(8,128)(2,1)} %gate_ref.5) | copy-start | bytes 98308
  22.8 14.7 %collective-permute-start.2 = (bf16[128,96,128]{2,1,0:T(8,128)(2,1)S(1)}, bf16[128,96,128]{2,1,0:T(8,128)(2,1)S(1)}, u32[]{:S(2)}, u32[]{:S(2)}) collective-permute-start(bf16[128,96,128]{2,1,0:T(8,128)(2,1)S(1)} %project_left.1.a_ref), channel_id=1, source_target_pairs={{0,1},{1,0},{2,3},{3,2},{64,65},{65,64},{66,67},{67,66},{4,5},{5,4... | collective-permute-start | bytes 9437192 | tf_op jit(solution)/shard_map/ppermute | solution.py:321
  24.2 9.1 %collective-permute-start.6 = (bf16[64,24,128]{2,1,0:T(8,128)(2,1)S(1)}, bf16[64,24,128]{2,1,0:T(8,128)(2,1)S(1)}, u32[]{:S(2)}, u32[]{:S(2)}) collective-permute-start(bf16[64,24,128]{2,1,0:T(8,128)(2,1)S(1)} %get-tuple-element.46), channel_id=1, source_target_pairs={{0,16},{1,49},{2,18},{3,51},{64,80},{65,113},{66,82},{67,115},{4,2... | collective-permute-start | bytes 1179656 | tf_op jit(solution)/shard_map/ppermute | solution.py:291
  27.2 36.8 %collective-permute-start.3 = (bf16[64,96,128]{2,1,0:T(8,128)(2,1)S(1)}, bf16[64,96,128]{2,1,0:T(8,128)(2,1)S(1)}, u32[]{:S(2)}, u32[]{:S(2)}) collective-permute-start(bf16[64,96,128]{2,1,0:T(8,128)(2,1)S(1)} %get-tuple-element.48), channel_id=1, source_target_pairs={{0,2},{1,3},{2,0},{3,1},{64,66},{65,67},{66,64},{67,65},{4,6},{5,7... | collective-permute-start | bytes 4718600 | tf_op jit(solution)/shard_map/ppermute | solution.py:322
  28.5 9.0 %collective-permute-start.9 = (bf16[64,24,128]{2,1,0:T(8,128)(2,1)S(1)}, bf16[64,24,128]{2,1,0:T(8,128)(2,1)S(1)}, u32[]{:S(2)}, u32[]{:S(2)}) collective-permute-start(bf16[64,24,128]{2,1,0:T(8,128)(2,1)S(1)} %get-tuple-element.47), channel_id=1, source_target_pairs={{0,4},{1,13},{2,6},{3,15},{64,68},{65,77},{66,70},{67,79},{4,8},{5... | collective-permute-start | bytes 1179656 | tf_op jit(solution)/shard_map/ppermute | solution.py:291
  31.5 9.1 %collective-permute-start.4 = (bf16[64,24,128]{2,1,0:T(8,128)(2,1)S(1)}, bf16[64,24,128]{2,1,0:T(8,128)(2,1)S(1)}, u32[]{:S(2)}, u32[]{:S(2)}) collective-permute-start(bf16[64,24,128]{2,1,0:T(8,128)(2,1)S(1)} %get-tuple-element.56), channel_id=1, source_target_pairs={{0,16},{1,49},{2,18},{3,51},{64,80},{65,113},{66,82},{67,115},{4,2... | collective-permute-start | bytes 1179656 | tf_op jit(solution)/shard_map/ppermute | solution.py:291
  33.3 9.0 %collective-permute-start.5 = (bf16[64,24,128]{2,1,0:T(8,128)(2,1)S(1)}, bf16[64,24,128]{2,1,0:T(8,128)(2,1)S(1)}, u32[]{:S(2)}, u32[]{:S(2)}) collective-permute-start(bf16[64,24,128]{2,1,0:T(8,128)(2,1)S(1)} %get-tuple-element.51), channel_id=1, source_target_pairs={{0,4},{1,13},{2,6},{3,15},{64,68},{65,77},{66,70},{67,79},{4,8},{5... | collective-permute-start | bytes 1179656 | tf_op jit(solution)/shard_map/ppermute | solution.py:291
  37.4 11.9 %copy-start.6 = (bf16[128,96,128]{2,1,0:T(8,128)(2,1)}, bf16[128,96,128]{2,1,0:T(8,128)(2,1)S(1)}, u32[]{:S(2)}) copy-start(bf16[128,96,128]{2,1,0:T(8,128)(2,1)S(1)} %collective-permute-done.2.b_ref) | copy-start | bytes 9437188
  37.4 9.0 %collective-permute-start.10 = (bf16[64,24,128]{2,1,0:T(8,128)(2,1)S(1)}, bf16[64,24,128]{2,1,0:T(8,128)(2,1)S(1)}, u32[]{:S(2)}, u32[]{:S(2)}) collective-permute-start(bf16[64,24,128]{2,1,0:T(8,128)(2,1)S(1)} %collective-permute-done.6), channel_id=1, source_target_pairs={{0,16},{1,49},{2,18},{3,51},{64,80},{65,113},{66,82},{67,115},{4,2... | collective-permute-start | bytes 1179656 | tf_op jit(solution)/shard_map/ppermute | solution.py:291
  38.9 9.0 %collective-permute-start.11 = (bf16[64,24,128]{2,1,0:T(8,128)(2,1)S(1)}, bf16[64,24,128]{2,1,0:T(8,128)(2,1)S(1)}, u32[]{:S(2)}, u32[]{:S(2)}) collective-permute-start(bf16[64,24,128]{2,1,0:T(8,128)(2,1)S(1)} %collective-permute-done.9), channel_id=1, source_target_pairs={{0,4},{1,13},{2,6},{3,15},{64,68},{65,77},{66,70},{67,79},{4,8},{5... | collective-permute-start | bytes 1179656 | tf_op jit(solution)/shard_map/ppermute | solution.py:291
  42.3 9.0 %collective-permute-start.7 = (bf16[64,24,128]{2,1,0:T(8,128)(2,1)S(1)}, bf16[64,24,128]{2,1,0:T(8,128)(2,1)S(1)}, u32[]{:S(2)}, u32[]{:S(2)}) collective-permute-start(bf16[64,24,128]{2,1,0:T(8,128)(2,1)S(1)} %collective-permute-done.4), channel_id=1, source_target_pairs={{0,16},{1,49},{2,18},{3,51},{64,80},{65,113},{66,82},{67,115},{4,2... | collective-permute-start | bytes 1179656 | tf_op jit(solution)/shard_map/ppermute | solution.py:291
  43.2 9.0 %collective-permute-start.8 = (bf16[64,24,128]{2,1,0:T(8,128)(2,1)S(1)}, bf16[64,24,128]{2,1,0:T(8,128)(2,1)S(1)}, u32[]{:S(2)}, u32[]{:S(2)}) collective-permute-start(bf16[64,24,128]{2,1,0:T(8,128)(2,1)S(1)} %collective-permute-done.5), channel_id=1, source_target_pairs={{0,4},{1,13},{2,6},{3,15},{64,68},{65,77},{66,70},{67,79},{4,8},{5... | collective-permute-start | bytes 1179656 | tf_op jit(solution)/shard_map/ppermute | solution.py:291
  47.9 9.0 %collective-permute-start.16 = (bf16[64,24,128]{2,1,0:T(8,128)(2,1)S(1)}, bf16[64,24,128]{2,1,0:T(8,128)(2,1)S(1)}, u32[]{:S(2)}, u32[]{:S(2)}) collective-permute-start(bf16[64,24,128]{2,1,0:T(8,128)(2,1)S(1)} %collective-permute-done.10), channel_id=1, source_target_pairs={{0,16},{1,49},{2,18},{3,51},{64,80},{65,113},{66,82},{67,115},{4,2... | collective-permute-start | bytes 1179656 | tf_op jit(solution)/shard_map/ppermute | solution.py:291
  49.2 9.1 %collective-permute-start.17 = (bf16[64,24,128]{2,1,0:T(8,128)(2,1)S(1)}, bf16[64,24,128]{2,1,0:T(8,128)(2,1)S(1)}, u32[]{:S(2)}, u32[]{:S(2)}) collective-permute-start(bf16[64,24,128]{2,1,0:T(8,128)(2,1)S(1)} %collective-permute-done.11), channel_id=1, source_target_pairs={{0,4},{1,13},{2,6},{3,15},{64,68},{65,77},{66,70},{67,79},{4,8},{5... | collective-permute-start | bytes 1179656 | tf_op jit(solution)/shard_map/ppermute | solution.py:291
  52.2 11.8 %collective-permute-start.12 = (bf16[64,24,128]{2,1,0:T(8,128)(2,1)S(1)}, bf16[64,24,128]{2,1,0:T(8,128)(2,1)S(1)}, u32[]{:S(2)}, u32[]{:S(2)}) collective-permute-start(bf16[64,24,128]{2,1,0:T(8,128)(2,1)S(1)} %collective-permute-done.7), channel_id=1, source_target_pairs={{0,16},{1,49},{2,18},{3,51},{64,80},{65,113},{66,82},{67,115},{4,2... | collective-permute-start | bytes 1179656 | tf_op jit(solution)/shard_map/ppermute | solution.py:291
  53.3 10.7 %collective-permute-start.13 = (bf16[64,24,128]{2,1,0:T(8,128)(2,1)S(1)}, bf16[64,24,128]{2,1,0:T(8,128)(2,1)S(1)}, u32[]{:S(2)}, u32[]{:S(2)}) collective-permute-start(bf16[64,24,128]{2,1,0:T(8,128)(2,1)S(1)} %collective-permute-done.8), channel_id=1, source_target_pairs={{0,4},{1,13},{2,6},{3,15},{64,68},{65,77},{66,70},{67,79},{4,8},{5... | collective-permute-start | bytes 1179656 | tf_op jit(solution)/shard_map/ppermute | solution.py:291
  57.0 11.4 %copy-start.11 = (bf16[64,96,128]{2,1,0:T(8,128)(2,1)}, bf16[64,96,128]{2,1,0:T(8,128)(2,1)S(1)}, u32[]{:S(2)}) copy-start(bf16[64,96,128]{2,1,0:T(8,128)(2,1)S(1)} %constant_dynamic-update-slice_fusion.refs_0_) | copy-start | bytes 4718596
  58.3 10.9 %copy-start.9 = (bf16[64,96,128]{2,1,0:T(8,128)(2,1)}, bf16[64,96,128]{2,1,0:T(8,128)(2,1)S(1)}, u32[]{:S(2)}) copy-start(bf16[64,96,128]{2,1,0:T(8,128)(2,1)S(1)} %constant_dynamic-update-slice_fusion.4.refs_4_) | copy-start | bytes 4718596
  58.3 21.8 %collective-permute-start.18 = (bf16[64,96,128]{2,1,0:T(8,128)(2,1)S(1)}, bf16[64,96,128]{2,1,0:T(8,128)(2,1)}, u32[]{:S(2)}, u32[]{:S(2)}) collective-permute-start(bf16[64,96,128]{2,1,0:T(8,128)(2,1)S(1)} %constant_dynamic-update-slice_fusion.refs_0_), channel_id=1, source_target_pairs={{0,4},{1,13},{2,6},{3,15},{64,68},{65,77},{66,70},{67,79},{4,8},{5... | collective-permute-start | bytes 4718600 | tf_op jit(solution)/shard_map/ppermute | solution.py:291
  58.4 21.8 %collective-permute-start.19 = (bf16[64,96,128]{2,1,0:T(8,128)(2,1)S(1)}, bf16[64,96,128]{2,1,0:T(8,128)(2,1)}, u32[]{:S(2)}, u32[]{:S(2)}) collective-permute-start(bf16[64,96,128]{2,1,0:T(8,128)(2,1)S(1)} %constant_dynamic-update-slice_fusion.4.refs_4_), channel_id=1, source_target_pairs={{0,16},{1,49},{2,18},{3,51},{64,80},{65,113},{66,82},{67,115},{4,2... | collective-permute-start | bytes 4718600 | tf_op jit(solution)/shard_map/ppermute | solution.py:291
  64.0 16.6 %collective-permute-start.14 = (bf16[64,96,128]{2,1,0:T(8,128)(2,1)S(1)}, bf16[64,96,128]{2,1,0:T(8,128)(2,1)S(1)}, u32[]{:S(2)}, u32[]{:S(2)}) collective-permute-start(bf16[64,96,128]{2,1,0:T(8,128)(2,1)S(1)} %collective-permute-done.3.c_ref), channel_id=1, source_target_pairs={{0,1},{1,0},{2,3},{3,2},{64,65},{65,64},{66,67},{67,66},{4,5},{5,4... | collective-permute-start | bytes 4718600 | tf_op jit(solution)/shard_map/ppermute | solution.py:336
  64.7 1.1 copy-start.15
  71.0 12.0 %copy-start.21 = (bf16[128,128]{1,0:T(8,128)(2,1)S(1)}, bf16[128,128]{1,0:T(8,128)(2,1)}, u32[]{:S(2)}) copy-start(bf16[128,128]{1,0:T(8,128)(2,1)} %w_ref.1) | copy-start | bytes 98308
  72.7 26.2 %collective-permute-start.23 = (bf16[64,96,128]{2,1,0:T(8,128)(2,1)}, bf16[64,96,128]{2,1,0:T(8,128)(2,1)}, u32[]{:S(2)}, u32[]{:S(2)}) collective-permute-start(bf16[64,96,128]{2,1,0:T(8,128)(2,1)} %constant_dynamic-update-slice_fusion.8.refs_0_), channel_id=1, source_target_pairs={{0,4},{1,13},{2,6},{3,15},{64,68},{65,77},{66,70},{67,79},{4,8},{5... | collective-permute-start | bytes 4718600 | tf_op jit(solution)/shard_map/ppermute | solution.py:291
  74.3 24.7 %collective-permute-start.24 = (bf16[64,96,128]{2,1,0:T(8,128)(2,1)}, bf16[64,96,128]{2,1,0:T(8,128)(2,1)}, u32[]{:S(2)}, u32[]{:S(2)}) collective-permute-start(bf16[64,96,128]{2,1,0:T(8,128)(2,1)} %constant_dynamic-update-slice_fusion.12.refs_4_), channel_id=1, source_target_pairs={{0,16},{1,49},{2,18},{3,51},{64,80},{65,113},{66,82},{67,115},{4,2... | collective-permute-start | bytes 4718600 | tf_op jit(solution)/shard_map/ppermute | solution.py:291
  80.2 33.6 %collective-permute-start.20 = (bf16[64,96,128]{2,1,0:T(8,128)(2,1)}, bf16[64,96,128]{2,1,0:T(8,128)(2,1)}, u32[]{:S(2)}, u32[]{:S(2)}) collective-permute-start(bf16[64,96,128]{2,1,0:T(8,128)(2,1)} %collective-permute-done.18.refs_1_), channel_id=1, source_target_pairs={{0,4},{1,13},{2,6},{3,15},{64,68},{65,77},{66,70},{67,79},{4,8},{5... | collective-permute-start | bytes 4718600 | tf_op jit(solution)/shard_map/ppermute | solution.py:291
  80.2 33.7 %collective-permute-start.21 = (bf16[64,96,128]{2,1,0:T(8,128)(2,1)}, bf16[64,96,128]{2,1,0:T(8,128)(2,1)}, u32[]{:S(2)}, u32[]{:S(2)}) collective-permute-start(bf16[64,96,128]{2,1,0:T(8,128)(2,1)} %collective-permute-done.19.refs_5_), channel_id=1, source_target_pairs={{0,16},{1,49},{2,18},{3,51},{64,80},{65,113},{66,82},{67,115},{4,2... | collective-permute-start | bytes 4718600 | tf_op jit(solution)/shard_map/ppermute | solution.py:291
  80.6 1.1 copy-start.17
  81.8 35.5 %collective-permute-start.15 = (bf16[64,96,128]{2,1,0:T(8,128)(2,1)}, bf16[64,96,128]{2,1,0:T(8,128)(2,1)}, u32[]{:S(2)}, u32[]{:S(2)}) collective-permute-start(bf16[64,96,128]{2,1,0:T(8,128)(2,1)} %get-tuple-element.63), channel_id=1, source_target_pairs={{0,2},{1,3},{2,0},{3,1},{64,66},{65,67},{66,64},{67,65},{4,6},{5,7... | collective-permute-start | bytes 4718600 | tf_op jit(solution)/shard_map/ppermute | solution.py:337
  83.1 3.4 %copy-start.1 = (bf16[128,256,128]{2,1,0:T(8,128)(2,1)S(1)}, bf16[128,256,128]{2,1,0:T(8,128)(2,1)}, u32[]{:S(2)}) copy-start(bf16[128,256,128]{2,1,0:T(8,128)(2,1)} %x_ref.5) | copy-start | bytes 25165828
  86.5 6.6 %copy-start.7 = (bf16[128,96,128]{2,1,0:T(8,128)(2,1)S(1)}, bf16[128,96,128]{2,1,0:T(8,128)(2,1)}, u32[]{:S(2)}) copy-start(bf16[128,96,128]{2,1,0:T(8,128)(2,1)} %copy-done.6) | copy-start | bytes 9437188
  86.5 6.6 %copy-start.16 = (bf16[64,96,128]{2,1,0:T(8,128)(2,1)S(1)}, bf16[64,96,128]{2,1,0:T(8,128)(2,1)}, u32[]{:S(2)}) copy-start(bf16[64,96,128]{2,1,0:T(8,128)(2,1)} %copy-done.15) | copy-start | bytes 4718596
  86.5 6.6 %copy-start.18 = (bf16[64,96,128]{2,1,0:T(8,128)(2,1)S(1)}, bf16[64,96,128]{2,1,0:T(8,128)(2,1)}, u32[]{:S(2)}) copy-start(bf16[64,96,128]{2,1,0:T(8,128)(2,1)} %copy-done.17) | copy-start | bytes 4718596
  86.5 12.5 %slice-start = ((s8[8388608]{0:T(1024)(128)(4,1)}), s8[4194304]{0:T(1024)(128)(4,1)S(1)}, s32[]{:S(2)}) async-start(s8[8388608]{0:T(1024)(128)(4,1)} %bitcast.1), calls=%async_computation | async-start | bytes 8388608
  93.0 5.9 %copy-start.4 = (bf16[128,128,128]{2,1,0:T(8,128)(2,1)}, bf16[128,128,128]{2,1,0:T(8,128)(2,1)S(1)}, u32[]{:S(2)}) copy-start(bf16[128,128,128]{2,1,0:T(8,128)(2,1)S(1)} %gate_values.2.refs_8_) | copy-start | bytes 12582916
  93.1 5.9 %slice-start.1 = ((s8[8388608]{0:T(1024)(128)(4,1)}), s8[4194304]{0:T(1024)(128)(4,1)S(1)}, s32[]{:S(2)}) async-start(s8[8388608]{0:T(1024)(128)(4,1)} %bitcast.1), calls=%async_computation.1 | async-start | bytes 8388608
  105.5 22.8 %copy-start.2 = (bf16[128,128,128]{2,1,0:T(8,128)(2,1)}, bf16[128,128,128]{2,1,0:T(8,128)(2,1)S(1)}, u32[]{:S(2)}) copy-start(bf16[128,128,128]{2,1,0:T(8,128)(2,1)S(1)} %gate_values.3.refs_8_) | copy-start | bytes 12582916
  105.6 53.2 %copy-start.10 = (bf16[64,96,128]{2,1,0:T(8,128)(2,1)S(1)}, bf16[64,96,128]{2,1,0:T(8,128)(2,1)}, u32[]{:S(2)}) copy-start(bf16[64,96,128]{2,1,0:T(8,128)(2,1)} %copy-done.9) | copy-start | bytes 4718596
  105.6 53.2 %copy-start.12 = (bf16[64,96,128]{2,1,0:T(8,128)(2,1)S(1)}, bf16[64,96,128]{2,1,0:T(8,128)(2,1)}, u32[]{:S(2)}) copy-start(bf16[64,96,128]{2,1,0:T(8,128)(2,1)} %copy-done.11) | copy-start | bytes 4718596
  105.6 53.2 %copy-start.24 = (bf16[128,128]{1,0:T(8,128)(2,1)S(1)}, bf16[128,128]{1,0:T(8,128)(2,1)}, u32[]{:S(2)}) copy-start(bf16[128,128]{1,0:T(8,128)(2,1)} %refs_9_.3) | copy-start | bytes 98308
  117.3 3.6 %collective-permute-start.22 = (bf16[64,96,128]{2,1,0:T(8,128)(2,1)}, bf16[64,96,128]{2,1,0:T(8,128)(2,1)S(1)}, u32[]{:S(2)}, u32[]{:S(2)}) collective-permute-start(bf16[64,96,128]{2,1,0:T(8,128)(2,1)} %collective-permute-done.15.c_ref), channel_id=1, source_target_pairs={{0,1},{1,0},{2,3},{3,2},{64,65},{65,64},{66,67},{67,66},{4,5},{5,4... | collective-permute-start | bytes 4718600 | tf_op jit(solution)/shard_map/ppermute | solution.py:344
  117.3 21.8 %collective-permute-start.25 = (bf16[64,96,128]{2,1,0:T(8,128)(2,1)}, bf16[64,96,128]{2,1,0:T(8,128)(2,1)S(1)}, u32[]{:S(2)}, u32[]{:S(2)}) collective-permute-start(bf16[64,96,128]{2,1,0:T(8,128)(2,1)} %collective-permute-done.23.refs_1_), channel_id=1, source_target_pairs={{0,4},{1,13},{2,6},{3,15},{64,68},{65,77},{66,70},{67,79},{4,8},{5... | collective-permute-start | bytes 4718600 | tf_op jit(solution)/shard_map/ppermute | solution.py:291
  118.9 21.9 %collective-permute-start.26 = (bf16[64,96,128]{2,1,0:T(8,128)(2,1)}, bf16[64,96,128]{2,1,0:T(8,128)(2,1)}, u32[]{:S(2)}, u32[]{:S(2)}) collective-permute-start(bf16[64,96,128]{2,1,0:T(8,128)(2,1)} %collective-permute-done.24.refs_5_), channel_id=1, source_target_pairs={{0,16},{1,49},{2,18},{3,51},{64,80},{65,113},{66,82},{67,115},{4,2... | collective-permute-start | bytes 4718600 | tf_op jit(solution)/shard_map/ppermute | solution.py:291
  119.3 36.7 %collective-permute-start.29 = (bf16[64,96,128]{2,1,0:T(8,128)(2,1)}, bf16[64,96,128]{2,1,0:T(8,128)(2,1)S(1)}, u32[]{:S(2)}, u32[]{:S(2)}) collective-permute-start(bf16[64,96,128]{2,1,0:T(8,128)(2,1)} %collective-permute-done.20.refs_2_), channel_id=1, source_target_pairs={{0,4},{1,13},{2,6},{3,15},{64,68},{65,77},{66,70},{67,79},{4,8},{5... | collective-permute-start | bytes 4718600 | tf_op jit(solution)/shard_map/ppermute | solution.py:291
  119.3 38.3 %collective-permute-start.30 = (bf16[64,96,128]{2,1,0:T(8,128)(2,1)}, bf16[64,96,128]{2,1,0:T(8,128)(2,1)S(1)}, u32[]{:S(2)}, u32[]{:S(2)}) collective-permute-start(bf16[64,96,128]{2,1,0:T(8,128)(2,1)} %collective-permute-done.21.refs_6_), channel_id=1, source_target_pairs={{0,16},{1,49},{2,18},{3,51},{64,80},{65,113},{66,82},{67,115},{4,2... | collective-permute-start | bytes 4718600 | tf_op jit(solution)/shard_map/ppermute | solution.py:291
  128.4 4.6 %copy-start = (bf16[128,128,384]{2,1,0:T(8,128)(2,1)}, bf16[128,128,384]{2,1,0:T(8,128)(2,1)S(1)}, u32[]{:S(2)}) copy-start(bf16[128,128,384]{2,1,0:T(8,128)(2,1)S(1)} %arrange_left.3.lx_ref.ly_ref) | copy-start | bytes 37748740
  140.8 39.9 %collective-permute-start.27 = (bf16[64,96,128]{2,1,0:T(8,128)(2,1)S(1)}, bf16[64,96,128]{2,1,0:T(8,128)(2,1)S(1)}, u32[]{:S(2)}, u32[]{:S(2)}) collective-permute-start(bf16[64,96,128]{2,1,0:T(8,128)(2,1)S(1)} %collective-permute-done.25.refs_2_), channel_id=1, source_target_pairs={{0,4},{1,13},{2,6},{3,15},{64,68},{65,77},{66,70},{67,79},{4,8},{5... | collective-permute-start | bytes 4718600 | tf_op jit(solution)/shard_map/ppermute | solution.py:291
  140.8 1.1 copy-start.19
  142.0 38.8 %collective-permute-start.28 = (bf16[64,96,128]{2,1,0:T(8,128)(2,1)}, bf16[64,96,128]{2,1,0:T(8,128)(2,1)S(1)}, u32[]{:S(2)}, u32[]{:S(2)}) collective-permute-start(bf16[64,96,128]{2,1,0:T(8,128)(2,1)} %collective-permute-done.26.refs_6_), channel_id=1, source_target_pairs={{0,16},{1,49},{2,18},{3,51},{64,80},{65,113},{66,82},{67,115},{4,2... | collective-permute-start | bytes 4718600 | tf_op jit(solution)/shard_map/ppermute | solution.py:291
  157.6 1.2 copy-start.13
  158.7 2.2 %copy-start.5 = (bf16[128,128,128]{2,1,0:T(8,128)(2,1)S(1)}, bf16[128,128,128]{2,1,0:T(8,128)(2,1)}, u32[]{:S(2)}) copy-start(bf16[128,128,128]{2,1,0:T(8,128)(2,1)} %copy-done.4) | copy-start | bytes 12582916
  160.9 1.4 copy-start.14
  162.3 18.4 %copy-start.3 = (bf16[128,128,128]{2,1,0:T(8,128)(2,1)S(1)}, bf16[128,128,128]{2,1,0:T(8,128)(2,1)}, u32[]{:S(2)}) copy-start(bf16[128,128,128]{2,1,0:T(8,128)(2,1)} %copy-done.2) | copy-start | bytes 12582916
  162.3 18.4 %copy-start.20 = (bf16[64,96,128]{2,1,0:T(8,128)(2,1)S(1)}, bf16[64,96,128]{2,1,0:T(8,128)(2,1)}, u32[]{:S(2)}) copy-start(bf16[64,96,128]{2,1,0:T(8,128)(2,1)} %copy-done.19) | copy-start | bytes 4718596

commit v4 on v3

--- a/solution.py
+++ b/solution.py
@@ -318,33 +318,31 @@
     halves_0 = project_right(blocks[0], after(others[0], left_local), right_proj, right_gate)
     f0 = [[half] for half in halves_0]
     step_on(f0, first_rings)
-    near_core = lax.ppermute(after(left_local, *others), AXES, SWAP_CORE)
-    far_0 = lax.ppermute(after(near[0], *others, *halves_0), AXES, SWAP_Z_LO)
     halves_1 = project_right(blocks[1], after(others[1], *halves_0), right_proj, right_gate)
+    near_core = lax.ppermute(after(left_local, *others, *halves_0), AXES, SWAP_CORE)
+    far_0 = lax.ppermute(after(near[0], *halves_1), AXES, SWAP_Z_LO)
     f1 = [[half] for half in halves_1]
     step_on(f1, first_rings)
-    step_on(f0, first_rings, near_core, *halves_1)
+    step_on(f0, first_rings, *halves_1)
     step_on(f1, first_rings, f0[0][1])
-    step_on(f0, first_rings, f1[0][1], f1[1][1])
+    step_on(f0, first_rings, f1[0][1], f1[1][1], near_core)
     step_on(f1, first_rings, f0[0][2], f0[1][2])
 
     c0 = joined(f0)
-    step_on(c0, second_rings, f1[0][2], f1[1][2])
+    step_on(c0, second_rings, f1[0][3], f1[1][3])
     c1 = joined(f1)
     step_on(c1, second_rings)
     step_on(c0, second_rings, far_0)
-    far_core_0 = lax.ppermute(after(far_0, f1[0][3], f1[1][3]), AXES, SWAP_CORE)
-    far_1 = lax.ppermute(after(near[1], far_core_0), AXES, SWAP_Z_LO)
-    gate_0 = gate_values(pair_gate, after(out_gate, c0[0][1], c0[1][1], far_core_0), 0, n_j)
+    far_core_0 = lax.ppermute(after(far_0, *[h[3] for h in f1]), AXES, SWAP_CORE)
+    far_1 = lax.ppermute(after(near[1], far_0), AXES, SWAP_Z_LO)
+    gate_0 = gate_values(pair_gate, after(out_gate, c0[0][1], c0[1][1]), 0, n_j)
     orders = left_orders()
     left = arrange_left(left_local, near_core, far_0, far_core_0, after(orders, gate_0), 0)
-    gate_1 = gate_values(pair_gate, after(out_gate, left, c1[0][1], c1[1][1]), 1, n_j)
+    gate_1 = gate_values(pair_gate, after(out_gate, gate_0, c1[0][1], c1[1][1]), 1, n_j)
     step_on(c1, second_rings, gate_1)
-    step_on(c0, second_rings, gate_1)
+    step_on(c0, second_rings)
     far_core_1 = lax.ppermute(after(far_1, c0[0][2], c0[1][2]), AXES, SWAP_CORE)
-    left = arrange_left(
-        left_local, near_core, far_1, far_core_1, after(orders, c0[0][2], c0[1][2]), 1, left
-    )
+    left = arrange_left(left_local, near_core, far_1, far_core_1, after(orders, c0[0][2], c0[1][2]), 1, left)
     step_on(c1, second_rings, left)
     whole = update_block(left, *c0, gate_0, out_proj, 0, n_blocks, 0, 1)
     return update_block(left, *c1, gate_1, out_proj, 1, n_blocks, 0, 1, whole)

time: 199 us -> 197 us (0.990)
  local copies, waits for them, and re-layouts: 28.1 us -> 22.3 us
  waiting for transfers between devices: 71.2 us -> 68.1 us
  starting transfers between devices: 24 us -> 26.9 us
  Pallas kernels: 74.9 us -> 77.8 us
    ppermute x24, waiting for transfers between devices: 55.3 us -> 43 us  [step_on(): held.append(lax.ppermute(piece, AXES, ring))]
    ppermute x4, waiting for transfers between devices: 8.34 us -> 20 us  [the longest x1 14.8 us: shards(): far_0 = lax.ppermute(after(near[0], *halves_1), AXES, SWAP_Z_LO)]
    pallas_call x2, Pallas kernels: 13.3 us -> 16.7 us  [arrange_left(): pl.pallas_call(arrange_kernel, grid=(steps,), in_specs=in_specs, out_spec...]
    ppermute x24, starting transfers between devices: 17.1 us -> 20.2 us  [step_on(): held.append(lax.ppermute(piece, AXES, ring))]
    unnamed x70 -> x80, local copies, waits for them, and re-layouts: 23.7 us -> 20.7 us
  transfers between devices with their start and end apart: 31 -> 31, of which waited for: 22 -> 18; matrix products, arithmetic and copies ran while one was open for 5% -> 1% of each run, Pallas kernels for 28% -> 30%
where the time goes in v4:
time: 197 us; the launch traced here: 196 us
  Pallas kernels  77.8 us (39%)
  waiting for transfers between devices  68.1 us (35%)
  starting transfers between devices  26.9 us (14%)
  local copies, waits for them, and re-layouts  22.3 us (11%)
    ppermute x24, waiting for transfers between devices, step_on(): held.append(lax.ppermute(piece, AXES, ring))  43 us
    pallas_call x2, Pallas kernels, update_block(): pl.pallas_call(functools.partial(update_kernel, n_sum), grid=(n_sum + n_o...  36.2 us
    unnamed x80, local copies, waits for them, and re-layouts  20.7 us
    ppermute x24, starting transfers between devices, step_on(): held.append(lax.ppermute(piece, AXES, ring))  20.2 us
    pallas_call x2, Pallas kernels, arrange_left(): pl.pallas_call(arrange_kernel, grid=(steps,), in_specs=in_specs, out_spec...  16.7 us
    ppermute x1, waiting for transfers between devices, shards(): far_0 = lax.ppermute(after(near[0], *halves_1), AXES, SWAP_Z_LO)  14.8 us
    pallas_call x2, Pallas kernels, gate_values(): pl.pallas_call(gate_kernel, grid=(n_i // block,), in_specs=[pl.BlockSpec(...  13.1 us
    pallas_call x1, Pallas kernels, project_left(): pl.pallas_call(left_kernel, grid=(n_k // block,), in_specs=[pl.BlockSpec(...  8.93 us
  transfers between devices with their start and end apart: 31, of which 18 were waited for; matrix products, arithmetic and copies ran while one was open for 1% of the time, Pallas kernels for 30%

profile of v4, /device:TPU:0, one launch (start us, length us, event | category | flops | bytes accessed | tf_op | source)
XLA Modules:
  0.0 196.1 jit_solution(16913125826254767929)
XLA Ops:
  0.0 1.2 fusion.45
  1.2 4.0 %collective-permute-start = (bf16[12,128,128]{2,1,0:T(8,128)(2,1)S(1)}, bf16[12,128,128]{2,1,0:T(8,128)(2,1)S(1)}, u32[]{:S(2)}, u32[]{:S(2)}) collective-permute-start(bf16[12,128,128]{2,1,0:T(8,128)(2,1)S(1)} %get-tuple-element.86.own_ref), channel_id=1, source_target_pairs={{0,64},{1,65},{2,66},{3,67},{64,0},{65,1},{66,2},{67,3},{4,68},{5,... | collective-permute-start | bytes 1179656 | tf_op jit(solution)/shard_map/ppermute | solution.py:315
  5.3 1.9 copy-done.7
  7.2 8.9 %project_left.1.a_ref = bf16[128,96,128]{2,1,0:T(8,128)(2,1)S(1)} custom-call(bf16[128,96,128]{2,1,0:T(8,128)(2,1)S(1)} %copy-done.7, bf16[128,128]{1,0:T(8,128)(2,1)S(1)} %copy-done.30, bf16[128,128]{1,0:T(8,128)(2,1)S(1)} %copy-done.31), custom_call_target="tpu_custom_call" | custom-call | flops 805306368 | bytes 12582912 | tf_op jit(solution)/shard_map/project_left/pallas_call | solution.py:80
  16.2 1.4 project_right.2
  17.6 5.1 %collective-permute-done.1.other_ref = bf16[12,128,128]{2,1,0:T(8,128)(2,1)S(1)} collective-permute-done((bf16[12,128,128]{2,1,0:T(8,128)(2,1)S(1)}, bf16[12,128,128]{2,1,0:T(8,128)(2,1)S(1)}, u32[]{:S(2)}, u32[]{:S(2)}) %collective-permute-start.1) | collective-permute-done | bytes 393248 | tf_op jit(solution)/shard_map/ppermute | solution.py:315
  22.8 1.5 collective-permute-start.5
  24.3 1.6 collective-permute-start.6
  25.9 1.4 project_right.3
  27.3 1.6 collective-permute-start.9
  28.8 1.6 collective-permute-start.10
  30.4 1.4 collective-permute-done.5
  31.8 1.5 collective-permute-done.6
  33.3 1.5 collective-permute-start.7
  34.8 0.4 collective-permute-start.8
  35.1 0.2 fusion.44
  35.3 1.0 collective-permute-done.9
  36.3 1.5 collective-permute-done.10
  37.8 1.2 collective-permute-start.13
  39.0 0.4 collective-permute-start.14
  39.5 2.8 %collective-permute-done.7 = bf16[64,24,128]{2,1,0:T(8,128)(2,1)S(1)} collective-permute-done((bf16[64,24,128]{2,1,0:T(8,128)(2,1)S(1)}, bf16[64,24,128]{2,1,0:T(8,128)(2,1)S(1)}, u32[]{:S(2)}, u32[]{:S(2)}) %collective-permute-start.7) | collective-permute-done | bytes 393248 | tf_op jit(solution)/shard_map/ppermute | solution.py:291
  42.3 1.3 collective-permute-start.3
  43.5 0.2 collective-permute-done.8
  43.8 1.6 copy-done.5
  45.4 1.2 collective-permute-start.11
  46.8 1.2 collective-permute-done.14
  48.0 1.1 collective-permute-start.15
  49.3 5.0 %collective-permute-done.11 = bf16[64,24,128]{2,1,0:T(8,128)(2,1)S(1)} collective-permute-done((bf16[64,24,128]{2,1,0:T(8,128)(2,1)S(1)}, bf16[64,24,128]{2,1,0:T(8,128)(2,1)S(1)}, u32[]{:S(2)}, u32[]{:S(2)}) %collective-permute-start.11) | collective-permute-done | bytes 393248 | tf_op jit(solution)/shard_map/ppermute | solution.py:291
  54.5 1.3 collective-permute-done.12
  55.8 2.8 %collective-permute-done.15 = bf16[64,24,128]{2,1,0:T(8,128)(2,1)S(1)} collective-permute-done((bf16[64,24,128]{2,1,0:T(8,128)(2,1)S(1)}, bf16[64,24,128]{2,1,0:T(8,128)(2,1)S(1)}, u32[]{:S(2)}, u32[]{:S(2)}) %collective-permute-start.15) | collective-permute-done | bytes 393248 | tf_op jit(solution)/shard_map/ppermute | solution.py:291
  58.6 1.3 collective-permute-done.16
  59.9 0.5 collective-permute-start.18
  61.1 0.6 collective-permute-start.23
  61.6 1.2 collective-permute-start.24
  62.9 14.8 %collective-permute-done.3.c_ref = bf16[64,96,128]{2,1,0:T(8,128)(2,1)} collective-permute-done((bf16[64,96,128]{2,1,0:T(8,128)(2,1)S(1)}, bf16[64,96,128]{2,1,0:T(8,128)(2,1)}, u32[]{:S(2)}, u32[]{:S(2)}) %collective-permute-start.3) | collective-permute-done | bytes 1572896 | tf_op jit(solution)/shard_map/ppermute | solution.py:323
  77.7 1.3 collective-permute-start.4
  79.0 2.6 %collective-permute-done.17.refs_1_ = bf16[64,96,128]{2,1,0:T(8,128)(2,1)S(1)} collective-permute-done((bf16[64,96,128]{2,1,0:T(8,128)(2,1)S(1)}, bf16[64,96,128]{2,1,0:T(8,128)(2,1)S(1)}, u32[]{:S(2)}, u32[]{:S(2)}) %collective-permute-start.17) | collective-permute-done | bytes 1572896 | tf_op jit(solution)/shard_map/ppermute | solution.py:291
  81.6 0.4 collective-permute-start.19
  82.0 0.2 collective-permute-start.20
  82.2 6.5 %gate_values.2.refs_8_ = bf16[128,128,128]{2,1,0:T(8,128)(2,1)S(1)} custom-call(bf16[128,256,128]{2,1,0:T(8,128)(2,1)S(1)} %bitcast.2, bf16[128,128]{1,0:T(8,128)(2,1)S(1)} %copy-done.26), custom_call_target="tpu_custom_call" | custom-call | flops 1000 | bytes 1000 | tf_op jit(solution)/shard_map/gate_values/pallas_call | solution.py:140
  88.8 2.0 %copy-done.3 = bf16[128,128,128]{2,1,0:T(8,128)(2,1)} copy-done((bf16[128,128,128]{2,1,0:T(8,128)(2,1)}, bf16[128,128,128]{2,1,0:T(8,128)(2,1)S(1)}, u32[]{:S(2)}) %copy-start.3) | copy-done | bytes 4194328
  90.8 7.7 %collective-permute-done.23.refs_1_ = bf16[64,96,128]{2,1,0:T(8,128)(2,1)} collective-permute-done((bf16[64,96,128]{2,1,0:T(8,128)(2,1)S(1)}, bf16[64,96,128]{2,1,0:T(8,128)(2,1)}, u32[]{:S(2)}, u32[]{:S(2)}) %collective-permute-start.23) | collective-permute-done | bytes 1572896 | tf_op jit(solution)/shard_map/ppermute | solution.py:291
  98.5 6.5 %gate_values.3.refs_8_ = bf16[128,128,128]{2,1,0:T(8,128)(2,1)S(1)} custom-call(bf16[128,256,128]{2,1,0:T(8,128)(2,1)S(1)} %bitcast.2, bf16[128,128]{1,0:T(8,128)(2,1)S(1)} %copy-done.26), custom_call_target="tpu_custom_call" | custom-call | flops 1000 | bytes 1000 | tf_op jit(solution)/shard_map/gate_values/pallas_call | solution.py:140
  105.1 1.9 copy-done.1
  107.0 5.2 %collective-permute-done.4.c_ref = bf16[64,96,128]{2,1,0:T(8,128)(2,1)} collective-permute-done((bf16[64,96,128]{2,1,0:T(8,128)(2,1)S(1)}, bf16[64,96,128]{2,1,0:T(8,128)(2,1)}, u32[]{:S(2)}, u32[]{:S(2)}) %collective-permute-start.4) | collective-permute-done | bytes 1572896 | tf_op jit(solution)/shard_map/ppermute | solution.py:337
  112.2 3.0 %collective-permute-done.19.refs_2_ = bf16[64,96,128]{2,1,0:T(8,128)(2,1)S(1)} collective-permute-done((bf16[64,96,128]{2,1,0:T(8,128)(2,1)S(1)}, bf16[64,96,128]{2,1,0:T(8,128)(2,1)S(1)}, u32[]{:S(2)}, u32[]{:S(2)}) %collective-permute-start.19) | collective-permute-done | bytes 1572896 | tf_op jit(solution)/shard_map/ppermute | solution.py:291
  115.3 1.1 copy-done.20
  116.4 1.1 copy-done.23
  117.5 0.5 collective-permute-start.26
  118.1 0.3 fusion
  118.3 0.1 add_convert_fusion.order_ref
  118.5 1.9 copy-done.6
  120.4 8.1 %arrange_left.2.rest_0_ = bf16[128,128,384]{2,1,0:T(8,128)(2,1)S(1)} custom-call(bf16[128,96,128]{2,1,0:T(8,128)(2,1)S(1)} %project_left.1.a_ref, bf16[128,96,128]{2,1,0:T(8,128)(2,1)S(1)} %copy-done.6, bf16[64,96,128]{2,1,0:T(8,128)(2,1)} %collective-permute-done.3.c_ref, bf16[64,96,128]{2,1,0:T(8,128)(2,1)} %collective-permute-done.22.d_ref, ...), custom_call_target="tpu_custom_call" | custom-call | flops 1000 | bytes 1000 | tf_op jit(solution)/shard_map/arrange_left/pallas_call | solution.py:181
  128.5 0.1 collective-permute-start.29
  128.7 1.5 collective-permute-start.30
  130.2 8.7 %arrange_left.3.lx_ref.ly_ref = bf16[128,128,384]{2,1,0:T(8,128)(2,1)S(1)} custom-call(bf16[128,96,128]{2,1,0:T(8,128)(2,1)S(1)} %project_left.1.a_ref, bf16[128,96,128]{2,1,0:T(8,128)(2,1)S(1)} %copy-done.6, bf16[64,96,128]{2,1,0:T(8,128)(2,1)} %collective-permute-done.4.c_ref, ...), custom_call_target="tpu_custom_call", output_to_operand_aliasing={{}: (5, {})} | custom-call | flops 1000 | bytes 1000 | tf_op jit(solution)/shard_map/arrange_left/pallas_call | solution.py:181
  138.9 4.6 %copy-done = bf16[128,128,384]{2,1,0:T(8,128)(2,1)} copy-done((bf16[128,128,384]{2,1,0:T(8,128)(2,1)}, bf16[128,128,384]{2,1,0:T(8,128)(2,1)S(1)}, u32[]{:S(2)}) %copy-start) | copy-done | bytes 12582936
  143.5 1.6 collective-permute-start.27
  145.0 1.5 collective-permute-start.28
  146.5 9.7 %collective-permute-done.29.refs_3_ = bf16[64,96,128]{2,1,0:T(8,128)(2,1)S(1)} collective-permute-done((bf16[64,96,128]{2,1,0:T(8,128)(2,1)S(1)}, bf16[64,96,128]{2,1,0:T(8,128)(2,1)S(1)}, u32[]{:S(2)}, u32[]{:S(2)}) %collective-permute-start.29) | collective-permute-done | bytes 1572896 | tf_op jit(solution)/shard_map/ppermute | solution.py:291
  156.3 2.2 %copy-done.4 = bf16[128,128,128]{2,1,0:T(8,128)(2,1)S(1)} copy-done((bf16[128,128,128]{2,1,0:T(8,128)(2,1)S(1)}, bf16[128,128,128]{2,1,0:T(8,128)(2,1)}, u32[]{:S(2)}) %copy-start.4) | copy-done | bytes 4194328
  158.5 17.8 %update_block.2.refs_10_ = bf16[128,256,128]{2,1,0:T(8,128)(2,1)} custom-call(bf16[128,128,384]{2,1,0:T(8,128)(2,1)} %copy-done, bf16[128,128,384]{2,1,0:T(8,128)(2,1)} %copy-done, bf16[64,96,128]{2,1,0:T(8,128)(2,1)S(1)} %copy-done.11, bf16[64,96,128]{2,1,0:T(8,128)(2,1)S(1)} %copy-done.17, bf16[64,96,128]{2,1,0:T(8,128)(2,1)S(1)} %copy-done.22, ...), custom_call_target="tpu_custom_call" | custom-call | flops 1000 | bytes 1000 | tf_op jit(solution)/shard_map/update_block/pallas_call | solution.py:270
  176.3 1.4 copy-done.15
  177.7 18.3 %update_block.3 = bf16[128,256,128]{2,1,0:T(8,128)(2,1)} custom-call(bf16[128,128,384]{2,1,0:T(8,128)(2,1)} %copy-done, bf16[128,128,384]{2,1,0:T(8,128)(2,1)} %copy-done, bf16[64,96,128]{2,1,0:T(8,128)(2,1)S(1)} %copy-done.15, bf16[64,96,128]{2,1,0:T(8,128)(2,1)} %collective-permute-done.23.refs_1_, ...), custom_call_target="tpu_custom_call", output_to_operand_aliasing={{}: (12, {})} | custom-call | flops 1000 | bytes 1000 | tf_op jit(solution)/shard_map/update_block/pallas_call | solution.py:270
  (102 shorter events, 1.5 us)
Async XLA Ops:
  0.0 5.3 %copy-start.30 = (bf16[128,128]{1,0:T(8,128)(2,1)S(1)}, bf16[128,128]{1,0:T(8,128)(2,1)}, u32[]{:S(2)}) copy-start(bf16[128,128]{1,0:T(8,128)(2,1)} %proj_ref.3) | copy-start | bytes 98308
  0.0 5.3 %copy-start.31 = (bf16[128,128]{1,0:T(8,128)(2,1)S(1)}, bf16[128,128]{1,0:T(8,128)(2,1)}, u32[]{:S(2)}) copy-start(bf16[128,128]{1,0:T(8,128)(2,1)} %gate_ref.3) | copy-start | bytes 98308
  1.2 15.0 %collective-permute-start = (bf16[12,128,128]{2,1,0:T(8,128)(2,1)S(1)}, bf16[12,128,128]{2,1,0:T(8,128)(2,1)S(1)}, u32[]{:S(2)}, u32[]{:S(2)}) collective-permute-start(bf16[12,128,128]{2,1,0:T(8,128)(2,1)S(1)} %get-tuple-element.86.own_ref), channel_id=1, source_target_pairs={{0,64},{1,65},{2,66},{3,67},{64,0},{65,1},{66,2},{67,3},{4,68},{5,... | collective-permute-start | bytes 1179656 | tf_op jit(solution)/shard_map/ppermute | solution.py:315
  5.2 17.5 %collective-permute-start.1 = (bf16[12,128,128]{2,1,0:T(8,128)(2,1)S(1)}, bf16[12,128,128]{2,1,0:T(8,128)(2,1)S(1)}, u32[]{:S(2)}, u32[]{:S(2)}) collective-permute-start(bf16[12,128,128]{2,1,0:T(8,128)(2,1)S(1)} %get-tuple-element.85.own_ref), channel_id=1, source_target_pairs={{0,64},{1,65},{2,66},{3,67},{64,0},{65,1},{66,2},{67,3},{4,68},{5,... | collective-permute-start | bytes 1179656 | tf_op jit(solution)/shard_map/ppermute | solution.py:315
  5.3 1.9 copy-start.7
  7.2 9.0 %copy-start.27 = (bf16[128,128]{1,0:T(8,128)(2,1)S(1)}, bf16[128,128]{1,0:T(8,128)(2,1)}, u32[]{:S(2)}) copy-start(bf16[128,128]{1,0:T(8,128)(2,1)} %proj_ref.5) | copy-start | bytes 98308
  7.2 9.0 %copy-start.28 = (bf16[128,128]{1,0:T(8,128)(2,1)S(1)}, bf16[128,128]{1,0:T(8,128)(2,1)}, u32[]{:S(2)}) copy-start(bf16[128,128]{1,0:T(8,128)(2,1)} %gate_ref.5) | copy-start | bytes 98308
  22.8 21.0 %collective-permute-start.2 = (bf16[128,96,128]{2,1,0:T(8,128)(2,1)S(1)}, bf16[128,96,128]{2,1,0:T(8,128)(2,1)S(1)}, u32[]{:S(2)}, u32[]{:S(2)}) collective-permute-start(bf16[128,96,128]{2,1,0:T(8,128)(2,1)S(1)} %project_left.1.a_ref), channel_id=1, source_target_pairs={{0,1},{1,0},{2,3},{3,2},{64,65},{65,64},{66,67},{67,66},{4,5},{5,4... | collective-permute-start | bytes 9437192 | tf_op jit(solution)/shard_map/ppermute | solution.py:322
  22.8 9.0 %collective-permute-start.5 = (bf16[64,24,128]{2,1,0:T(8,128)(2,1)S(1)}, bf16[64,24,128]{2,1,0:T(8,128)(2,1)S(1)}, u32[]{:S(2)}, u32[]{:S(2)}) collective-permute-start(bf16[64,24,128]{2,1,0:T(8,128)(2,1)S(1)} %get-tuple-element.45), channel_id=1, source_target_pairs={{0,16},{1,49},{2,18},{3,51},{64,80},{65,113},{66,82},{67,115},{4,2... | collective-permute-start | bytes 1179656 | tf_op jit(solution)/shard_map/ppermute | solution.py:291
  24.3 9.0 %collective-permute-start.6 = (bf16[64,24,128]{2,1,0:T(8,128)(2,1)S(1)}, bf16[64,24,128]{2,1,0:T(8,128)(2,1)S(1)}, u32[]{:S(2)}, u32[]{:S(2)}) collective-permute-start(bf16[64,24,128]{2,1,0:T(8,128)(2,1)S(1)} %get-tuple-element.46), channel_id=1, source_target_pairs={{0,4},{1,13},{2,6},{3,15},{64,68},{65,77},{66,70},{67,79},{4,8},{5... | collective-permute-start | bytes 1179656 | tf_op jit(solution)/shard_map/ppermute | solution.py:291
  27.3 9.1 %collective-permute-start.9 = (bf16[64,24,128]{2,1,0:T(8,128)(2,1)S(1)}, bf16[64,24,128]{2,1,0:T(8,128)(2,1)S(1)}, u32[]{:S(2)}, u32[]{:S(2)}) collective-permute-start(bf16[64,24,128]{2,1,0:T(8,128)(2,1)S(1)} %get-tuple-element.49), channel_id=1, source_target_pairs={{0,16},{1,49},{2,18},{3,51},{64,80},{65,113},{66,82},{67,115},{4,2... | collective-permute-start | bytes 1179656 | tf_op jit(solution)/shard_map/ppermute | solution.py:291
  28.8 9.0 %collective-permute-start.10 = (bf16[64,24,128]{2,1,0:T(8,128)(2,1)S(1)}, bf16[64,24,128]{2,1,0:T(8,128)(2,1)S(1)}, u32[]{:S(2)}, u32[]{:S(2)}) collective-permute-start(bf16[64,24,128]{2,1,0:T(8,128)(2,1)S(1)} %get-tuple-element.50), channel_id=1, source_target_pairs={{0,4},{1,13},{2,6},{3,15},{64,68},{65,77},{66,70},{67,79},{4,8},{5... | collective-permute-start | bytes 1179656 | tf_op jit(solution)/shard_map/ppermute | solution.py:291
  33.3 9.0 %collective-permute-start.7 = (bf16[64,24,128]{2,1,0:T(8,128)(2,1)S(1)}, bf16[64,24,128]{2,1,0:T(8,128)(2,1)S(1)}, u32[]{:S(2)}, u32[]{:S(2)}) collective-permute-start(bf16[64,24,128]{2,1,0:T(8,128)(2,1)S(1)} %collective-permute-done.5), channel_id=1, source_target_pairs={{0,16},{1,49},{2,18},{3,51},{64,80},{65,113},{66,82},{67,115},{4,2... | collective-permute-start | bytes 1179656 | tf_op jit(solution)/shard_map/ppermute | solution.py:291
  34.8 9.0 %collective-permute-start.8 = (bf16[64,24,128]{2,1,0:T(8,128)(2,1)S(1)}, bf16[64,24,128]{2,1,0:T(8,128)(2,1)S(1)}, u32[]{:S(2)}, u32[]{:S(2)}) collective-permute-start(bf16[64,24,128]{2,1,0:T(8,128)(2,1)S(1)} %collective-permute-done.6), channel_id=1, source_target_pairs={{0,4},{1,13},{2,6},{3,15},{64,68},{65,77},{66,70},{67,79},{4,8},{5... | collective-permute-start | bytes 1179656 | tf_op jit(solution)/shard_map/ppermute | solution.py:291
  35.1 47.1 %slice-start = ((s8[8388608]{0:T(1024)(128)(4,1)}), s8[4194304]{0:T(1024)(128)(4,1)S(1)}, s32[]{:S(2)}) async-start(s8[8388608]{0:T(1024)(128)(4,1)} %bitcast.1), calls=%async_computation | async-start | bytes 8388608
  37.8 9.0 %collective-permute-start.13 = (bf16[64,24,128]{2,1,0:T(8,128)(2,1)S(1)}, bf16[64,24,128]{2,1,0:T(8,128)(2,1)S(1)}, u32[]{:S(2)}, u32[]{:S(2)}) collective-permute-start(bf16[64,24,128]{2,1,0:T(8,128)(2,1)S(1)} %collective-permute-done.9), channel_id=1, source_target_pairs={{0,16},{1,49},{2,18},{3,51},{64,80},{65,113},{66,82},{67,115},{4,2... | collective-permute-start | bytes 1179656 | tf_op jit(solution)/shard_map/ppermute | solution.py:291
  39.0 9.0 %collective-permute-start.14 = (bf16[64,24,128]{2,1,0:T(8,128)(2,1)S(1)}, bf16[64,24,128]{2,1,0:T(8,128)(2,1)S(1)}, u32[]{:S(2)}, u32[]{:S(2)}) collective-permute-start(bf16[64,24,128]{2,1,0:T(8,128)(2,1)S(1)} %collective-permute-done.10), channel_id=1, source_target_pairs={{0,4},{1,13},{2,6},{3,15},{64,68},{65,77},{66,70},{67,79},{4,8},{5... | collective-permute-start | bytes 1179656 | tf_op jit(solution)/shard_map/ppermute | solution.py:291
  42.3 35.4 %collective-permute-start.3 = (bf16[64,96,128]{2,1,0:T(8,128)(2,1)S(1)}, bf16[64,96,128]{2,1,0:T(8,128)(2,1)}, u32[]{:S(2)}, u32[]{:S(2)}) collective-permute-start(bf16[64,96,128]{2,1,0:T(8,128)(2,1)S(1)} %get-tuple-element.51), channel_id=1, source_target_pairs={{0,2},{1,3},{2,0},{3,1},{64,66},{65,67},{66,64},{67,65},{4,6},{5,7... | collective-permute-start | bytes 4718600 | tf_op jit(solution)/shard_map/ppermute | solution.py:323
  43.7 1.6 copy-start.5
  45.4 9.0 %collective-permute-start.11 = (bf16[64,24,128]{2,1,0:T(8,128)(2,1)S(1)}, bf16[64,24,128]{2,1,0:T(8,128)(2,1)S(1)}, u32[]{:S(2)}, u32[]{:S(2)}) collective-permute-start(bf16[64,24,128]{2,1,0:T(8,128)(2,1)S(1)} %collective-permute-done.7), channel_id=1, source_target_pairs={{0,16},{1,49},{2,18},{3,51},{64,80},{65,113},{66,82},{67,115},{4,2... | collective-permute-start | bytes 1179656 | tf_op jit(solution)/shard_map/ppermute | solution.py:291
  46.7 9.1 %collective-permute-start.12 = (bf16[64,24,128]{2,1,0:T(8,128)(2,1)S(1)}, bf16[64,24,128]{2,1,0:T(8,128)(2,1)S(1)}, u32[]{:S(2)}, u32[]{:S(2)}) collective-permute-start(bf16[64,24,128]{2,1,0:T(8,128)(2,1)S(1)} %collective-permute-done.8), channel_id=1, source_target_pairs={{0,4},{1,13},{2,6},{3,15},{64,68},{65,77},{66,70},{67,79},{4,8},{5... | collective-permute-start | bytes 1179656 | tf_op jit(solution)/shard_map/ppermute | solution.py:291
  46.8 35.4 %slice-start.1 = ((s8[8388608]{0:T(1024)(128)(4,1)}), s8[4194304]{0:T(1024)(128)(4,1)S(1)}, s32[]{:S(2)}) async-start(s8[8388608]{0:T(1024)(128)(4,1)} %bitcast.1), calls=%async_computation.1 | async-start | bytes 8388608
  48.0 10.6 %collective-permute-start.15 = (bf16[64,24,128]{2,1,0:T(8,128)(2,1)S(1)}, bf16[64,24,128]{2,1,0:T(8,128)(2,1)S(1)}, u32[]{:S(2)}, u32[]{:S(2)}) collective-permute-start(bf16[64,24,128]{2,1,0:T(8,128)(2,1)S(1)} %collective-permute-done.13), channel_id=1, source_target_pairs={{0,16},{1,49},{2,18},{3,51},{64,80},{65,113},{66,82},{67,115},{4,2... | collective-permute-start | bytes 1179656 | tf_op jit(solution)/shard_map/ppermute | solution.py:291
  49.2 10.8 %collective-permute-start.16 = (bf16[64,24,128]{2,1,0:T(8,128)(2,1)S(1)}, bf16[64,24,128]{2,1,0:T(8,128)(2,1)S(1)}, u32[]{:S(2)}, u32[]{:S(2)}) collective-permute-start(bf16[64,24,128]{2,1,0:T(8,128)(2,1)S(1)} %collective-permute-done.14), channel_id=1, source_target_pairs={{0,4},{1,13},{2,6},{3,15},{64,68},{65,77},{66,70},{67,79},{4,8},{5... | collective-permute-start | bytes 1179656 | tf_op jit(solution)/shard_map/ppermute | solution.py:291
  54.4 6.1 %copy-start.10 = (bf16[64,96,128]{2,1,0:T(8,128)(2,1)}, bf16[64,96,128]{2,1,0:T(8,128)(2,1)S(1)}, u32[]{:S(2)}) copy-start(bf16[64,96,128]{2,1,0:T(8,128)(2,1)S(1)} %constant_dynamic-update-slice_fusion.refs_0_) | copy-start | bytes 4718596
  55.8 4.9 %copy-start.8 = (bf16[64,96,128]{2,1,0:T(8,128)(2,1)}, bf16[64,96,128]{2,1,0:T(8,128)(2,1)S(1)}, u32[]{:S(2)}) copy-start(bf16[64,96,128]{2,1,0:T(8,128)(2,1)S(1)} %constant_dynamic-update-slice_fusion.4.refs_4_) | copy-start | bytes 4718596
  59.9 21.6 %collective-permute-start.17 = (bf16[64,96,128]{2,1,0:T(8,128)(2,1)S(1)}, bf16[64,96,128]{2,1,0:T(8,128)(2,1)S(1)}, u32[]{:S(2)}, u32[]{:S(2)}) collective-permute-start(bf16[64,96,128]{2,1,0:T(8,128)(2,1)S(1)} %constant_dynamic-update-slice_fusion.refs_0_), channel_id=1, source_target_pairs={{0,4},{1,13},{2,6},{3,15},{64,68},{65,77},{66,70},{67,79},{4,8},{5... | collective-permute-start | bytes 4718600 | tf_op jit(solution)/shard_map/ppermute | solution.py:291
  59.9 21.6 %collective-permute-start.18 = (bf16[64,96,128]{2,1,0:T(8,128)(2,1)S(1)}, bf16[64,96,128]{2,1,0:T(8,128)(2,1)S(1)}, u32[]{:S(2)}, u32[]{:S(2)}) collective-permute-start(bf16[64,96,128]{2,1,0:T(8,128)(2,1)S(1)} %constant_dynamic-update-slice_fusion.4.refs_4_), channel_id=1, source_target_pairs={{0,16},{1,49},{2,18},{3,51},{64,80},{65,113},{66,82},{67,115},{4,2... | collective-permute-start | bytes 4718600 | tf_op jit(solution)/shard_map/ppermute | solution.py:291
  60.7 21.5 %copy-start.26 = (bf16[128,128]{1,0:T(8,128)(2,1)S(1)}, bf16[128,128]{1,0:T(8,128)(2,1)}, u32[]{:S(2)}) copy-start(bf16[128,128]{1,0:T(8,128)(2,1)} %w_ref.1) | copy-start | bytes 98308
  61.0 27.8 %copy-start.14 = (bf16[64,96,128]{2,1,0:T(8,128)(2,1)}, bf16[64,96,128]{2,1,0:T(8,128)(2,1)S(1)}, u32[]{:S(2)}) copy-start(bf16[64,96,128]{2,1,0:T(8,128)(2,1)S(1)} %constant_dynamic-update-slice_fusion.8.refs_0_) | copy-start | bytes 4718596
  61.0 27.7 %copy-start.12 = (bf16[64,96,128]{2,1,0:T(8,128)(2,1)}, bf16[64,96,128]{2,1,0:T(8,128)(2,1)S(1)}, u32[]{:S(2)}) copy-start(bf16[64,96,128]{2,1,0:T(8,128)(2,1)S(1)} %constant_dynamic-update-slice_fusion.12.refs_4_) | copy-start | bytes 4718596
  61.1 37.5 %collective-permute-start.23 = (bf16[64,96,128]{2,1,0:T(8,128)(2,1)S(1)}, bf16[64,96,128]{2,1,0:T(8,128)(2,1)}, u32[]{:S(2)}, u32[]{:S(2)}) collective-permute-start(bf16[64,96,128]{2,1,0:T(8,128)(2,1)S(1)} %constant_dynamic-update-slice_fusion.8.refs_0_), channel_id=1, source_target_pairs={{0,4},{1,13},{2,6},{3,15},{64,68},{65,77},{66,70},{67,79},{4,8},{5... | collective-permute-start | bytes 4718600 | tf_op jit(solution)/shard_map/ppermute | solution.py:291
  61.6 36.9 %collective-permute-start.24 = (bf16[64,96,128]{2,1,0:T(8,128)(2,1)S(1)}, bf16[64,96,128]{2,1,0:T(8,128)(2,1)}, u32[]{:S(2)}, u32[]{:S(2)}) collective-permute-start(bf16[64,96,128]{2,1,0:T(8,128)(2,1)S(1)} %constant_dynamic-update-slice_fusion.12.refs_4_), channel_id=1, source_target_pairs={{0,16},{1,49},{2,18},{3,51},{64,80},{65,113},{66,82},{67,115},{4,2... | collective-permute-start | bytes 4718600 | tf_op jit(solution)/shard_map/ppermute | solution.py:291
  77.7 34.5 %collective-permute-start.4 = (bf16[64,96,128]{2,1,0:T(8,128)(2,1)S(1)}, bf16[64,96,128]{2,1,0:T(8,128)(2,1)}, u32[]{:S(2)}, u32[]{:S(2)}) collective-permute-start(bf16[64,96,128]{2,1,0:T(8,128)(2,1)S(1)} %get-tuple-element.52), channel_id=1, source_target_pairs={{0,2},{1,3},{2,0},{3,1},{64,66},{65,67},{66,64},{67,65},{4,6},{5,7... | collective-permute-start | bytes 4718600 | tf_op jit(solution)/shard_map/ppermute | solution.py:337
  81.6 7.2 %copy-start.16 = (bf16[64,96,128]{2,1,0:T(8,128)(2,1)}, bf16[64,96,128]{2,1,0:T(8,128)(2,1)S(1)}, u32[]{:S(2)}) copy-start(bf16[64,96,128]{2,1,0:T(8,128)(2,1)S(1)} %collective-permute-done.17.refs_1_) | copy-start | bytes 4718596
  81.6 7.2 %copy-start.18 = (bf16[64,96,128]{2,1,0:T(8,128)(2,1)}, bf16[64,96,128]{2,1,0:T(8,128)(2,1)S(1)}, u32[]{:S(2)}) copy-start(bf16[64,96,128]{2,1,0:T(8,128)(2,1)S(1)} %collective-permute-done.18.refs_5_) | copy-start | bytes 4718596
  81.6 33.7 %collective-permute-start.19 = (bf16[64,96,128]{2,1,0:T(8,128)(2,1)S(1)}, bf16[64,96,128]{2,1,0:T(8,128)(2,1)S(1)}, u32[]{:S(2)}, u32[]{:S(2)}) collective-permute-start(bf16[64,96,128]{2,1,0:T(8,128)(2,1)S(1)} %collective-permute-done.17.refs_1_), channel_id=1, source_target_pairs={{0,4},{1,13},{2,6},{3,15},{64,68},{65,77},{66,70},{67,79},{4,8},{5... | collective-permute-start | bytes 4718600 | tf_op jit(solution)/shard_map/ppermute | solution.py:291
  82.0 33.3 %collective-permute-start.20 = (bf16[64,96,128]{2,1,0:T(8,128)(2,1)S(1)}, bf16[64,96,128]{2,1,0:T(8,128)(2,1)S(1)}, u32[]{:S(2)}, u32[]{:S(2)}) collective-permute-start(bf16[64,96,128]{2,1,0:T(8,128)(2,1)S(1)} %collective-permute-done.18.refs_5_), channel_id=1, source_target_pairs={{0,16},{1,49},{2,18},{3,51},{64,80},{65,113},{66,82},{67,115},{4,2... | collective-permute-start | bytes 4718600 | tf_op jit(solution)/shard_map/ppermute | solution.py:291
  88.8 2.0 %copy-start.3 = (bf16[128,128,128]{2,1,0:T(8,128)(2,1)}, bf16[128,128,128]{2,1,0:T(8,128)(2,1)S(1)}, u32[]{:S(2)}) copy-start(bf16[128,128,128]{2,1,0:T(8,128)(2,1)S(1)} %gate_values.2.refs_8_) | copy-start | bytes 12582916
  98.5 19.9 %collective-permute-start.22 = (bf16[64,96,128]{2,1,0:T(8,128)(2,1)}, bf16[64,96,128]{2,1,0:T(8,128)(2,1)}, u32[]{:S(2)}, u32[]{:S(2)}) collective-permute-start(bf16[64,96,128]{2,1,0:T(8,128)(2,1)} %collective-permute-done.3.c_ref), channel_id=1, source_target_pairs={{0,1},{1,0},{2,3},{3,2},{64,65},{65,64},{66,67},{67,66},{4,5},{5,4... | collective-permute-start | bytes 4718600 | tf_op jit(solution)/shard_map/ppermute | solution.py:336
  105.1 1.9 copy-start.1
  115.3 1.1 copy-start.20
  116.4 13.8 %collective-permute-start.21 = (bf16[64,96,128]{2,1,0:T(8,128)(2,1)}, bf16[64,96,128]{2,1,0:T(8,128)(2,1)}, u32[]{:S(2)}, u32[]{:S(2)}) collective-permute-start(bf16[64,96,128]{2,1,0:T(8,128)(2,1)} %collective-permute-done.4.c_ref), channel_id=1, source_target_pairs={{0,1},{1,0},{2,3},{3,2},{64,65},{65,64},{66,67},{67,66},{4,5},{5,4... | collective-permute-start | bytes 4718600 | tf_op jit(solution)/shard_map/ppermute | solution.py:344
  117.5 25.9 %collective-permute-start.25 = (bf16[64,96,128]{2,1,0:T(8,128)(2,1)}, bf16[64,96,128]{2,1,0:T(8,128)(2,1)}, u32[]{:S(2)}, u32[]{:S(2)}) collective-permute-start(bf16[64,96,128]{2,1,0:T(8,128)(2,1)} %collective-permute-done.23.refs_1_), channel_id=1, source_target_pairs={{0,4},{1,13},{2,6},{3,15},{64,68},{65,77},{66,70},{67,79},{4,8},{5... | collective-permute-start | bytes 4718600 | tf_op jit(solution)/shard_map/ppermute | solution.py:291
  117.5 25.9 %collective-permute-start.26 = (bf16[64,96,128]{2,1,0:T(8,128)(2,1)}, bf16[64,96,128]{2,1,0:T(8,128)(2,1)}, u32[]{:S(2)}, u32[]{:S(2)}) collective-permute-start(bf16[64,96,128]{2,1,0:T(8,128)(2,1)} %collective-permute-done.24.refs_5_), channel_id=1, source_target_pairs={{0,16},{1,49},{2,18},{3,51},{64,80},{65,113},{66,82},{67,115},{4,2... | collective-permute-start | bytes 4718600 | tf_op jit(solution)/shard_map/ppermute | solution.py:291
  118.5 1.9 copy-start.6
  120.4 8.1 %copy-start.21 = (bf16[64,96,128]{2,1,0:T(8,128)(2,1)S(1)}, bf16[64,96,128]{2,1,0:T(8,128)(2,1)}, u32[]{:S(2)}) copy-start(bf16[64,96,128]{2,1,0:T(8,128)(2,1)} %copy-done.20) | copy-start | bytes 4718596
  120.4 8.3 %copy-start.24 = (bf16[64,96,128]{2,1,0:T(8,128)(2,1)S(1)}, bf16[64,96,128]{2,1,0:T(8,128)(2,1)}, u32[]{:S(2)}) copy-start(bf16[64,96,128]{2,1,0:T(8,128)(2,1)} %copy-done.23) | copy-start | bytes 4718596
  128.4 27.8 %copy-start.9 = (bf16[64,96,128]{2,1,0:T(8,128)(2,1)S(1)}, bf16[64,96,128]{2,1,0:T(8,128)(2,1)}, u32[]{:S(2)}) copy-start(bf16[64,96,128]{2,1,0:T(8,128)(2,1)} %copy-done.8) | copy-start | bytes 4718596
  128.4 27.8 %copy-start.11 = (bf16[64,96,128]{2,1,0:T(8,128)(2,1)S(1)}, bf16[64,96,128]{2,1,0:T(8,128)(2,1)}, u32[]{:S(2)}) copy-start(bf16[64,96,128]{2,1,0:T(8,128)(2,1)} %copy-done.10) | copy-start | bytes 4718596
  128.5 27.8 %copy-start.17 = (bf16[64,96,128]{2,1,0:T(8,128)(2,1)S(1)}, bf16[64,96,128]{2,1,0:T(8,128)(2,1)}, u32[]{:S(2)}) copy-start(bf16[64,96,128]{2,1,0:T(8,128)(2,1)} %copy-done.16) | copy-start | bytes 4718596
  128.5 27.8 %copy-start.19 = (bf16[64,96,128]{2,1,0:T(8,128)(2,1)S(1)}, bf16[64,96,128]{2,1,0:T(8,128)(2,1)}, u32[]{:S(2)}) copy-start(bf16[64,96,128]{2,1,0:T(8,128)(2,1)} %copy-done.18) | copy-start | bytes 4718596
  128.5 27.8 %copy-start.22 = (bf16[64,96,128]{2,1,0:T(8,128)(2,1)S(1)}, bf16[64,96,128]{2,1,0:T(8,128)(2,1)}, u32[]{:S(2)}) copy-start(bf16[64,96,128]{2,1,0:T(8,128)(2,1)} %copy-done.20) | copy-start | bytes 4718596
  128.5 27.8 %copy-start.25 = (bf16[64,96,128]{2,1,0:T(8,128)(2,1)S(1)}, bf16[64,96,128]{2,1,0:T(8,128)(2,1)}, u32[]{:S(2)}) copy-start(bf16[64,96,128]{2,1,0:T(8,128)(2,1)} %copy-done.23) | copy-start | bytes 4718596
  128.5 27.8 %copy-start.29 = (bf16[128,128]{1,0:T(8,128)(2,1)S(1)}, bf16[128,128]{1,0:T(8,128)(2,1)}, u32[]{:S(2)}) copy-start(bf16[128,128]{1,0:T(8,128)(2,1)} %refs_9_.3) | copy-start | bytes 98308
  128.5 27.7 %collective-permute-start.29 = (bf16[64,96,128]{2,1,0:T(8,128)(2,1)S(1)}, bf16[64,96,128]{2,1,0:T(8,128)(2,1)S(1)}, u32[]{:S(2)}, u32[]{:S(2)}) collective-permute-start(bf16[64,96,128]{2,1,0:T(8,128)(2,1)S(1)} %copy-done.21), channel_id=1, source_target_pairs={{0,4},{1,13},{2,6},{3,15},{64,68},{65,77},{66,70},{67,79},{4,8},{5... | collective-permute-start | bytes 4718600 | tf_op jit(solution)/shard_map/ppermute | solution.py:291
  128.7 27.6 %collective-permute-start.30 = (bf16[64,96,128]{2,1,0:T(8,128)(2,1)S(1)}, bf16[64,96,128]{2,1,0:T(8,128)(2,1)S(1)}, u32[]{:S(2)}, u32[]{:S(2)}) collective-permute-start(bf16[64,96,128]{2,1,0:T(8,128)(2,1)S(1)} %copy-done.24), channel_id=1, source_target_pairs={{0,16},{1,49},{2,18},{3,51},{64,80},{65,113},{66,82},{67,115},{4,2... | collective-permute-start | bytes 4718600 | tf_op jit(solution)/shard_map/ppermute | solution.py:291
  130.2 46.1 %copy-start.13 = (bf16[64,96,128]{2,1,0:T(8,128)(2,1)S(1)}, bf16[64,96,128]{2,1,0:T(8,128)(2,1)}, u32[]{:S(2)}) copy-start(bf16[64,96,128]{2,1,0:T(8,128)(2,1)} %copy-done.12) | copy-start | bytes 4718596
  138.9 4.6 %copy-start = (bf16[128,128,384]{2,1,0:T(8,128)(2,1)}, bf16[128,128,384]{2,1,0:T(8,128)(2,1)S(1)}, u32[]{:S(2)}) copy-start(bf16[128,128,384]{2,1,0:T(8,128)(2,1)S(1)} %arrange_left.3.lx_ref.ly_ref) | copy-start | bytes 37748740
  143.5 32.8 %collective-permute-start.27 = (bf16[64,96,128]{2,1,0:T(8,128)(2,1)}, bf16[64,96,128]{2,1,0:T(8,128)(2,1)S(1)}, u32[]{:S(2)}, u32[]{:S(2)}) collective-permute-start(bf16[64,96,128]{2,1,0:T(8,128)(2,1)} %collective-permute-done.25.refs_2_), channel_id=1, source_target_pairs={{0,4},{1,13},{2,6},{3,15},{64,68},{65,77},{66,70},{67,79},{4,8},{5... | collective-permute-start | bytes 4718600 | tf_op jit(solution)/shard_map/ppermute | solution.py:291
  145.0 31.3 %collective-permute-start.28 = (bf16[64,96,128]{2,1,0:T(8,128)(2,1)}, bf16[64,96,128]{2,1,0:T(8,128)(2,1)S(1)}, u32[]{:S(2)}, u32[]{:S(2)}) collective-permute-start(bf16[64,96,128]{2,1,0:T(8,128)(2,1)} %collective-permute-done.26.refs_6_), channel_id=1, source_target_pairs={{0,16},{1,49},{2,18},{3,51},{64,80},{65,113},{66,82},{67,115},{4,2... | collective-permute-start | bytes 4718600 | tf_op jit(solution)/shard_map/ppermute | solution.py:291
  156.3 2.2 %copy-start.4 = (bf16[128,128,128]{2,1,0:T(8,128)(2,1)S(1)}, bf16[128,128,128]{2,1,0:T(8,128)(2,1)}, u32[]{:S(2)}) copy-start(bf16[128,128,128]{2,1,0:T(8,128)(2,1)} %copy-done.3) | copy-start | bytes 12582916
  158.5 17.9 %copy-start.2 = (bf16[128,128,128]{2,1,0:T(8,128)(2,1)S(1)}, bf16[128,128,128]{2,1,0:T(8,128)(2,1)}, u32[]{:S(2)}) copy-start(bf16[128,128,128]{2,1,0:T(8,128)(2,1)} %copy-done.1) | copy-start | bytes 12582916
  176.3 1.4 copy-start.15
  (1 other events, 1.1 us)

commit v5 on v4

--- a/solution.py
+++ b/solution.py
@@ -244,7 +244,7 @@
 def update_block(left, x_parts, y_parts, gate, weights, at, n_blocks, part, n_parts, whole=None):
     n_c, n_i, depth = left.shape
     half, n_k, n_j = x_parts[0].shape
-    c_block, i_block = 16, 16
+    c_block, i_block = 16, 32
     rows = n_i // n_parts
     n_sum = half // c_block
     n_out = rows // i_block

time: 197 us -> 194 us (0.985)
  Pallas kernels: 77.8 us -> 75.4 us
    pallas_call x2, Pallas kernels: 36.2 us -> 33.8 us  [update_block(): pl.pallas_call(functools.partial(update_kernel, n_sum), grid=(n_sum + n_o...]
where the time goes in v5:
time: 194 us
  Pallas kernels  75.4 us (39%)
  waiting for transfers between devices  68.1 us (35%)
  starting transfers between devices  26.9 us (14%)
  local copies, waits for them, and re-layouts  22.3 us (11%)
    ppermute x24, waiting for transfers between devices, step_on(): held.append(lax.ppermute(piece, AXES, ring))  43 us
    pallas_call x2, Pallas kernels, update_block(): pl.pallas_call(functools.partial(update_kernel, n_sum), grid=(n_sum + n_o...  33.8 us
    unnamed x80, local copies, waits for them, and re-layouts  20.7 us
    ppermute x24, starting transfers between devices, step_on(): held.append(lax.ppermute(piece, AXES, ring))  20.2 us
    pallas_call x2, Pallas kernels, arrange_left(): pl.pallas_call(arrange_kernel, grid=(steps,), in_specs=in_specs, out_spec...  16.7 us
    ppermute x1, waiting for transfers between devices, shards(): far_0 = lax.ppermute(after(near[0], *halves_1), AXES, SWAP_Z_LO)  14.8 us
    pallas_call x2, Pallas kernels, gate_values(): pl.pallas_call(gate_kernel, grid=(n_i // block,), in_specs=[pl.BlockSpec(...  13.1 us
    pallas_call x1, Pallas kernels, project_left(): pl.pallas_call(left_kernel, grid=(n_k // block,), in_specs=[pl.BlockSpec(...  8.93 us
  transfers between devices with their start and end apart: 31, of which 18 were waited for; matrix products, arithmetic and copies ran while one was open for 1% of the time, Pallas kernels for 30%

profile of v5, /device:TPU:0, one launch (start us, length us, event | category | flops | bytes accessed | tf_op | source)
XLA Modules:
  0.0 193.7 jit_solution(741935774133584727)
XLA Ops:
  0.0 1.2 fusion.45
  1.2 4.0 %collective-permute-start = (bf16[12,128,128]{2,1,0:T(8,128)(2,1)S(1)}, bf16[12,128,128]{2,1,0:T(8,128)(2,1)S(1)}, u32[]{:S(2)}, u32[]{:S(2)}) collective-permute-start(bf16[12,128,128]{2,1,0:T(8,128)(2,1)S(1)} %get-tuple-element.86.own_ref), channel_id=1, source_target_pairs={{0,64},{1,65},{2,66},{3,67},{64,0},{65,1},{66,2},{67,3},{4,68},{5,... | collective-permute-start | bytes 1179656 | tf_op jit(solution)/shard_map/ppermute | solution.py:315
  5.3 1.9 copy-done.7
  7.2 8.9 %project_left.1.a_ref = bf16[128,96,128]{2,1,0:T(8,128)(2,1)S(1)} custom-call(bf16[128,96,128]{2,1,0:T(8,128)(2,1)S(1)} %copy-done.7, bf16[128,128]{1,0:T(8,128)(2,1)S(1)} %copy-done.30, bf16[128,128]{1,0:T(8,128)(2,1)S(1)} %copy-done.31), custom_call_target="tpu_custom_call" | custom-call | flops 805306368 | bytes 12582912 | tf_op jit(solution)/shard_map/project_left/pallas_call | solution.py:80
  16.2 1.4 project_right.2
  17.6 5.1 %collective-permute-done.1.other_ref = bf16[12,128,128]{2,1,0:T(8,128)(2,1)S(1)} collective-permute-done((bf16[12,128,128]{2,1,0:T(8,128)(2,1)S(1)}, bf16[12,128,128]{2,1,0:T(8,128)(2,1)S(1)}, u32[]{:S(2)}, u32[]{:S(2)}) %collective-permute-start.1) | collective-permute-done | bytes 393248 | tf_op jit(solution)/shard_map/ppermute | solution.py:315
  22.8 1.5 collective-permute-start.5
  24.3 1.6 collective-permute-start.6
  25.9 1.4 project_right.3
  27.3 1.6 collective-permute-start.9
  28.8 1.6 collective-permute-start.10
  30.4 1.4 collective-permute-done.5
  31.8 1.5 collective-permute-done.6
  33.3 1.5 collective-permute-start.7
  34.8 0.4 collective-permute-start.8
  35.1 0.2 fusion.44
  35.3 1.0 collective-permute-done.9
  36.3 1.5 collective-permute-done.10
  37.8 1.2 collective-permute-start.13
  39.0 0.4 collective-permute-start.14
  39.5 2.8 %collective-permute-done.7 = bf16[64,24,128]{2,1,0:T(8,128)(2,1)S(1)} collective-permute-done((bf16[64,24,128]{2,1,0:T(8,128)(2,1)S(1)}, bf16[64,24,128]{2,1,0:T(8,128)(2,1)S(1)}, u32[]{:S(2)}, u32[]{:S(2)}) %collective-permute-start.7) | collective-permute-done | bytes 393248 | tf_op jit(solution)/shard_map/ppermute | solution.py:291
  42.3 1.3 collective-permute-start.3
  43.5 0.2 collective-permute-done.8
  43.8 1.6 copy-done.5
  45.4 1.2 collective-permute-start.11
  46.8 1.2 collective-permute-done.14
  48.0 1.1 collective-permute-start.15
  49.3 5.0 %collective-permute-done.11 = bf16[64,24,128]{2,1,0:T(8,128)(2,1)S(1)} collective-permute-done((bf16[64,24,128]{2,1,0:T(8,128)(2,1)S(1)}, bf16[64,24,128]{2,1,0:T(8,128)(2,1)S(1)}, u32[]{:S(2)}, u32[]{:S(2)}) %collective-permute-start.11) | collective-permute-done | bytes 393248 | tf_op jit(solution)/shard_map/ppermute | solution.py:291
  54.5 1.3 collective-permute-done.12
  55.8 2.8 %collective-permute-done.15 = bf16[64,24,128]{2,1,0:T(8,128)(2,1)S(1)} collective-permute-done((bf16[64,24,128]{2,1,0:T(8,128)(2,1)S(1)}, bf16[64,24,128]{2,1,0:T(8,128)(2,1)S(1)}, u32[]{:S(2)}, u32[]{:S(2)}) %collective-permute-start.15) | collective-permute-done | bytes 393248 | tf_op jit(solution)/shard_map/ppermute | solution.py:291
  58.6 1.3 collective-permute-done.16
  59.9 0.5 collective-permute-start.18
  61.1 0.6 collective-permute-start.23
  61.6 1.2 collective-permute-start.24
  62.9 14.8 %collective-permute-done.3.c_ref = bf16[64,96,128]{2,1,0:T(8,128)(2,1)} collective-permute-done((bf16[64,96,128]{2,1,0:T(8,128)(2,1)S(1)}, bf16[64,96,128]{2,1,0:T(8,128)(2,1)}, u32[]{:S(2)}, u32[]{:S(2)}) %collective-permute-start.3) | collective-permute-done | bytes 1572896 | tf_op jit(solution)/shard_map/ppermute | solution.py:323
  77.7 1.3 collective-permute-start.4
  79.0 2.6 %collective-permute-done.17.refs_1_ = bf16[64,96,128]{2,1,0:T(8,128)(2,1)S(1)} collective-permute-done((bf16[64,96,128]{2,1,0:T(8,128)(2,1)S(1)}, bf16[64,96,128]{2,1,0:T(8,128)(2,1)S(1)}, u32[]{:S(2)}, u32[]{:S(2)}) %collective-permute-start.17) | collective-permute-done | bytes 1572896 | tf_op jit(solution)/shard_map/ppermute | solution.py:291
  81.6 0.4 collective-permute-start.19
  82.0 0.2 collective-permute-start.20
  82.2 6.5 %gate_values.2.refs_8_ = bf16[128,128,128]{2,1,0:T(8,128)(2,1)S(1)} custom-call(bf16[128,256,128]{2,1,0:T(8,128)(2,1)S(1)} %bitcast.2, bf16[128,128]{1,0:T(8,128)(2,1)S(1)} %copy-done.26), custom_call_target="tpu_custom_call" | custom-call | flops 1000 | bytes 1000 | tf_op jit(solution)/shard_map/gate_values/pallas_call | solution.py:140
  88.8 2.0 %copy-done.3 = bf16[128,128,128]{2,1,0:T(8,128)(2,1)} copy-done((bf16[128,128,128]{2,1,0:T(8,128)(2,1)}, bf16[128,128,128]{2,1,0:T(8,128)(2,1)S(1)}, u32[]{:S(2)}) %copy-start.3) | copy-done | bytes 4194328
  90.8 7.7 %collective-permute-done.23.refs_1_ = bf16[64,96,128]{2,1,0:T(8,128)(2,1)} collective-permute-done((bf16[64,96,128]{2,1,0:T(8,128)(2,1)S(1)}, bf16[64,96,128]{2,1,0:T(8,128)(2,1)}, u32[]{:S(2)}, u32[]{:S(2)}) %collective-permute-start.23) | collective-permute-done | bytes 1572896 | tf_op jit(solution)/shard_map/ppermute | solution.py:291
  98.5 6.5 %gate_values.3.refs_8_ = bf16[128,128,128]{2,1,0:T(8,128)(2,1)S(1)} custom-call(bf16[128,256,128]{2,1,0:T(8,128)(2,1)S(1)} %bitcast.2, bf16[128,128]{1,0:T(8,128)(2,1)S(1)} %copy-done.26), custom_call_target="tpu_custom_call" | custom-call | flops 1000 | bytes 1000 | tf_op jit(solution)/shard_map/gate_values/pallas_call | solution.py:140
  105.1 1.9 %copy-done.1 = bf16[128,128,128]{2,1,0:T(8,128)(2,1)} copy-done((bf16[128,128,128]{2,1,0:T(8,128)(2,1)}, bf16[128,128,128]{2,1,0:T(8,128)(2,1)S(1)}, u32[]{:S(2)}) %copy-start.1) | copy-done | bytes 4194328
  107.0 5.2 %collective-permute-done.4.c_ref = bf16[64,96,128]{2,1,0:T(8,128)(2,1)} collective-permute-done((bf16[64,96,128]{2,1,0:T(8,128)(2,1)S(1)}, bf16[64,96,128]{2,1,0:T(8,128)(2,1)}, u32[]{:S(2)}, u32[]{:S(2)}) %collective-permute-start.4) | collective-permute-done | bytes 1572896 | tf_op jit(solution)/shard_map/ppermute | solution.py:337
  112.2 3.0 %collective-permute-done.19.refs_2_ = bf16[64,96,128]{2,1,0:T(8,128)(2,1)S(1)} collective-permute-done((bf16[64,96,128]{2,1,0:T(8,128)(2,1)S(1)}, bf16[64,96,128]{2,1,0:T(8,128)(2,1)S(1)}, u32[]{:S(2)}, u32[]{:S(2)}) %collective-permute-start.19) | collective-permute-done | bytes 1572896 | tf_op jit(solution)/shard_map/ppermute | solution.py:291
  115.3 1.1 copy-done.20
  116.4 1.1 copy-done.23
  117.5 0.5 collective-permute-start.26
  118.1 0.3 fusion
  118.3 0.1 add_convert_fusion.order_ref
  118.5 1.9 copy-done.6
  120.4 8.1 %arrange_left.2.rest_0_ = bf16[128,128,384]{2,1,0:T(8,128)(2,1)S(1)} custom-call(bf16[128,96,128]{2,1,0:T(8,128)(2,1)S(1)} %project_left.1.a_ref, bf16[128,96,128]{2,1,0:T(8,128)(2,1)S(1)} %copy-done.6, bf16[64,96,128]{2,1,0:T(8,128)(2,1)} %collective-permute-done.3.c_ref, bf16[64,96,128]{2,1,0:T(8,128)(2,1)} %collective-permute-done.22.d_ref, ...), custom_call_target="tpu_custom_call" | custom-call | flops 1000 | bytes 1000 | tf_op jit(solution)/shard_map/arrange_left/pallas_call | solution.py:181
  128.5 0.1 collective-permute-start.29
  128.7 1.5 collective-permute-start.30
  130.2 8.7 %arrange_left.3.lx_ref.ly_ref = bf16[128,128,384]{2,1,0:T(8,128)(2,1)S(1)} custom-call(bf16[128,96,128]{2,1,0:T(8,128)(2,1)S(1)} %project_left.1.a_ref, bf16[128,96,128]{2,1,0:T(8,128)(2,1)S(1)} %copy-done.6, bf16[64,96,128]{2,1,0:T(8,128)(2,1)} %collective-permute-done.4.c_ref, ...), custom_call_target="tpu_custom_call", output_to_operand_aliasing={{}: (5, {})} | custom-call | flops 1000 | bytes 1000 | tf_op jit(solution)/shard_map/arrange_left/pallas_call | solution.py:181
  138.9 4.6 %copy-done = bf16[128,128,384]{2,1,0:T(8,128)(2,1)} copy-done((bf16[128,128,384]{2,1,0:T(8,128)(2,1)}, bf16[128,128,384]{2,1,0:T(8,128)(2,1)S(1)}, u32[]{:S(2)}) %copy-start) | copy-done | bytes 12582936
  143.5 1.6 collective-permute-start.27
  145.0 1.5 collective-permute-start.28
  146.5 9.7 %collective-permute-done.29.refs_3_ = bf16[64,96,128]{2,1,0:T(8,128)(2,1)S(1)} collective-permute-done((bf16[64,96,128]{2,1,0:T(8,128)(2,1)S(1)}, bf16[64,96,128]{2,1,0:T(8,128)(2,1)S(1)}, u32[]{:S(2)}, u32[]{:S(2)}) %collective-permute-start.29) | collective-permute-done | bytes 1572896 | tf_op jit(solution)/shard_map/ppermute | solution.py:291
  156.3 2.2 %copy-done.4 = bf16[128,128,128]{2,1,0:T(8,128)(2,1)S(1)} copy-done((bf16[128,128,128]{2,1,0:T(8,128)(2,1)S(1)}, bf16[128,128,128]{2,1,0:T(8,128)(2,1)}, u32[]{:S(2)}) %copy-start.4) | copy-done | bytes 4194328
  158.5 16.7 %update_block.2.refs_10_ = bf16[128,256,128]{2,1,0:T(8,128)(2,1)} custom-call(bf16[128,128,384]{2,1,0:T(8,128)(2,1)} %copy-done, bf16[128,128,384]{2,1,0:T(8,128)(2,1)} %copy-done, bf16[64,96,128]{2,1,0:T(8,128)(2,1)S(1)} %copy-done.11, bf16[64,96,128]{2,1,0:T(8,128)(2,1)S(1)} %copy-done.17, bf16[64,96,128]{2,1,0:T(8,128)(2,1)S(1)} %copy-done.22, ...), custom_call_target="tpu_custom_call" | custom-call | flops 1000 | bytes 1000 | tf_op jit(solution)/shard_map/update_block/pallas_call | solution.py:270
  175.2 1.4 copy-done.15
  176.6 17.2 %update_block.3 = bf16[128,256,128]{2,1,0:T(8,128)(2,1)} custom-call(bf16[128,128,384]{2,1,0:T(8,128)(2,1)} %copy-done, bf16[128,128,384]{2,1,0:T(8,128)(2,1)} %copy-done, bf16[64,96,128]{2,1,0:T(8,128)(2,1)S(1)} %copy-done.15, bf16[64,96,128]{2,1,0:T(8,128)(2,1)} %collective-permute-done.23.refs_1_, ...), custom_call_target="tpu_custom_call", output_to_operand_aliasing={{}: (12, {})} | custom-call | flops 1000 | bytes 1000 | tf_op jit(solution)/shard_map/update_block/pallas_call | solution.py:270
  (102 shorter events, 1.5 us)
Async XLA Ops:
  0.0 5.3 %copy-start.30 = (bf16[128,128]{1,0:T(8,128)(2,1)S(1)}, bf16[128,128]{1,0:T(8,128)(2,1)}, u32[]{:S(2)}) copy-start(bf16[128,128]{1,0:T(8,128)(2,1)} %proj_ref.3) | copy-start | bytes 98308
  0.0 5.3 %copy-start.31 = (bf16[128,128]{1,0:T(8,128)(2,1)S(1)}, bf16[128,128]{1,0:T(8,128)(2,1)}, u32[]{:S(2)}) copy-start(bf16[128,128]{1,0:T(8,128)(2,1)} %gate_ref.3) | copy-start | bytes 98308
  1.2 15.0 %collective-permute-start = (bf16[12,128,128]{2,1,0:T(8,128)(2,1)S(1)}, bf16[12,128,128]{2,1,0:T(8,128)(2,1)S(1)}, u32[]{:S(2)}, u32[]{:S(2)}) collective-permute-start(bf16[12,128,128]{2,1,0:T(8,128)(2,1)S(1)} %get-tuple-element.86.own_ref), channel_id=1, source_target_pairs={{0,64},{1,65},{2,66},{3,67},{64,0},{65,1},{66,2},{67,3},{4,68},{5,... | collective-permute-start | bytes 1179656 | tf_op jit(solution)/shard_map/ppermute | solution.py:315
  5.2 17.5 %collective-permute-start.1 = (bf16[12,128,128]{2,1,0:T(8,128)(2,1)S(1)}, bf16[12,128,128]{2,1,0:T(8,128)(2,1)S(1)}, u32[]{:S(2)}, u32[]{:S(2)}) collective-permute-start(bf16[12,128,128]{2,1,0:T(8,128)(2,1)S(1)} %get-tuple-element.85.own_ref), channel_id=1, source_target_pairs={{0,64},{1,65},{2,66},{3,67},{64,0},{65,1},{66,2},{67,3},{4,68},{5,... | collective-permute-start | bytes 1179656 | tf_op jit(solution)/shard_map/ppermute | solution.py:315
  5.3 1.9 copy-start.7
  7.2 9.0 %copy-start.27 = (bf16[128,128]{1,0:T(8,128)(2,1)S(1)}, bf16[128,128]{1,0:T(8,128)(2,1)}, u32[]{:S(2)}) copy-start(bf16[128,128]{1,0:T(8,128)(2,1)} %proj_ref.5) | copy-start | bytes 98308
  7.2 9.0 %copy-start.28 = (bf16[128,128]{1,0:T(8,128)(2,1)S(1)}, bf16[128,128]{1,0:T(8,128)(2,1)}, u32[]{:S(2)}) copy-start(bf16[128,128]{1,0:T(8,128)(2,1)} %gate_ref.5) | copy-start | bytes 98308
  22.8 21.0 %collective-permute-start.2 = (bf16[128,96,128]{2,1,0:T(8,128)(2,1)S(1)}, bf16[128,96,128]{2,1,0:T(8,128)(2,1)S(1)}, u32[]{:S(2)}, u32[]{:S(2)}) collective-permute-start(bf16[128,96,128]{2,1,0:T(8,128)(2,1)S(1)} %project_left.1.a_ref), channel_id=1, source_target_pairs={{0,1},{1,0},{2,3},{3,2},{64,65},{65,64},{66,67},{67,66},{4,5},{5,4... | collective-permute-start | bytes 9437192 | tf_op jit(solution)/shard_map/ppermute | solution.py:322
  22.8 9.0 %collective-permute-start.5 = (bf16[64,24,128]{2,1,0:T(8,128)(2,1)S(1)}, bf16[64,24,128]{2,1,0:T(8,128)(2,1)S(1)}, u32[]{:S(2)}, u32[]{:S(2)}) collective-permute-start(bf16[64,24,128]{2,1,0:T(8,128)(2,1)S(1)} %get-tuple-element.45), channel_id=1, source_target_pairs={{0,16},{1,49},{2,18},{3,51},{64,80},{65,113},{66,82},{67,115},{4,2... | collective-permute-start | bytes 1179656 | tf_op jit(solution)/shard_map/ppermute | solution.py:291
  24.3 9.0 %collective-permute-start.6 = (bf16[64,24,128]{2,1,0:T(8,128)(2,1)S(1)}, bf16[64,24,128]{2,1,0:T(8,128)(2,1)S(1)}, u32[]{:S(2)}, u32[]{:S(2)}) collective-permute-start(bf16[64,24,128]{2,1,0:T(8,128)(2,1)S(1)} %get-tuple-element.46), channel_id=1, source_target_pairs={{0,4},{1,13},{2,6},{3,15},{64,68},{65,77},{66,70},{67,79},{4,8},{5... | collective-permute-start | bytes 1179656 | tf_op jit(solution)/shard_map/ppermute | solution.py:291
  27.3 9.1 %collective-permute-start.9 = (bf16[64,24,128]{2,1,0:T(8,128)(2,1)S(1)}, bf16[64,24,128]{2,1,0:T(8,128)(2,1)S(1)}, u32[]{:S(2)}, u32[]{:S(2)}) collective-permute-start(bf16[64,24,128]{2,1,0:T(8,128)(2,1)S(1)} %get-tuple-element.49), channel_id=1, source_target_pairs={{0,16},{1,49},{2,18},{3,51},{64,80},{65,113},{66,82},{67,115},{4,2... | collective-permute-start | bytes 1179656 | tf_op jit(solution)/shard_map/ppermute | solution.py:291
  28.8 9.0 %collective-permute-start.10 = (bf16[64,24,128]{2,1,0:T(8,128)(2,1)S(1)}, bf16[64,24,128]{2,1,0:T(8,128)(2,1)S(1)}, u32[]{:S(2)}, u32[]{:S(2)}) collective-permute-start(bf16[64,24,128]{2,1,0:T(8,128)(2,1)S(1)} %get-tuple-element.50), channel_id=1, source_target_pairs={{0,4},{1,13},{2,6},{3,15},{64,68},{65,77},{66,70},{67,79},{4,8},{5... | collective-permute-start | bytes 1179656 | tf_op jit(solution)/shard_map/ppermute | solution.py:291
  33.3 9.0 %collective-permute-start.7 = (bf16[64,24,128]{2,1,0:T(8,128)(2,1)S(1)}, bf16[64,24,128]{2,1,0:T(8,128)(2,1)S(1)}, u32[]{:S(2)}, u32[]{:S(2)}) collective-permute-start(bf16[64,24,128]{2,1,0:T(8,128)(2,1)S(1)} %collective-permute-done.5), channel_id=1, source_target_pairs={{0,16},{1,49},{2,18},{3,51},{64,80},{65,113},{66,82},{67,115},{4,2... | collective-permute-start | bytes 1179656 | tf_op jit(solution)/shard_map/ppermute | solution.py:291
  34.8 9.0 %collective-permute-start.8 = (bf16[64,24,128]{2,1,0:T(8,128)(2,1)S(1)}, bf16[64,24,128]{2,1,0:T(8,128)(2,1)S(1)}, u32[]{:S(2)}, u32[]{:S(2)}) collective-permute-start(bf16[64,24,128]{2,1,0:T(8,128)(2,1)S(1)} %collective-permute-done.6), channel_id=1, source_target_pairs={{0,4},{1,13},{2,6},{3,15},{64,68},{65,77},{66,70},{67,79},{4,8},{5... | collective-permute-start | bytes 1179656 | tf_op jit(solution)/shard_map/ppermute | solution.py:291
  35.1 47.1 %slice-start = ((s8[8388608]{0:T(1024)(128)(4,1)}), s8[4194304]{0:T(1024)(128)(4,1)S(1)}, s32[]{:S(2)}) async-start(s8[8388608]{0:T(1024)(128)(4,1)} %bitcast.1), calls=%async_computation | async-start | bytes 8388608
  37.8 9.0 %collective-permute-start.13 = (bf16[64,24,128]{2,1,0:T(8,128)(2,1)S(1)}, bf16[64,24,128]{2,1,0:T(8,128)(2,1)S(1)}, u32[]{:S(2)}, u32[]{:S(2)}) collective-permute-start(bf16[64,24,128]{2,1,0:T(8,128)(2,1)S(1)} %collective-permute-done.9), channel_id=1, source_target_pairs={{0,16},{1,49},{2,18},{3,51},{64,80},{65,113},{66,82},{67,115},{4,2... | collective-permute-start | bytes 1179656 | tf_op jit(solution)/shard_map/ppermute | solution.py:291
  39.0 9.0 %collective-permute-start.14 = (bf16[64,24,128]{2,1,0:T(8,128)(2,1)S(1)}, bf16[64,24,128]{2,1,0:T(8,128)(2,1)S(1)}, u32[]{:S(2)}, u32[]{:S(2)}) collective-permute-start(bf16[64,24,128]{2,1,0:T(8,128)(2,1)S(1)} %collective-permute-done.10), channel_id=1, source_target_pairs={{0,4},{1,13},{2,6},{3,15},{64,68},{65,77},{66,70},{67,79},{4,8},{5... | collective-permute-start | bytes 1179656 | tf_op jit(solution)/shard_map/ppermute | solution.py:291
  42.3 35.4 %collective-permute-start.3 = (bf16[64,96,128]{2,1,0:T(8,128)(2,1)S(1)}, bf16[64,96,128]{2,1,0:T(8,128)(2,1)}, u32[]{:S(2)}, u32[]{:S(2)}) collective-permute-start(bf16[64,96,128]{2,1,0:T(8,128)(2,1)S(1)} %get-tuple-element.51), channel_id=1, source_target_pairs={{0,2},{1,3},{2,0},{3,1},{64,66},{65,67},{66,64},{67,65},{4,6},{5,7... | collective-permute-start | bytes 4718600 | tf_op jit(solution)/shard_map/ppermute | solution.py:323
  43.7 1.6 copy-start.5
  45.4 9.0 %collective-permute-start.11 = (bf16[64,24,128]{2,1,0:T(8,128)(2,1)S(1)}, bf16[64,24,128]{2,1,0:T(8,128)(2,1)S(1)}, u32[]{:S(2)}, u32[]{:S(2)}) collective-permute-start(bf16[64,24,128]{2,1,0:T(8,128)(2,1)S(1)} %collective-permute-done.7), channel_id=1, source_target_pairs={{0,16},{1,49},{2,18},{3,51},{64,80},{65,113},{66,82},{67,115},{4,2... | collective-permute-start | bytes 1179656 | tf_op jit(solution)/shard_map/ppermute | solution.py:291
  46.7 9.1 %collective-permute-start.12 = (bf16[64,24,128]{2,1,0:T(8,128)(2,1)S(1)}, bf16[64,24,128]{2,1,0:T(8,128)(2,1)S(1)}, u32[]{:S(2)}, u32[]{:S(2)}) collective-permute-start(bf16[64,24,128]{2,1,0:T(8,128)(2,1)S(1)} %collective-permute-done.8), channel_id=1, source_target_pairs={{0,4},{1,13},{2,6},{3,15},{64,68},{65,77},{66,70},{67,79},{4,8},{5... | collective-permute-start | bytes 1179656 | tf_op jit(solution)/shard_map/ppermute | solution.py:291
  46.8 35.4 %slice-start.1 = ((s8[8388608]{0:T(1024)(128)(4,1)}), s8[4194304]{0:T(1024)(128)(4,1)S(1)}, s32[]{:S(2)}) async-start(s8[8388608]{0:T(1024)(128)(4,1)} %bitcast.1), calls=%async_computation.1 | async-start | bytes 8388608
  48.0 10.6 %collective-permute-start.15 = (bf16[64,24,128]{2,1,0:T(8,128)(2,1)S(1)}, bf16[64,24,128]{2,1,0:T(8,128)(2,1)S(1)}, u32[]{:S(2)}, u32[]{:S(2)}) collective-permute-start(bf16[64,24,128]{2,1,0:T(8,128)(2,1)S(1)} %collective-permute-done.13), channel_id=1, source_target_pairs={{0,16},{1,49},{2,18},{3,51},{64,80},{65,113},{66,82},{67,115},{4,2... | collective-permute-start | bytes 1179656 | tf_op jit(solution)/shard_map/ppermute | solution.py:291
  49.2 10.8 %collective-permute-start.16 = (bf16[64,24,128]{2,1,0:T(8,128)(2,1)S(1)}, bf16[64,24,128]{2,1,0:T(8,128)(2,1)S(1)}, u32[]{:S(2)}, u32[]{:S(2)}) collective-permute-start(bf16[64,24,128]{2,1,0:T(8,128)(2,1)S(1)} %collective-permute-done.14), channel_id=1, source_target_pairs={{0,4},{1,13},{2,6},{3,15},{64,68},{65,77},{66,70},{67,79},{4,8},{5... | collective-permute-start | bytes 1179656 | tf_op jit(solution)/shard_map/ppermute | solution.py:291
  54.4 6.1 %copy-start.10 = (bf16[64,96,128]{2,1,0:T(8,128)(2,1)}, bf16[64,96,128]{2,1,0:T(8,128)(2,1)S(1)}, u32[]{:S(2)}) copy-start(bf16[64,96,128]{2,1,0:T(8,128)(2,1)S(1)} %constant_dynamic-update-slice_fusion.refs_0_) | copy-start | bytes 4718596
  55.8 4.9 %copy-start.8 = (bf16[64,96,128]{2,1,0:T(8,128)(2,1)}, bf16[64,96,128]{2,1,0:T(8,128)(2,1)S(1)}, u32[]{:S(2)}) copy-start(bf16[64,96,128]{2,1,0:T(8,128)(2,1)S(1)} %constant_dynamic-update-slice_fusion.4.refs_4_) | copy-start | bytes 4718596
  59.9 21.6 %collective-permute-start.17 = (bf16[64,96,128]{2,1,0:T(8,128)(2,1)S(1)}, bf16[64,96,128]{2,1,0:T(8,128)(2,1)S(1)}, u32[]{:S(2)}, u32[]{:S(2)}) collective-permute-start(bf16[64,96,128]{2,1,0:T(8,128)(2,1)S(1)} %constant_dynamic-update-slice_fusion.refs_0_), channel_id=1, source_target_pairs={{0,4},{1,13},{2,6},{3,15},{64,68},{65,77},{66,70},{67,79},{4,8},{5... | collective-permute-start | bytes 4718600 | tf_op jit(solution)/shard_map/ppermute | solution.py:291
  59.9 21.6 %collective-permute-start.18 = (bf16[64,96,128]{2,1,0:T(8,128)(2,1)S(1)}, bf16[64,96,128]{2,1,0:T(8,128)(2,1)S(1)}, u32[]{:S(2)}, u32[]{:S(2)}) collective-permute-start(bf16[64,96,128]{2,1,0:T(8,128)(2,1)S(1)} %constant_dynamic-update-slice_fusion.4.refs_4_), channel_id=1, source_target_pairs={{0,16},{1,49},{2,18},{3,51},{64,80},{65,113},{66,82},{67,115},{4,2... | collective-permute-start | bytes 4718600 | tf_op jit(solution)/shard_map/ppermute | solution.py:291
  60.7 21.5 %copy-start.26 = (bf16[128,128]{1,0:T(8,128)(2,1)S(1)}, bf16[128,128]{1,0:T(8,128)(2,1)}, u32[]{:S(2)}) copy-start(bf16[128,128]{1,0:T(8,128)(2,1)} %w_ref.1) | copy-start | bytes 98308
  61.0 27.8 %copy-start.14 = (bf16[64,96,128]{2,1,0:T(8,128)(2,1)}, bf16[64,96,128]{2,1,0:T(8,128)(2,1)S(1)}, u32[]{:S(2)}) copy-start(bf16[64,96,128]{2,1,0:T(8,128)(2,1)S(1)} %constant_dynamic-update-slice_fusion.8.refs_0_) | copy-start | bytes 4718596
  61.0 27.7 %copy-start.12 = (bf16[64,96,128]{2,1,0:T(8,128)(2,1)}, bf16[64,96,128]{2,1,0:T(8,128)(2,1)S(1)}, u32[]{:S(2)}) copy-start(bf16[64,96,128]{2,1,0:T(8,128)(2,1)S(1)} %constant_dynamic-update-slice_fusion.12.refs_4_) | copy-start | bytes 4718596
  61.1 37.5 %collective-permute-start.23 = (bf16[64,96,128]{2,1,0:T(8,128)(2,1)S(1)}, bf16[64,96,128]{2,1,0:T(8,128)(2,1)}, u32[]{:S(2)}, u32[]{:S(2)}) collective-permute-start(bf16[64,96,128]{2,1,0:T(8,128)(2,1)S(1)} %constant_dynamic-update-slice_fusion.8.refs_0_), channel_id=1, source_target_pairs={{0,4},{1,13},{2,6},{3,15},{64,68},{65,77},{66,70},{67,79},{4,8},{5... | collective-permute-start | bytes 4718600 | tf_op jit(solution)/shard_map/ppermute | solution.py:291
  61.6 36.9 %collective-permute-start.24 = (bf16[64,96,128]{2,1,0:T(8,128)(2,1)S(1)}, bf16[64,96,128]{2,1,0:T(8,128)(2,1)}, u32[]{:S(2)}, u32[]{:S(2)}) collective-permute-start(bf16[64,96,128]{2,1,0:T(8,128)(2,1)S(1)} %constant_dynamic-update-slice_fusion.12.refs_4_), channel_id=1, source_target_pairs={{0,16},{1,49},{2,18},{3,51},{64,80},{65,113},{66,82},{67,115},{4,2... | collective-permute-start | bytes 4718600 | tf_op jit(solution)/shard_map/ppermute | solution.py:291
  77.7 34.5 %collective-permute-start.4 = (bf16[64,96,128]{2,1,0:T(8,128)(2,1)S(1)}, bf16[64,96,128]{2,1,0:T(8,128)(2,1)}, u32[]{:S(2)}, u32[]{:S(2)}) collective-permute-start(bf16[64,96,128]{2,1,0:T(8,128)(2,1)S(1)} %get-tuple-element.52), channel_id=1, source_target_pairs={{0,2},{1,3},{2,0},{3,1},{64,66},{65,67},{66,64},{67,65},{4,6},{5,7... | collective-permute-start | bytes 4718600 | tf_op jit(solution)/shard_map/ppermute | solution.py:337
  81.6 7.2 %copy-start.16 = (bf16[64,96,128]{2,1,0:T(8,128)(2,1)}, bf16[64,96,128]{2,1,0:T(8,128)(2,1)S(1)}, u32[]{:S(2)}) copy-start(bf16[64,96,128]{2,1,0:T(8,128)(2,1)S(1)} %collective-permute-done.17.refs_1_) | copy-start | bytes 4718596
  81.6 7.2 %copy-start.18 = (bf16[64,96,128]{2,1,0:T(8,128)(2,1)}, bf16[64,96,128]{2,1,0:T(8,128)(2,1)S(1)}, u32[]{:S(2)}) copy-start(bf16[64,96,128]{2,1,0:T(8,128)(2,1)S(1)} %collective-permute-done.18.refs_5_) | copy-start | bytes 4718596
  81.6 33.7 %collective-permute-start.19 = (bf16[64,96,128]{2,1,0:T(8,128)(2,1)S(1)}, bf16[64,96,128]{2,1,0:T(8,128)(2,1)S(1)}, u32[]{:S(2)}, u32[]{:S(2)}) collective-permute-start(bf16[64,96,128]{2,1,0:T(8,128)(2,1)S(1)} %collective-permute-done.17.refs_1_), channel_id=1, source_target_pairs={{0,4},{1,13},{2,6},{3,15},{64,68},{65,77},{66,70},{67,79},{4,8},{5... | collective-permute-start | bytes 4718600 | tf_op jit(solution)/shard_map/ppermute | solution.py:291
  82.0 33.3 %collective-permute-start.20 = (bf16[64,96,128]{2,1,0:T(8,128)(2,1)S(1)}, bf16[64,96,128]{2,1,0:T(8,128)(2,1)S(1)}, u32[]{:S(2)}, u32[]{:S(2)}) collective-permute-start(bf16[64,96,128]{2,1,0:T(8,128)(2,1)S(1)} %collective-permute-done.18.refs_5_), channel_id=1, source_target_pairs={{0,16},{1,49},{2,18},{3,51},{64,80},{65,113},{66,82},{67,115},{4,2... | collective-permute-start | bytes 4718600 | tf_op jit(solution)/shard_map/ppermute | solution.py:291
  88.8 2.0 %copy-start.3 = (bf16[128,128,128]{2,1,0:T(8,128)(2,1)}, bf16[128,128,128]{2,1,0:T(8,128)(2,1)S(1)}, u32[]{:S(2)}) copy-start(bf16[128,128,128]{2,1,0:T(8,128)(2,1)S(1)} %gate_values.2.refs_8_) | copy-start | bytes 12582916
  98.5 19.9 %collective-permute-start.22 = (bf16[64,96,128]{2,1,0:T(8,128)(2,1)}, bf16[64,96,128]{2,1,0:T(8,128)(2,1)}, u32[]{:S(2)}, u32[]{:S(2)}) collective-permute-start(bf16[64,96,128]{2,1,0:T(8,128)(2,1)} %collective-permute-done.3.c_ref), channel_id=1, source_target_pairs={{0,1},{1,0},{2,3},{3,2},{64,65},{65,64},{66,67},{67,66},{4,5},{5,4... | collective-permute-start | bytes 4718600 | tf_op jit(solution)/shard_map/ppermute | solution.py:336
  105.1 1.9 %copy-start.1 = (bf16[128,128,128]{2,1,0:T(8,128)(2,1)}, bf16[128,128,128]{2,1,0:T(8,128)(2,1)S(1)}, u32[]{:S(2)}) copy-start(bf16[128,128,128]{2,1,0:T(8,128)(2,1)S(1)} %gate_values.3.refs_8_) | copy-start | bytes 12582916
  115.3 1.1 copy-start.20
  116.4 13.8 %collective-permute-start.21 = (bf16[64,96,128]{2,1,0:T(8,128)(2,1)}, bf16[64,96,128]{2,1,0:T(8,128)(2,1)}, u32[]{:S(2)}, u32[]{:S(2)}) collective-permute-start(bf16[64,96,128]{2,1,0:T(8,128)(2,1)} %collective-permute-done.4.c_ref), channel_id=1, source_target_pairs={{0,1},{1,0},{2,3},{3,2},{64,65},{65,64},{66,67},{67,66},{4,5},{5,4... | collective-permute-start | bytes 4718600 | tf_op jit(solution)/shard_map/ppermute | solution.py:344
  117.5 25.9 %collective-permute-start.25 = (bf16[64,96,128]{2,1,0:T(8,128)(2,1)}, bf16[64,96,128]{2,1,0:T(8,128)(2,1)}, u32[]{:S(2)}, u32[]{:S(2)}) collective-permute-start(bf16[64,96,128]{2,1,0:T(8,128)(2,1)} %collective-permute-done.23.refs_1_), channel_id=1, source_target_pairs={{0,4},{1,13},{2,6},{3,15},{64,68},{65,77},{66,70},{67,79},{4,8},{5... | collective-permute-start | bytes 4718600 | tf_op jit(solution)/shard_map/ppermute | solution.py:291
  117.5 25.9 %collective-permute-start.26 = (bf16[64,96,128]{2,1,0:T(8,128)(2,1)}, bf16[64,96,128]{2,1,0:T(8,128)(2,1)}, u32[]{:S(2)}, u32[]{:S(2)}) collective-permute-start(bf16[64,96,128]{2,1,0:T(8,128)(2,1)} %collective-permute-done.24.refs_5_), channel_id=1, source_target_pairs={{0,16},{1,49},{2,18},{3,51},{64,80},{65,113},{66,82},{67,115},{4,2... | collective-permute-start | bytes 4718600 | tf_op jit(solution)/shard_map/ppermute | solution.py:291
  118.5 1.9 copy-start.6
  120.4 8.1 %copy-start.21 = (bf16[64,96,128]{2,1,0:T(8,128)(2,1)S(1)}, bf16[64,96,128]{2,1,0:T(8,128)(2,1)}, u32[]{:S(2)}) copy-start(bf16[64,96,128]{2,1,0:T(8,128)(2,1)} %copy-done.20) | copy-start | bytes 4718596
  120.4 8.3 %copy-start.24 = (bf16[64,96,128]{2,1,0:T(8,128)(2,1)S(1)}, bf16[64,96,128]{2,1,0:T(8,128)(2,1)}, u32[]{:S(2)}) copy-start(bf16[64,96,128]{2,1,0:T(8,128)(2,1)} %copy-done.23) | copy-start | bytes 4718596
  128.4 27.8 %copy-start.9 = (bf16[64,96,128]{2,1,0:T(8,128)(2,1)S(1)}, bf16[64,96,128]{2,1,0:T(8,128)(2,1)}, u32[]{:S(2)}) copy-start(bf16[64,96,128]{2,1,0:T(8,128)(2,1)} %copy-done.8) | copy-start | bytes 4718596
  128.4 27.8 %copy-start.11 = (bf16[64,96,128]{2,1,0:T(8,128)(2,1)S(1)}, bf16[64,96,128]{2,1,0:T(8,128)(2,1)}, u32[]{:S(2)}) copy-start(bf16[64,96,128]{2,1,0:T(8,128)(2,1)} %copy-done.10) | copy-start | bytes 4718596
  128.5 27.8 %copy-start.17 = (bf16[64,96,128]{2,1,0:T(8,128)(2,1)S(1)}, bf16[64,96,128]{2,1,0:T(8,128)(2,1)}, u32[]{:S(2)}) copy-start(bf16[64,96,128]{2,1,0:T(8,128)(2,1)} %copy-done.16) | copy-start | bytes 4718596
  128.5 27.8 %copy-start.19 = (bf16[64,96,128]{2,1,0:T(8,128)(2,1)S(1)}, bf16[64,96,128]{2,1,0:T(8,128)(2,1)}, u32[]{:S(2)}) copy-start(bf16[64,96,128]{2,1,0:T(8,128)(2,1)} %copy-done.18) | copy-start | bytes 4718596
  128.5 27.8 %copy-start.22 = (bf16[64,96,128]{2,1,0:T(8,128)(2,1)S(1)}, bf16[64,96,128]{2,1,0:T(8,128)(2,1)}, u32[]{:S(2)}) copy-start(bf16[64,96,128]{2,1,0:T(8,128)(2,1)} %copy-done.20) | copy-start | bytes 4718596
  128.5 27.8 %copy-start.25 = (bf16[64,96,128]{2,1,0:T(8,128)(2,1)S(1)}, bf16[64,96,128]{2,1,0:T(8,128)(2,1)}, u32[]{:S(2)}) copy-start(bf16[64,96,128]{2,1,0:T(8,128)(2,1)} %copy-done.23) | copy-start | bytes 4718596
  128.5 27.8 %copy-start.29 = (bf16[128,128]{1,0:T(8,128)(2,1)S(1)}, bf16[128,128]{1,0:T(8,128)(2,1)}, u32[]{:S(2)}) copy-start(bf16[128,128]{1,0:T(8,128)(2,1)} %refs_9_.3) | copy-start | bytes 98308
  128.5 27.7 %collective-permute-start.29 = (bf16[64,96,128]{2,1,0:T(8,128)(2,1)S(1)}, bf16[64,96,128]{2,1,0:T(8,128)(2,1)S(1)}, u32[]{:S(2)}, u32[]{:S(2)}) collective-permute-start(bf16[64,96,128]{2,1,0:T(8,128)(2,1)S(1)} %copy-done.21), channel_id=1, source_target_pairs={{0,4},{1,13},{2,6},{3,15},{64,68},{65,77},{66,70},{67,79},{4,8},{5... | collective-permute-start | bytes 4718600 | tf_op jit(solution)/shard_map/ppermute | solution.py:291
  128.7 27.6 %collective-permute-start.30 = (bf16[64,96,128]{2,1,0:T(8,128)(2,1)S(1)}, bf16[64,96,128]{2,1,0:T(8,128)(2,1)S(1)}, u32[]{:S(2)}, u32[]{:S(2)}) collective-permute-start(bf16[64,96,128]{2,1,0:T(8,128)(2,1)S(1)} %copy-done.24), channel_id=1, source_target_pairs={{0,16},{1,49},{2,18},{3,51},{64,80},{65,113},{66,82},{67,115},{4,2... | collective-permute-start | bytes 4718600 | tf_op jit(solution)/shard_map/ppermute | solution.py:291
  130.2 45.0 %copy-start.13 = (bf16[64,96,128]{2,1,0:T(8,128)(2,1)S(1)}, bf16[64,96,128]{2,1,0:T(8,128)(2,1)}, u32[]{:S(2)}) copy-start(bf16[64,96,128]{2,1,0:T(8,128)(2,1)} %copy-done.12) | copy-start | bytes 4718596
  138.9 4.6 %copy-start = (bf16[128,128,384]{2,1,0:T(8,128)(2,1)}, bf16[128,128,384]{2,1,0:T(8,128)(2,1)S(1)}, u32[]{:S(2)}) copy-start(bf16[128,128,384]{2,1,0:T(8,128)(2,1)S(1)} %arrange_left.3.lx_ref.ly_ref) | copy-start | bytes 37748740
  143.5 31.7 %collective-permute-start.27 = (bf16[64,96,128]{2,1,0:T(8,128)(2,1)}, bf16[64,96,128]{2,1,0:T(8,128)(2,1)S(1)}, u32[]{:S(2)}, u32[]{:S(2)}) collective-permute-start(bf16[64,96,128]{2,1,0:T(8,128)(2,1)} %collective-permute-done.25.refs_2_), channel_id=1, source_target_pairs={{0,4},{1,13},{2,6},{3,15},{64,68},{65,77},{66,70},{67,79},{4,8},{5... | collective-permute-start | bytes 4718600 | tf_op jit(solution)/shard_map/ppermute | solution.py:291
  145.0 30.1 %collective-permute-start.28 = (bf16[64,96,128]{2,1,0:T(8,128)(2,1)}, bf16[64,96,128]{2,1,0:T(8,128)(2,1)S(1)}, u32[]{:S(2)}, u32[]{:S(2)}) collective-permute-start(bf16[64,96,128]{2,1,0:T(8,128)(2,1)} %collective-permute-done.26.refs_6_), channel_id=1, source_target_pairs={{0,16},{1,49},{2,18},{3,51},{64,80},{65,113},{66,82},{67,115},{4,2... | collective-permute-start | bytes 4718600 | tf_op jit(solution)/shard_map/ppermute | solution.py:291
  156.3 2.2 %copy-start.4 = (bf16[128,128,128]{2,1,0:T(8,128)(2,1)S(1)}, bf16[128,128,128]{2,1,0:T(8,128)(2,1)}, u32[]{:S(2)}) copy-start(bf16[128,128,128]{2,1,0:T(8,128)(2,1)} %copy-done.3) | copy-start | bytes 12582916
  158.5 16.7 %copy-start.2 = (bf16[128,128,128]{2,1,0:T(8,128)(2,1)S(1)}, bf16[128,128,128]{2,1,0:T(8,128)(2,1)}, u32[]{:S(2)}) copy-start(bf16[128,128,128]{2,1,0:T(8,128)(2,1)} %copy-done.1) | copy-start | bytes 12582916
  175.2 1.4 copy-start.15
  (1 other events, 1.1 us)
